TPU v7x, 256 devices: a whole 4x4x8 slice. The times are simulated.
256 devices in a mesh: dp: 32 (over x, y, z_hi), fsdp: 8 (over z_lo, core).
Axes of the slice: x: 4, y: 4, z: 8 (z_hi: 2, z_lo: 4; z = z_hi * 4 + z_lo), core: 2. Of those that a mesh axis runs over, the one named last changes fastest.
Arguments:
- acts: bfloat16 [32768, 7168], P('dp', 'fsdp'), may hold values from -6 to 6
- out_grads: bfloat16 [32768, 12288], P('dp'), may hold values from -0.0625 to 0.0625
- basis: bfloat16 [7168, 512], P('fsdp'), may hold values from -0.0625 to 0.0625
- weight: bfloat16 [7168, 12288], P('fsdp', 'dp'), may hold values from -6 to 6
- first_moment: float32 [512, 12288], P('fsdp', 'dp'), may hold values from -0.3 to 0.3
- second_moment: float32 [512, 12288], P('fsdp', 'dp'), may hold values from 0.002 to 0.02
Outputs:
- new_weight: bfloat16 [7168, 12288], P(None, 'dp')
- new_first: float32 [512, 12288], P('fsdp', 'dp')
- new_second: float32 [512, 12288], P('fsdp', 'dp')
All inputs are finite; a program needn't handle non-finite values.
Results may differ from a plain program's by a relative error of at most 0.0049.
Values may be sent and summed in bfloat16 or wider, within the bound.
No kernel may reach another device: no remote copies, remote signals or barrier semaphores. Data moves between devices by JAX's collectives and lax.ppermute only.
A program may use at most 128 MiB of HBM per device.

v0:
```python
import jax
import jax.numpy as jnp
from jax import lax
from jax.sharding import PartitionSpec as P

first_fix = 0.99997343860111
second_fix = 0.0952078528


def shards(acts, out_grads, basis, weight, first_moment, second_moment):
    rank_local = first_moment.shape[0]
    partial_t = lax.dot_general(
        basis, acts, (((0,), (1,)), ((), ())), preferred_element_type=jnp.float32
    )
    summed = lax.psum(partial_t, "fsdp")
    offset = lax.axis_index("fsdp") * rank_local
    ranks_t = lax.dynamic_slice_in_dim(summed, offset, rank_local, 0).astype(jnp.bfloat16)
    picked = out_grads
    grad = lax.psum_scatter(
        lax.dot_general(
            picked, ranks_t, (((0,), (1,)), ((), ())), preferred_element_type=jnp.float32
        ),
        "dp",
        scatter_dimension=0,
        tiled=True,
    ).T
    new_first = 0.9 * first_moment + 0.1 * grad
    new_second = 0.999 * second_moment + 0.001 * grad * grad
    direction = (new_first / first_fix / (jnp.sqrt(new_second / second_fix) + 1e-08)).astype(
        jnp.bfloat16
    )
    picked = basis
    lifted = jnp.dot(
        picked,
        lax.all_gather(direction, "fsdp", axis=0, tiled=True),
        preferred_element_type=jnp.float32,
    )
    updated = (weight.astype(jnp.float32) - 8.0 * lifted).astype(jnp.bfloat16)
    new_weight = lax.all_gather(updated, "fsdp", axis=0, tiled=True)
    return (new_weight, new_first, new_second)


def solution(mesh):
    placed = (
        P("dp", "fsdp"),
        P("dp", None),
        P("fsdp", None),
        P("fsdp", "dp"),
        P("fsdp", "dp"),
        P("fsdp", "dp"),
    )
    return jax.shard_map(
        shards,
        mesh=mesh,
        in_specs=placed,
        out_specs=(P(None, "dp"), P("fsdp", "dp"), P("fsdp", "dp")),
        check_vma=False,
    )
```

profile of v0, /device:TPU:1, one launch (start us, length us, event | category | flops | bytes accessed | tf_op | source)
XLA Modules:
  0.0 445.5 jit_solution(12410708836224020560)
XLA Ops:
  7.2 0.0 copy-start
  7.2 0.0 reduce-scatter.2.cloned.1.call-start
  7.2 1.4 copy-done
  8.7 3.8 fusion.8
  12.5 64.2 %all-reduce.1 = bf16[512,1024]{1,0:T(8,128)(2,1)S(1)} all-reduce(f32[512,1024]{1,0:T(8,128)} %fusion.8), channel_id=1, replica_groups=mesh['dp'=32,'fsdp'=8] {'fsdp'}, use_global_device_ids=true, to_apply=%region_0.0 | all-reduce | flops 524288 | bytes 3145728 | tf_op jit(solution)/shard_map/psum | solution.py:15
  76.7 14.3 %convolution_bitcast_fusion = f32[12288,64]{0,1:T(8,128)} fusion(bf16[1024,12288]{1,0:T(8,128)(2,1)} %param.7, bf16[512,1024]{1,0:T(8,128)(2,1)S(1)} %all-reduce.1, s32[]{:T(128)S(6)} %select_n.3), kind=kOutput, calls=%fused_computation | convolution fusion | flops 1610612736 | bytes 28442628 | tf_op jit(solution)/shard_map/dot_general | solution.py:20
  91.0 0.0 copy-start.1
  91.0 0.0 copy-start.2
  91.0 0.0 copy-start.3
  91.0 0.0 reduce-scatter.2.cloned.1.call-update
  91.0 0.0 all-gather.2.cloned.1.call-start
  91.1 1.0 copy-done.1
  92.1 0.4 copy.9
  92.4 257.8 %reduce-scatter.2.cloned.1.call-done = f32[384,64]{0,1:T(8,128)} async-done(((f32[12288,64]{0,1:T(8,128)}), f32[384,64]{0,1:T(8,128)}) %reduce-scatter.2.cloned.1.call-update) | async-done | bytes 98320 | tf_op jit(solution)/shard_map/reduce_scatter | solution.py:19
  350.2 0.0 copy-done.2
  350.2 0.0 copy-done.3
  350.2 1.6 divide_convert_fusion
  351.9 17.6 %all_gather.6 = bf16[512,384]{1,0:T(8,128)(2,1)S(1)} all-gather(bf16[64,384]{1,0:T(8,128)(2,1)S(1)} %get-tuple-element.6), channel_id=1, replica_groups=mesh['dp'=32,'fsdp'=8] {'fsdp'}, dimensions={0}, use_global_device_ids=true | all-gather | bytes 442368 | tf_op jit(solution)/shard_map/all_gather | solution.py:35
  369.5 2.6 fusion.2
  372.1 0.0 all-gather.2.cloned.1.call-update
  372.2 58.2 %all-gather.2.cloned.1.call-done = bf16[7168,384]{0,1:T(8,128)(2,1)} async-done(((bf16[896,384]{0,1:T(8,128)(2,1)}), bf16[7168,384]{0,1:T(8,128)(2,1)}) %all-gather.2.cloned.1.call-update) | async-done | bytes 5505040 | tf_op jit(solution)/shard_map/all_gather | solution.py:39
  430.4 8.3 %copy.10 = bf16[7168,384]{1,0:T(8,128)(2,1)} copy(bf16[7168,384]{0,1:T(8,128)(2,1)} %all-gather.2.cloned.1.call-done) | data formatting | bytes 11010048
Async XLA Ops:
  7.2 1.5 copy-start
  7.2 343.0 %reduce-scatter.2.cloned.1.call-start = ((), (), s32[]{:S(2)}) async-start(), calls=%async_computation.1 | async-start | bytes 3244032 | tf_op jit(solution)/shard_map/reduce_scatter | solution.py:19
  91.0 1.1 copy-start.1
  91.0 259.2 %copy-start.2 = (f32[64,384]{1,0:T(8,128)S(1)}, f32[64,384]{1,0:T(8,128)}, u32[]{:S(2)}) copy-start(f32[64,384]{1,0:T(8,128)} %param.10) | copy-start | bytes 294916
  91.0 259.2 %copy-start.3 = (f32[64,384]{1,0:T(8,128)S(1)}, f32[64,384]{1,0:T(8,128)}, u32[]{:S(2)}) copy-start(f32[64,384]{1,0:T(8,128)} %param.11) | copy-start | bytes 294916
  91.0 339.4 %all-gather.2.cloned.1.call-start = ((), (), s32[]{:S(2)}) async-start(), calls=%async_computation.2 | async-start | bytes 6193152 | tf_op jit(solution)/shard_map/all_gather | solution.py:39
Sparse Core Ops, SparseCore 0:
  91.1 259.0 reduce-scatter.1
  372.3 58.0 all-gather.1
where the time goes:
time: 448 us; the launch traced here: 446 us
  waiting for transfers between devices  316 us (71%)
  blocking collectives  81.9 us (18%)
  matrix products  20.7 us (5%)
  between operations  14.1 us (3%)
  local copies, waits for them, and re-layouts  11.1 us (2%)
    reduce_scatter x1, waiting for transfers between devices, shards(): lax.psum_scatter(lax.dot_general(picked, ranks_t, (((0,), (1,)), ((), ())...  258 us
    psum x1, blocking collectives, shards(): summed = lax.psum(partial_t, 'fsdp')  64.2 us
    all_gather x1, waiting for transfers between devices, shards(): new_weight = lax.all_gather(updated, 'fsdp', axis=0, tiled=True)  58.2 us
    all_gather x1, blocking collectives, shards(): lax.all_gather(direction, 'fsdp', axis=0, tiled=True)  17.6 us
    dot_general x1, matrix products, shards(): lax.dot_general(picked, ranks_t, (((0,), (1,)), ((), ())), preferred_elem...  14.3 us
    unnamed x10, local copies, waits for them, and re-layouts  11.1 us
  transfers between devices with their start and end apart: 2, of which 2 were waited for; matrix products, arithmetic and copies ran while one was open for 0% of the time, Pallas kernels for 0%

commit v1 on v0

v1 whole, which is shorter than its diff:
```python
import jax
import jax.numpy as jnp
from jax import lax
from jax.experimental import pallas as pl
from jax.experimental.pallas import tpu as pltpu
from jax.sharding import Mesh, PartitionSpec as P

first_fix = 0.99997343860111
second_fix = 0.0952078528

DP = ("x", "y", "zh")
FSDP = ("zl", "core")
BF = jnp.bfloat16
F32 = jnp.float32


def grad_kernel(ranks_ref, grads_ref, out_ref):
    both = jnp.dot(ranks_ref[...], grads_ref[...], preferred_element_type=F32).astype(BF)
    half = out_ref.shape[-1]
    for i in range(2):
        out_ref[0, i] = both[:, i * half : (i + 1) * half]


def grad_blocks(ranks, out_grads, blocks):
    rank_local, tokens = ranks.shape
    width = out_grads.shape[1] // blocks
    return pl.pallas_call(
        grad_kernel,
        grid=(blocks // 2,),
        in_specs=[
            pl.BlockSpec((rank_local, tokens), lambda j: (0, 0)),
            pl.BlockSpec((tokens, 2 * width), lambda j: (0, j)),
        ],
        out_specs=pl.BlockSpec((1, 2, rank_local, width), lambda j: (j, 0, 0, 0)),
        out_shape=jax.ShapeDtypeStruct((blocks // 2, 2, rank_local, width), BF),
        compiler_params=pltpu.CompilerParams(vmem_limit_bytes=32 * 2**20),
        cost_estimate=pl.CostEstimate(
            flops=2 * rank_local * tokens * blocks * width,
            bytes_accessed=2 * tokens * blocks * width,
            transcendentals=0,
        ),
    )(ranks, out_grads)


def lift_kernel(where_ref, *refs):
    pieces, (mine_ref, other_ref, weight_ref, weight2_ref, out_ref, dirs) = refs[:4], refs[4:]
    core, zl = where_ref[0], where_ref[1]
    pair = pieces[0].shape[0]

    @pl.when(pl.program_id(0) == 0)
    def _():
        for r, piece in enumerate(pieces):
            at = lax.rem(zl - r + 4, 4) * pair
            dirs[pl.ds(pl.multiple_of(at, pair), pair), :] = piece[...]

    rows = weight_ref.shape[1]
    part = mine_ref.shape[3]
    for b_ref, w_ref, c in ((mine_ref, weight_ref, core), (other_ref, weight2_ref, 1 - core)):
        for x in range(4):
            block = jnp.concatenate([b_ref[x, y, 0] for y in range(4)], axis=-1)
            lifted = jnp.dot(block, dirs[...], preferred_element_type=F32)
            old = w_ref[0, x * part : (x + 1) * part, :].astype(F32)
            at = pl.multiple_of(c * rows + x * part, part)
            out_ref[pl.ds(at, part), :] = (old - 8.0 * lifted).astype(BF)


def lift(where, pieces, mine, other, weight_mine, weight_other):
    _, rows, width = weight_mine.shape
    pair = pieces[0].shape[0]
    part, lanes = mine.shape[3:]
    basis_spec = pl.BlockSpec((4, 4, 1, part, lanes), lambda i, w: (0, 0, i, 0, 0))
    weight_spec = pl.BlockSpec((1, rows, width), lambda i, w: (i, 0, 0))
    return pl.pallas_call(
        lift_kernel,
        grid_spec=pltpu.PrefetchScalarGridSpec(
            num_scalar_prefetch=1,
            grid=(4,),
            in_specs=[pl.BlockSpec((pair, width), lambda i, w: (0, 0))] * 4
            + [basis_spec] * 2
            + [weight_spec] * 2,
            out_specs=pl.BlockSpec((2 * rows, width), lambda i, w: (i, 0)),
            scratch_shapes=[pltpu.VMEM((4 * pair, width), BF)],
        ),
        out_shape=jax.ShapeDtypeStruct((8 * rows, width), BF),
        compiler_params=pltpu.CompilerParams(vmem_limit_bytes=32 * 2**20),
        cost_estimate=pl.CostEstimate(
            flops=2 * 8 * rows * 4 * pair * width,
            bytes_accessed=2 * 8 * rows * (2 * width + 4 * pair),
            transcendentals=0,
        ),
    )(where, *pieces, mine, other, weight_mine, weight_other)


def swap(value, axis):
    return lax.ppermute(value, axis, [(0, 1), (1, 0)])


def around(value, shift):
    return lax.ppermute(value, "zl", [(i, (i + shift) % 4) for i in range(4)])


def pick(value, at, axis=0):
    return lax.dynamic_index_in_dim(value, at, axis, keepdims=False)


def shards(acts, out_grads, basis, weight, first_moment, second_moment):
    rank_local, width = first_moment.shape
    rows, rank = basis.shape
    tokens = acts.shape[0]
    x, y, zh, zl, core = (lax.axis_index(a) for a in ("x", "y", "zh", "zl", "core"))

    with jax.named_scope("gather_ahead"):
        weight_mine = lax.all_gather(weight, "zl")
        tile = lax.dynamic_slice(basis, (x * (rows // 4), y * (rank // 4)), (rows // 4, rank // 4))
        tiles = lax.dynamic_update_index_in_dim(
            jnp.zeros((4,) + tile.shape, BF), tile, zl, 0
        )
        for r in range(1, 4):
            tiles = lax.dynamic_update_index_in_dim(
                tiles, around(tile, r), (zl - r) % 4, 0
            )
        mine = lax.all_gather(tiles, ("x", "y")).reshape((4, 4) + tiles.shape)
        other = swap(mine, "core")
        weight_other = swap(weight_mine, "core")

    with jax.named_scope("project"):
        partial_t = lax.dot_general(
            basis, acts, (((0,), (1,)), ((), ())), preferred_element_type=F32
        ).reshape(4, 2, rank_local, tokens)
        got = swap(pick(partial_t, 1 - core, 1).astype(BF), "core")
        mixed = pick(partial_t, core, 1) + got.astype(F32)
        total = pick(mixed, zl)
        for r in range(1, 4):
            total = total + around(pick(mixed, (zl + r) % 4).astype(BF), r).astype(F32)
        ranks_t = total.astype(BF)

    with jax.named_scope("grad"):
        blocks = grad_blocks(ranks_t, out_grads, 32)
        parts = lax.all_to_all(blocks, ("x", "y"), 0, 0)
        halves = jnp.sum(parts.astype(F32), axis=0)
        grad = pick(halves, zh) + swap(pick(halves, 1 - zh).astype(BF), "zh").astype(F32)

    with jax.named_scope("adam"):
        new_first = 0.9 * first_moment + 0.1 * grad
        new_second = 0.999 * second_moment + 0.001 * grad * grad
        direction = (
            new_first / first_fix / (jnp.sqrt(new_second / second_fix) + 1e-08)
        ).astype(BF)

    with jax.named_scope("lift"):
        theirs = swap(direction, "core")
        pair = jnp.where(
            core == 0,
            jnp.concatenate([direction, theirs]),
            jnp.concatenate([theirs, direction]),
        )
        pieces = [pair] + [around(pair, r) for r in range(1, 4)]
        where = jnp.stack([core, zl]).astype(jnp.int32)
        new_weight = lift(where, pieces, mine, other, weight_mine, weight_other)
    return (new_weight, new_first, new_second)


def solution(mesh):
    split = Mesh(mesh.devices.reshape(4, 4, 2, 4, 2), DP + FSDP)
    placed = (
        P(DP, FSDP),
        P(DP, None),
        P(FSDP, None),
        P(FSDP, DP),
        P(FSDP, DP),
        P(FSDP, DP),
    )
    return jax.shard_map(
        shards,
        mesh=split,
        in_specs=placed,
        out_specs=(P(None, DP), P(FSDP, DP), P(FSDP, DP)),
        check_vma=False,
    )
```

time: 448 us -> 231 us (0.52)
  waiting for transfers between devices: 316 us -> 147 us
  blocking collectives: 81.9 us -> 0 us
  starting transfers between devices: 0.08 us -> 29.6 us
  Pallas kernels: 0 us -> 25.4 us
  matrix products: 20.7 us -> 2.48 us
    reduce_scatter x1 -> x0, waiting for transfers between devices: 258 us -> none  [shards(): lax.psum_scatter(lax.dot_general(picked, ranks_t, (((0,), (1,)), ((), ())...]
    psum x1 -> x0, blocking collectives: 64.2 us -> none  [shards(): summed = lax.psum(partial_t, 'fsdp')]
    all_gather x1 -> x2, waiting for transfers between devices: 58.2 us -> 107 us  [the longest x1 56.5 us: shards(): weight_mine = lax.all_gather(weight, 'zl')]
    pallas_call x0 -> x2, Pallas kernels: none -> 25.4 us  [the longest x1 16.8 us: grad_blocks(): pl.pallas_call(grad_kernel, grid=(blocks // 2,), in_specs=[pl.BlockSpec((...]
    all_to_all x0 -> x1, waiting for transfers between devices: none -> 23.7 us  [shards(): parts = lax.all_to_all(blocks, ('x', 'y'), 0, 0)]
    ppermute x0 -> x14, starting transfers between devices: none -> 23.3 us  [the longest x9 13.1 us: around(): return lax.ppermute(value, 'zl', [(i, (i + shift) % 4) for i in range(4)])]
    all_gather x1 -> x0, blocking collectives: 17.6 us -> none  [shards(): lax.all_gather(direction, 'fsdp', axis=0, tiled=True)]
    dot_general x2 -> x0, matrix products: 16.9 us -> none  [the longest x1 14.3 us: shards(): lax.dot_general(picked, ranks_t, (((0,), (1,)), ((), ())), preferred_elem...]
  transfers between devices with their start and end apart: 2 -> 17, of which waited for: 2 -> 10; matrix products, arithmetic and copies ran while one was open for 0% -> 3% of each run, Pallas kernels for 0% -> 7%
where the time goes in v1:
time: 231 us; the launch traced here: 230 us
  waiting for transfers between devices  147 us (64%)
  starting transfers between devices  29.6 us (13%)
  Pallas kernels  25.4 us (11%)
  between operations  14.2 us (6%)
  local copies, waits for them, and re-layouts  7.64 us (3%)
  other arithmetic  4.31 us (2%)
  matrix products  2.48 us (1%)
    all_gather x1, waiting for transfers between devices, shards(): weight_mine = lax.all_gather(weight, 'zl')  56.5 us
    all_gather x1, waiting for transfers between devices, shards(): mine = lax.all_gather(tiles, ('x', 'y')).reshape((4, 4) + tiles.shape)  50.4 us
    all_to_all x1, waiting for transfers between devices, shards(): parts = lax.all_to_all(blocks, ('x', 'y'), 0, 0)  23.7 us
    pallas_call x1, Pallas kernels, grad_blocks(): pl.pallas_call(grad_kernel, grid=(blocks // 2,), in_specs=[pl.BlockSpec((...  16.8 us
    ppermute x9, starting transfers between devices, around(): return lax.ppermute(value, 'zl', [(i, (i + shift) % 4) for i in range(4)])  13.1 us
    ppermute x9, waiting for transfers between devices, around(): return lax.ppermute(value, 'zl', [(i, (i + shift) % 4) for i in range(4)])  11.4 us
    ppermute x5, starting transfers between devices, swap(): return lax.ppermute(value, axis, [(0, 1), (1, 0)])  10.2 us
    pallas_call x1, Pallas kernels, lift(): pl.pallas_call(lift_kernel, grid_spec=pltpu.PrefetchScalarGridSpec(num_sc...  8.63 us
  transfers between devices with their start and end apart: 17, of which 10 were waited for; matrix products, arithmetic and copies ran while one was open for 3% of the time, Pallas kernels for 7%

profile of v1, /device:TPU:1, one launch (start us, length us, event | category | flops | bytes accessed | tf_op | source)
XLA Modules:
  0.0 230.4 jit_solution(2331072761583353426)
XLA Ops:
  8.2 2.5 %collective-permute-start.9 = (bf16[224,128]{1,0:T(8,128)(2,1)S(1)}, bf16[224,128]{1,0:T(8,128)(2,1)S(1)}, u32[]{:S(2)}, u32[]{:S(2)}) collective-permute-start(bf16[224,128]{1,0:T(8,128)(2,1)S(1)} %get-tuple-element.4), channel_id=1, source_target_pairs={{0,2},{2,4},{4,6},{6,0},{1,3},{3,5},{5,7},{7,1},{8,10},{10,12},{12... | collective-permute-start | bytes 172040 | tf_op jit(solution)/shard_map/gather_ahead/ppermute | solution.py:99
  10.8 3.0 %collective-permute-start.10 = (bf16[224,128]{1,0:T(8,128)(2,1)S(1)}, bf16[224,128]{1,0:T(8,128)(2,1)S(1)}, u32[]{:S(2)}, u32[]{:S(2)}) collective-permute-start(bf16[224,128]{1,0:T(8,128)(2,1)S(1)} %get-tuple-element.4), channel_id=1, source_target_pairs={{0,4},{2,6},{4,0},{6,2},{1,5},{3,7},{5,1},{7,3},{8,12},{10,14},{12... | collective-permute-start | bytes 172040 | tf_op jit(solution)/shard_map/gather_ahead/ppermute | solution.py:99
  15.1 2.0 collective-permute-done.10
  19.6 2.5 %fusion.10 = f32[512,1024]{1,0:T(8,128)S(1)} fusion(bf16[896,512]{1,0:T(8,128)(2,1)} %param.8, bf16[1024,896]{1,0:T(8,128)(2,1)S(1)} %copy-done), kind=kOutput, calls=%fused_computation.27 | convolution fusion | flops 939524096 | bytes 4849664 | tf_op jit(solution)/shard_map/project/dot_general | solution.py:127
  22.1 1.3 copy-done.3
  23.5 1.5 collective-permute-start
  25.0 50.4 %all-gather.4.cloned.1.call-done = bf16[16,4,224,128]{3,2,1,0:T(8,128)(2,1)} async-done(((bf16[1,4,224,128]{3,2,1,0:T(8,128)(2,1)}), bf16[16,4,224,128]{3,2,1,0:T(8,128)(2,1)}) %all-gather.4.cloned.1.call-update) | async-done | bytes 3670032 | tf_op jit(solution)/shard_map/gather_ahead/all_gather | solution.py:122
  76.4 1.4 bitcast_add_fusion
  77.9 1.4 collective-permute-start.1
  79.2 2.1 collective-permute-start.3
  81.7 56.5 %all-gather.6.cloned.1.call-done = bf16[3584,384]{1,0:T(8,128)(2,1)} async-done(((bf16[896,384]{1,0:T(8,128)(2,1)}), bf16[3584,384]{1,0:T(8,128)(2,1)}) %all-gather.6.cloned.1.call-update) | async-done | bytes 2752528 | tf_op jit(solution)/shard_map/gather_ahead/all_gather | solution.py:113
  139.7 16.8 %grad.1 = bf16[16,2,64,384]{3,2,1,0:T(8,128)(2,1)} custom-call(bf16[64,1024]{1,0:T(8,128)(2,1)S(1)} %fusion.3.ranks_ref, bf16[1024,12288]{1,0:T(8,128)(2,1)} %grads_ref.1), custom_call_target="tpu_custom_call" | custom-call | flops 1610612736 | bytes 25165824 | tf_op jit(solution)/shard_map/grad/pallas_call | solution.py:27
  156.5 6.2 %all-to-all-start = ((bf16[16,2,64,384]{3,2,1,0:T(8,128)(2,1)}), bf16[16,2,64,384]{3,2,1,0:T(8,128)(2,1)S(1)}, u32[]{:S(2)}, u32[]{:S(2)}) async-start(bf16[16,2,64,384]{3,2,1,0:T(8,128)(2,1)} %grad.1), calls=%async_computation | async-start | bytes 3145728 | tf_op jit(solution)/shard_map/grad/all_to_all | solution.py:139
  162.6 23.7 %all-to-all-done = bf16[16,2,64,384]{3,2,1,0:T(8,128)(2,1)S(1)} async-done(((bf16[16,2,64,384]{3,2,1,0:T(8,128)(2,1)}), bf16[16,2,64,384]{3,2,1,0:T(8,128)(2,1)S(1)}, u32[]{:S(2)}, u32[]{:S(2)}) %all-to-all-start) | async-done | bytes 1572896 | tf_op jit(solution)/shard_map/grad/all_to_all | solution.py:139
  187.2 3.8 %collective-permute-start.4 = (bf16[64,384]{1,0:T(8,128)(2,1)S(1)}, bf16[64,384]{1,0:T(8,128)(2,1)S(1)}, u32[]{:S(2)}, u32[]{:S(2)}) collective-permute-start(bf16[64,384]{1,0:T(8,128)(2,1)S(1)} %fusion.8), channel_id=1, source_target_pairs={{0,8},{8,0},{1,9},{9,1},{2,10},{10,2},{3,11},{11,3},{4,12},{12,4},... | collective-permute-start | bytes 147464 | tf_op jit(solution)/shard_map/grad/ppermute | solution.py:95
  191.1 3.2 %collective-permute-done.4 = bf16[64,384]{1,0:T(8,128)(2,1)S(1)} collective-permute-done((bf16[64,384]{1,0:T(8,128)(2,1)S(1)}, bf16[64,384]{1,0:T(8,128)(2,1)S(1)}, u32[]{:S(2)}, u32[]{:S(2)}) %collective-permute-start.4) | collective-permute-done | bytes 49184 | tf_op jit(solution)/shard_map/grad/ppermute | solution.py:95
  194.3 1.7 divide_convert_fusion
  196.0 3.3 %collective-permute-start.5 = (bf16[64,384]{1,0:T(8,128)(2,1)S(1)}, bf16[64,384]{1,0:T(8,128)(2,1)S(1)}, u32[]{:S(2)}, u32[]{:S(2)}) collective-permute-start(bf16[64,384]{1,0:T(8,128)(2,1)S(1)} %get-tuple-element.5), channel_id=1, source_target_pairs={{0,1},{1,0},{2,3},{3,2},{4,5},{5,4},{6,7},{7,6},{8,9},{9,8},{10,11... | collective-permute-start | bytes 147464 | tf_op jit(solution)/shard_map/lift/ppermute | solution.py:95
  200.2 1.6 collective-permute-start.8
  201.9 1.4 collective-permute-start.6
  204.3 6.8 %collective-permute-done.7.refs_2_ = bf16[128,384]{1,0:T(8,128)(2,1)S(1)} collective-permute-done((bf16[128,384]{1,0:T(8,128)(2,1)S(1)}, bf16[128,384]{1,0:T(8,128)(2,1)S(1)}, u32[]{:S(2)}, u32[]{:S(2)}) %collective-permute-start.7) | collective-permute-done | bytes 98336 | tf_op jit(solution)/shard_map/lift/ppermute | solution.py:99
  211.1 2.0 copy-done.1
  213.2 1.8 copy-done.2
  214.9 8.6 %lift.1 = bf16[7168,384]{1,0:T(8,128)(2,1)} custom-call(s32[2]{0:T(128)S(1)} %pad_add_fusion.where_ref, bf16[128,384]{1,0:T(8,128)(2,1)S(1)} %maximum_select_fusion.refs_0_, bf16[128,384]{1,0:T(8,128)(2,1)S(1)} %collective-permute-done.6.refs_1_, bf16[128,384]{1,0:T(8,128)(2,1)S(1)} %collective-permute-done.7.refs_2_, ...), custom_call_target="tpu_custom_call" | custom-call | flops 2818572288 | bytes 18350080 | tf_op jit(solution)/shard_map/lift/pallas_call | solution.py:73
  (43 shorter events, 10.9 us)
Async XLA Ops:
  7.2 12.4 %copy-start = (bf16[1024,896]{1,0:T(8,128)(2,1)S(1)}, bf16[1024,896]{1,0:T(8,128)(2,1)}, u32[]{:S(2)}) copy-start(bf16[1024,896]{1,0:T(8,128)(2,1)} %param.6) | copy-start | bytes 5505028
  7.2 68.2 %all-gather.4.cloned.1.call-start = ((), (), s32[]{:S(2)}) async-start(), calls=%async_computation.1 | async-start | bytes 3899392 | tf_op jit(solution)/shard_map/gather_ahead/all_gather | solution.py:122
  8.2 6.9 %collective-permute-start.9 = (bf16[224,128]{1,0:T(8,128)(2,1)S(1)}, bf16[224,128]{1,0:T(8,128)(2,1)S(1)}, u32[]{:S(2)}, u32[]{:S(2)}) collective-permute-start(bf16[224,128]{1,0:T(8,128)(2,1)S(1)} %get-tuple-element.4), channel_id=1, source_target_pairs={{0,2},{2,4},{4,6},{6,0},{1,3},{3,5},{5,7},{7,1},{8,10},{10,12},{12... | collective-permute-start | bytes 172040 | tf_op jit(solution)/shard_map/gather_ahead/ppermute | solution.py:99
  10.8 6.3 %collective-permute-start.10 = (bf16[224,128]{1,0:T(8,128)(2,1)S(1)}, bf16[224,128]{1,0:T(8,128)(2,1)S(1)}, u32[]{:S(2)}, u32[]{:S(2)}) collective-permute-start(bf16[224,128]{1,0:T(8,128)(2,1)S(1)} %get-tuple-element.4), channel_id=1, source_target_pairs={{0,4},{2,6},{4,0},{6,2},{1,5},{3,7},{5,1},{7,3},{8,12},{10,14},{12... | collective-permute-start | bytes 172040 | tf_op jit(solution)/shard_map/gather_ahead/ppermute | solution.py:99
  13.8 4.3 %collective-permute-start.11 = (bf16[224,128]{1,0:T(8,128)(2,1)S(1)}, bf16[224,128]{1,0:T(8,128)(2,1)S(1)}, u32[]{:S(2)}, u32[]{:S(2)}) collective-permute-start(bf16[224,128]{1,0:T(8,128)(2,1)S(1)} %get-tuple-element.4), channel_id=1, source_target_pairs={{0,6},{2,0},{4,2},{6,4},{1,7},{3,1},{5,3},{7,5},{8,14},{10,8},{12,... | collective-permute-start | bytes 172040 | tf_op jit(solution)/shard_map/gather_ahead/ppermute | solution.py:99
  18.1 0.7 copy-start.4
  18.8 119.4 %all-gather.6.cloned.1.call-start = ((), (), s32[]{:S(2)}) async-start(), calls=%async_computation.2 | async-start | bytes 3440640 | tf_op jit(solution)/shard_map/gather_ahead/all_gather | solution.py:113
  22.1 1.3 copy-start.3
  23.5 53.0 %collective-permute-start = (bf16[4,64,1024]{2,1,0:T(8,128)(2,1)S(1)}, bf16[4,64,1024]{2,1,0:T(8,128)(2,1)S(1)}, u32[]{:S(2)}, u32[]{:S(2)}) collective-permute-start(bf16[4,64,1024]{2,1,0:T(8,128)(2,1)S(1)} %fusion), channel_id=1, source_target_pairs={{0,1},{1,0},{2,3},{3,2},{4,5},{5,4},{6,7},{7,6},{8,9},{9,8},{10,11... | collective-permute-start | bytes 1572872 | tf_op jit(solution)/shard_map/project/ppermute | solution.py:95
  75.4 135.8 %collective-permute-start.12 = (bf16[4,4,4,224,128]{4,3,2,1,0:T(8,128)(2,1)}, bf16[4,4,4,224,128]{4,3,2,1,0:T(8,128)(2,1)}, u32[]{:S(2)}, u32[]{:S(2)}) collective-permute-start(bf16[4,4,4,224,128]{4,3,2,1,0:T(8,128)(2,1)} %bitcast.47), channel_id=1, source_target_pairs={{0,1},{1,0},{2,3},{3,2},{4,5},{5,4},{6,7},{7,6},{8,9},{9,8},{10,11... | collective-permute-start | bytes 11010056 | tf_op jit(solution)/shard_map/gather_ahead/ppermute | solution.py:95
  77.9 60.8 %collective-permute-start.1 = (bf16[64,1024]{1,0:T(8,128)(2,1)S(1)}, bf16[64,1024]{1,0:T(8,128)(2,1)S(1)}, u32[]{:S(2)}, u32[]{:S(2)}) collective-permute-start(bf16[64,1024]{1,0:T(8,128)(2,1)S(1)} %get-tuple-element.8), channel_id=1, source_target_pairs={{0,2},{2,4},{4,6},{6,0},{1,3},{3,5},{5,7},{7,1},{8,10},{10,12},{12... | collective-permute-start | bytes 393224 | tf_op jit(solution)/shard_map/project/ppermute | solution.py:99
  79.2 59.5 %collective-permute-start.3 = (bf16[64,1024]{1,0:T(8,128)(2,1)S(1)}, bf16[64,1024]{1,0:T(8,128)(2,1)S(1)}, u32[]{:S(2)}, u32[]{:S(2)}) collective-permute-start(bf16[64,1024]{1,0:T(8,128)(2,1)S(1)} %get-tuple-element.9), channel_id=1, source_target_pairs={{0,6},{2,0},{4,2},{6,4},{1,7},{3,1},{5,3},{7,5},{8,14},{10,8},{12,... | collective-permute-start | bytes 393224 | tf_op jit(solution)/shard_map/project/ppermute | solution.py:99
  81.3 57.4 %collective-permute-start.2 = (bf16[64,1024]{1,0:T(8,128)(2,1)S(1)}, bf16[64,1024]{1,0:T(8,128)(2,1)}, u32[]{:S(2)}, u32[]{:S(2)}) collective-permute-start(bf16[64,1024]{1,0:T(8,128)(2,1)S(1)} %get-tuple-element.10), channel_id=1, source_target_pairs={{0,4},{2,6},{4,0},{6,2},{1,5},{3,7},{5,1},{7,3},{8,12},{10,14},{12... | collective-permute-start | bytes 393224 | tf_op jit(solution)/shard_map/project/ppermute | solution.py:99
  138.2 72.9 %collective-permute-start.13 = (bf16[4,896,384]{2,1,0:T(8,128)(2,1)}, bf16[4,896,384]{2,1,0:T(8,128)(2,1)}, u32[]{:S(2)}, u32[]{:S(2)}) collective-permute-start(bf16[4,896,384]{2,1,0:T(8,128)(2,1)} %bitcast.49), channel_id=1, source_target_pairs={{0,1},{1,0},{2,3},{3,2},{4,5},{5,4},{6,7},{7,6},{8,9},{9,8},{10,11... | collective-permute-start | bytes 8257544 | tf_op jit(solution)/shard_map/gather_ahead/ppermute | solution.py:95
  156.5 37.8 %copy-start.6 = (f32[64,384]{1,0:T(8,128)S(1)}, f32[64,384]{1,0:T(8,128)}, u32[]{:S(2)}) copy-start(f32[64,384]{1,0:T(8,128)} %param.10) | copy-start | bytes 294916
  156.5 29.9 %all-to-all-start = ((bf16[16,2,64,384]{3,2,1,0:T(8,128)(2,1)}), bf16[16,2,64,384]{3,2,1,0:T(8,128)(2,1)S(1)}, u32[]{:S(2)}, u32[]{:S(2)}) async-start(bf16[16,2,64,384]{3,2,1,0:T(8,128)(2,1)} %grad.1), calls=%async_computation | async-start | bytes 3145728 | tf_op jit(solution)/shard_map/grad/all_to_all | solution.py:139
  186.5 0.7 copy-start.5
  187.2 7.0 %collective-permute-start.4 = (bf16[64,384]{1,0:T(8,128)(2,1)S(1)}, bf16[64,384]{1,0:T(8,128)(2,1)S(1)}, u32[]{:S(2)}, u32[]{:S(2)}) collective-permute-start(bf16[64,384]{1,0:T(8,128)(2,1)S(1)} %fusion.8), channel_id=1, source_target_pairs={{0,8},{8,0},{1,9},{9,1},{2,10},{10,2},{3,11},{11,3},{4,12},{12,4},... | collective-permute-start | bytes 147464 | tf_op jit(solution)/shard_map/grad/ppermute | solution.py:95
  196.0 4.2 %collective-permute-start.5 = (bf16[64,384]{1,0:T(8,128)(2,1)S(1)}, bf16[64,384]{1,0:T(8,128)(2,1)S(1)}, u32[]{:S(2)}, u32[]{:S(2)}) collective-permute-start(bf16[64,384]{1,0:T(8,128)(2,1)S(1)} %get-tuple-element.5), channel_id=1, source_target_pairs={{0,1},{1,0},{2,3},{3,2},{4,5},{5,4},{6,7},{7,6},{8,9},{9,8},{10,11... | collective-permute-start | bytes 147464 | tf_op jit(solution)/shard_map/lift/ppermute | solution.py:95
  200.2 4.1 %collective-permute-start.8 = (bf16[128,384]{1,0:T(8,128)(2,1)S(1)}, bf16[128,384]{1,0:T(8,128)(2,1)S(1)}, u32[]{:S(2)}, u32[]{:S(2)}) collective-permute-start(bf16[128,384]{1,0:T(8,128)(2,1)S(1)} %maximum_select_fusion.refs_0_), channel_id=1, source_target_pairs={{0,6},{2,0},{4,2},{6,4},{1,7},{3,1},{5,3},{7,5},{8,14},{10,8},{12,... | collective-permute-start | bytes 294920 | tf_op jit(solution)/shard_map/lift/ppermute | solution.py:99
  201.8 9.3 %collective-permute-start.7 = (bf16[128,384]{1,0:T(8,128)(2,1)S(1)}, bf16[128,384]{1,0:T(8,128)(2,1)S(1)}, u32[]{:S(2)}, u32[]{:S(2)}) collective-permute-start(bf16[128,384]{1,0:T(8,128)(2,1)S(1)} %maximum_select_fusion.refs_0_), channel_id=1, source_target_pairs={{0,4},{2,6},{4,0},{6,2},{1,5},{3,7},{5,1},{7,3},{8,12},{10,14},{12... | collective-permute-start | bytes 294920 | tf_op jit(solution)/shard_map/lift/ppermute | solution.py:99
  201.9 9.2 %collective-permute-start.6 = (bf16[128,384]{1,0:T(8,128)(2,1)S(1)}, bf16[128,384]{1,0:T(8,128)(2,1)S(1)}, u32[]{:S(2)}, u32[]{:S(2)}) collective-permute-start(bf16[128,384]{1,0:T(8,128)(2,1)S(1)} %maximum_select_fusion.refs_0_), channel_id=1, source_target_pairs={{0,2},{2,4},{4,6},{6,0},{1,3},{3,5},{5,7},{7,1},{8,10},{10,12},{12... | collective-permute-start | bytes 294920 | tf_op jit(solution)/shard_map/lift/ppermute | solution.py:99
  211.1 2.0 copy-start.1
  213.2 1.8 copy-start.2
Sparse Core Ops, SparseCore 0:
  19.0 56.3 all-gather.3
  77.2 60.9 all-gather.5

commit v2 on v1

v2 whole, which is shorter than its diff:
```python
import jax
import jax.numpy as jnp
from jax import lax
from jax.experimental import pallas as pl
from jax.experimental.pallas import tpu as pltpu
from jax.sharding import Mesh, PartitionSpec as P

first_fix = 0.99997343860111
second_fix = 0.0952078528

DP = ("x", "y", "zh")
FSDP = ("zl", "core")
BF = jnp.bfloat16
F32 = jnp.float32


def grad_kernel(where_ref, ranks_ref, grads_ref, out_ref):
    del where_ref
    product = jnp.dot(ranks_ref[...], grads_ref[...], preferred_element_type=F32).astype(BF)
    width = out_ref.shape[-1]
    for i in range(out_ref.shape[0]):
        out_ref[i] = product[:, i * width : (i + 1) * width]


def grad_blocks(target, ranks, out_grads, blocks, width):
    rank_local, tokens = ranks.shape
    step = 4
    count = blocks // step
    return pl.pallas_call(
        grad_kernel,
        grid_spec=pltpu.PrefetchScalarGridSpec(
            num_scalar_prefetch=1,
            grid=(count,),
            in_specs=[
                pl.BlockSpec((rank_local, tokens), lambda j, w: (0, 0)),
                pl.BlockSpec((tokens, step * width), lambda j, w: (0, w[0] * count + j)),
            ],
            out_specs=pl.BlockSpec((step, rank_local, width), lambda j, w: (j, 0, 0)),
        ),
        out_shape=jax.ShapeDtypeStruct((blocks, rank_local, width), BF),
        compiler_params=pltpu.CompilerParams(vmem_limit_bytes=60 * 2**20),
        cost_estimate=pl.CostEstimate(flops=1024, bytes_accessed=1024, transcendentals=0),
    )(target, ranks, out_grads)


def lift_kernel(where_ref, *refs):
    pieces, weights, rest = refs[:4], refs[4:8], refs[8:]
    basis_ref, (out_ref, dirs, old, sems) = rest[0], rest[-4:]
    zl = where_ref[1]
    step = pl.program_id(0)
    pair = pieces[0].shape[0]
    copies = [
        pltpu.make_async_copy(weights[i], old.at[i], sems.at[i]) for i in range(4)
    ]

    @pl.when(step == 0)
    def _():
        for copy in copies:
            copy.start()
        for r, piece in enumerate(pieces):
            at = lax.rem(zl - r + 4, 4) * pair
            dirs[pl.ds(pl.multiple_of(at, pair), pair), :] = piece[...]

    for r in range(4):

        @pl.when(step == r)
        def _():
            copies[r].wait()

    part = basis_ref.shape[3]
    for x in range(4):
        block = jnp.concatenate([basis_ref[x, y, 0] for y in range(4)], axis=-1)
        lifted = jnp.dot(block, dirs[...], preferred_element_type=F32)
        before = old[step, x * part : (x + 1) * part, :].astype(F32)
        out_ref[x * part : (x + 1) * part, :] = (before - 8.0 * lifted).astype(BF)


def lift(where, pieces, weights, basis, filled=None):
    rows, width = weights[0].shape
    pair = pieces[0].shape[0]
    part, lanes = basis.shape[3:]
    anywhere = pl.BlockSpec(memory_space=pl.ANY)
    extra = [] if filled is None else [filled]
    return pl.pallas_call(
        lift_kernel,
        grid_spec=pltpu.PrefetchScalarGridSpec(
            num_scalar_prefetch=1,
            grid=(4,),
            in_specs=[pl.BlockSpec((pair, width), lambda i, w: (0, 0))] * 4
            + [anywhere] * 4
            + [pl.BlockSpec((4, 4, 1, part, lanes), lambda i, w: (0, 0, i, 0, 0))]
            + [anywhere] * len(extra),
            out_specs=pl.BlockSpec(
                (rows, width), lambda i, w: (lax.rem(w[1] - i + 4, 4) * 2 + w[0], 0)
            ),
            scratch_shapes=[
                pltpu.VMEM((4 * pair, width), BF),
                pltpu.VMEM((4, rows, width), BF),
                pltpu.SemaphoreType.DMA((4,)),
            ],
        ),
        out_shape=jax.ShapeDtypeStruct((8 * rows, width), BF),
        input_output_aliases={} if filled is None else {10: 0},
        compiler_params=pltpu.CompilerParams(vmem_limit_bytes=56 * 2**20),
        cost_estimate=pl.CostEstimate(
            flops=8 * rows * 4 * pair * width,
            bytes_accessed=8 * rows * (2 * width + 4 * pair),
            transcendentals=0,
        ),
    )(where, *pieces, *weights, basis, *extra)


def swap(value, axis):
    return lax.ppermute(value, axis, [(0, 1), (1, 0)])


def around(value, shift, axis="zl"):
    return lax.ppermute(value, axis, [(i, (i + shift) % 4) for i in range(4)])


def pick(value, at, axis=0):
    return lax.dynamic_index_in_dim(value, at, axis, keepdims=False)


def after(value, *others):
    return lax.optimization_barrier((value, *others))


def shards(acts, out_grads, basis, weight, first_moment, second_moment):
    rank_local, width = first_moment.shape
    rows, rank = basis.shape
    tokens = acts.shape[0]
    x, y, zh, zl, core = (lax.axis_index(a) for a in ("x", "y", "zh", "zl", "core"))

    with jax.named_scope("gather_ahead"):
        tile = lax.dynamic_slice(basis, (x * (rows // 4), y * (rank // 4)), (rows // 4, rank // 4))
        tiles = [tile] + [around(tile, r) for r in range(1, 4)]
        first_hop = around(weight, 1)

    with jax.named_scope("project"):
        partial_t = lax.dot_general(
            basis, acts, (((0,), (1,)), ((), ())), preferred_element_type=F32
        ).reshape(4, 2, rank_local, tokens)
    partial_t, *tiles = after(partial_t, *tiles)
    with jax.named_scope("gather_ahead"):
        mine = lax.all_gather(jnp.stack(tiles), ("x", "y")).reshape((4, 4, 4) + tile.shape)
    with jax.named_scope("project"):
        got = swap(pick(partial_t, 1 - core, 1).astype(BF), "core")
        mixed = pick(partial_t, core, 1) + got.astype(F32)
        total = pick(mixed, zl)
        for r in range(1, 4):
            total = total + around(pick(mixed, (zl + r) % 4).astype(BF), r).astype(F32)
        ranks_t = total.astype(BF)

    ranks_t, first_hop, weight = after(ranks_t, first_hop, weight)
    with jax.named_scope("gather_ahead"):
        second_hop = around(first_hop, 1)
        others = [swap(weight, "core")]

    with jax.named_scope("grad"):
        sums = []
        for r in (2, 1, 3, 0):
            target = jnp.reshape((x + r) % 4, (1,)).astype(jnp.int32)
            blocks = grad_blocks(target, ranks_t, out_grads, 8, width)
            ranks_t, blocks = after(ranks_t, blocks)
            sums.append(around(blocks, r, "x") if r else blocks)
        over_x = sum(part.astype(F32) for part in sums).reshape(4, 2, rank_local, width)
    over_x, first_hop, second_hop, others[0] = after(over_x, first_hop, second_hop, others[0])
    with jax.named_scope("gather_ahead"):
        third_hop = around(second_hop, 1)
        others.append(swap(first_hop, "core"))
    with jax.named_scope("grad"):
        halves = pick(over_x, y)
        for r in range(1, 4):
            halves = halves + around(pick(over_x, (y + r) % 4).astype(BF), r, "y").astype(F32)
    halves, second_hop, others[1] = after(halves, second_hop, others[1])
    with jax.named_scope("gather_ahead"):
        others.append(swap(second_hop, "core"))
    with jax.named_scope("grad"):
        grad = pick(halves, zh) + swap(pick(halves, 1 - zh).astype(BF), "zh").astype(F32)

    with jax.named_scope("adam"):
        new_first = 0.9 * first_moment + 0.1 * grad
        new_second = 0.999 * second_moment + 0.001 * grad * grad
        direction = (
            new_first / first_fix / (jnp.sqrt(new_second / second_fix) + 1e-08)
        ).astype(BF)

    with jax.named_scope("lift"):
        theirs = swap(direction, "core")
        theirs, third_hop, mine, others[2] = after(theirs, third_hop, mine, others[2])
        pair = jnp.where(
            core == 0,
            jnp.concatenate([direction, theirs]),
            jnp.concatenate([theirs, direction]),
        )
        pieces = [pair] + [around(pair, r) for r in range(1, 4)]
        other = swap(mine, "core")
        others.append(swap(third_hop, "core"))
        hops = [weight, first_hop, second_hop, third_hop]
        where = jnp.stack([core, zl]).astype(jnp.int32)
        half_done = lift(where, pieces, hops, mine)
        where = jnp.stack([1 - core, zl]).astype(jnp.int32)
        new_weight = lift(where, pieces, others, other, half_done)
    return (new_weight, new_first, new_second)


def solution(mesh):
    split = Mesh(mesh.devices.reshape(4, 4, 2, 4, 2), DP + FSDP)
    placed = (
        P(DP, FSDP),
        P(DP, None),
        P(FSDP, None),
        P(FSDP, DP),
        P(FSDP, DP),
        P(FSDP, DP),
    )
    return jax.shard_map(
        shards,
        mesh=split,
        in_specs=placed,
        out_specs=(P(None, DP), P(FSDP, DP), P(FSDP, DP)),
        check_vma=False,
    )
```

time: 231 us -> 162 us (0.70)
  waiting for transfers between devices: 147 us -> 55.8 us
  starting transfers between devices: 29.6 us -> 41.4 us
  Pallas kernels: 25.4 us -> 32.4 us
  other arithmetic: 4.31 us -> 9.17 us
  local copies, waits for them, and re-layouts: 7.64 us -> 5 us
    all_gather x2 -> x1, waiting for transfers between devices: 107 us -> 0.01 us  [shards(): lax.all_gather(jnp.stack(tiles), ('x', 'y')).reshape((4, 4, 4) + tile.shape)]
    ppermute x9 -> x18, waiting for transfers between devices: 11.4 us -> 44.8 us  [around(): return lax.ppermute(value, axis, [(i, (i + shift) % 4) for i in range(4)])]
    all_to_all x1 -> x0, waiting for transfers between devices: 23.7 us -> none  [shards(): parts = lax.all_to_all(blocks, ('x', 'y'), 0, 0)]
    ppermute x9 -> x18, starting transfers between devices: 13.1 us -> 28.8 us  [around(): return lax.ppermute(value, axis, [(i, (i + shift) % 4) for i in range(4)])]
    ppermute x5 -> x8, waiting for transfers between devices: 4.08 us -> 10.9 us  [swap(): return lax.ppermute(value, axis, [(0, 1), (1, 0)])]
    pallas_call x1 -> x2, Pallas kernels: 8.63 us -> 15 us  [lift(): pl.pallas_call(lift_kernel, grid_spec=pltpu.PrefetchScalarGridSpec(num_sc...]
    all_to_all x1 -> x0, starting transfers between devices: 6.16 us -> none  [shards(): parts = lax.all_to_all(blocks, ('x', 'y'), 0, 0)]
    unnamed x14 -> x22, local copies, waits for them, and re-layouts: 6.48 us -> 1.95 us
  transfers between devices with their start and end apart: 17 -> 27, of which waited for: 10 -> 12; matrix products, arithmetic and copies ran while one was open for 3% -> 9% of each run, Pallas kernels for 7% -> 15%
where the time goes in v2:
time: 162 us
  waiting for transfers between devices  55.8 us (34%)
  starting transfers between devices  41.4 us (26%)
  Pallas kernels  32.4 us (20%)
  between operations  14.2 us (9%)
  other arithmetic  9.17 us (6%)
  local copies, waits for them, and re-layouts  5 us (3%)
  matrix products  3.79 us (2%)
    ppermute x18, waiting for transfers between devices, around(): return lax.ppermute(value, axis, [(i, (i + shift) % 4) for i in range(4)])  44.8 us
    ppermute x18, starting transfers between devices, around(): return lax.ppermute(value, axis, [(i, (i + shift) % 4) for i in range(4)])  28.8 us
    pallas_call x4, Pallas kernels, grad_blocks(): pl.pallas_call(grad_kernel, grid_spec=pltpu.PrefetchScalarGridSpec(num_sc...  17.5 us
    pallas_call x2, Pallas kernels, lift(): pl.pallas_call(lift_kernel, grid_spec=pltpu.PrefetchScalarGridSpec(num_sc...  15 us
    ppermute x8, starting transfers between devices, swap(): return lax.ppermute(value, axis, [(0, 1), (1, 0)])  12.5 us
    ppermute x8, waiting for transfers between devices, swap(): return lax.ppermute(value, axis, [(0, 1), (1, 0)])  10.9 us
    dot_general x1, matrix products, shards(): lax.dot_general(basis, acts, (((0,), (1,)), ((), ())), preferred_element_...  3.79 us
  transfers between devices with their start and end apart: 27, of which 12 were waited for; matrix products, arithmetic and copies ran while one was open for 9% of the time, Pallas kernels for 15%

profile of v2, /device:TPU:1, one launch (start us, length us, event | category | flops | bytes accessed | tf_op | source)
XLA Modules:
  0.0 161.8 jit_solution(4483552654890820327)
XLA Ops:
  8.2 2.5 %collective-permute-start = (bf16[224,128]{1,0:T(8,128)(2,1)S(1)}, bf16[224,128]{1,0:T(8,128)(2,1)S(1)}, u32[]{:S(2)}, u32[]{:S(2)}) collective-permute-start(bf16[224,128]{1,0:T(8,128)(2,1)S(1)} %dynamic_slice.43), channel_id=1, source_target_pairs={{0,2},{2,4},{4,6},{6,0},{1,3},{3,5},{5,7},{7,1},{8,10},{10,12},{12... | collective-permute-start | bytes 172040 | tf_op jit(solution)/shard_map/gather_ahead/ppermute | solution.py:118
  10.7 3.0 %collective-permute-start.1 = (bf16[224,128]{1,0:T(8,128)(2,1)S(1)}, bf16[224,128]{1,0:T(8,128)(2,1)S(1)}, u32[]{:S(2)}, u32[]{:S(2)}) collective-permute-start(bf16[224,128]{1,0:T(8,128)(2,1)S(1)} %dynamic_slice.43), channel_id=1, source_target_pairs={{0,4},{2,6},{4,0},{6,2},{1,5},{3,7},{5,1},{7,3},{8,12},{10,14},{12... | collective-permute-start | bytes 172040 | tf_op jit(solution)/shard_map/gather_ahead/ppermute | solution.py:118
  14.4 3.8 %fusion.15 = f32[512,1024]{1,0:T(8,128)} fusion(bf16[896,512]{1,0:T(8,128)(2,1)} %param.8, bf16[1024,896]{1,0:T(8,128)(2,1)S(1)} %copy-done), kind=kOutput, calls=%fused_computation.34 | convolution fusion | flops 939524096 | bytes 4849664 | tf_op jit(solution)/shard_map/project/dot_general | solution.py:141
  28.4 15.4 %collective-permute-done.4 = bf16[64,1024]{1,0:T(8,128)(2,1)S(1)} collective-permute-done((bf16[64,1024]{1,0:T(8,128)(2,1)S(1)}, bf16[64,1024]{1,0:T(8,128)(2,1)S(1)}, u32[]{:S(2)}, u32[]{:S(2)}) %collective-permute-start.4) | collective-permute-done | bytes 131104 | tf_op jit(solution)/shard_map/project/ppermute | solution.py:118
  43.7 5.9 %collective-permute-done.5 = bf16[64,1024]{1,0:T(8,128)(2,1)S(1)} collective-permute-done((bf16[64,1024]{1,0:T(8,128)(2,1)S(1)}, bf16[64,1024]{1,0:T(8,128)(2,1)S(1)}, u32[]{:S(2)}, u32[]{:S(2)}) %collective-permute-start.5) | collective-permute-done | bytes 131104 | tf_op jit(solution)/shard_map/project/ppermute | solution.py:118
  51.3 3.2 %collective-permute-start.11 = (bf16[896,384]{1,0:T(8,128)(2,1)}, bf16[896,384]{1,0:T(8,128)(2,1)}, u32[]{:S(2)}, u32[]{:S(2)}) collective-permute-start(bf16[896,384]{1,0:T(8,128)(2,1)} %collective-permute-done.7.refs_5_), channel_id=1, source_target_pairs={{0,2},{2,4},{4,6},{6,0},{1,3},{3,5},{5,7},{7,1},{8,10},{10,12},{12... | collective-permute-start | bytes 2064392 | tf_op jit(solution)/shard_map/gather_ahead/ppermute | solution.py:118
  55.3 4.5 %grad.4 = bf16[8,64,384]{2,1,0:T(8,128)(2,1)} custom-call(s32[1]{0:T(128)} %bitcast.9.where_ref, bf16[64,1024]{1,0:T(8,128)(2,1)} %fusion.3.ranks_ref, bf16[1024,12288]{1,0:T(8,128)(2,1)} %grads_ref.7), custom_call_target="tpu_custom_call" | custom-call | flops 1024 | bytes 1024 | tf_op jit(solution)/shard_map/grad/pallas_call | solution.py:29
  59.8 4.2 %grad.5 = bf16[8,64,384]{2,1,0:T(8,128)(2,1)} custom-call(s32[1]{0:T(128)} %bitcast.10.where_ref, bf16[64,1024]{1,0:T(8,128)(2,1)} %fusion.3.ranks_ref, bf16[1024,12288]{1,0:T(8,128)(2,1)} %grads_ref.7), custom_call_target="tpu_custom_call" | custom-call | flops 1024 | bytes 1024 | tf_op jit(solution)/shard_map/grad/pallas_call | solution.py:29
  64.1 4.5 %grad.6 = bf16[8,64,384]{2,1,0:T(8,128)(2,1)} custom-call(s32[1]{0:T(128)} %bitcast.11.where_ref, bf16[64,1024]{1,0:T(8,128)(2,1)} %fusion.3.ranks_ref, bf16[1024,12288]{1,0:T(8,128)(2,1)} %grads_ref.7), custom_call_target="tpu_custom_call" | custom-call | flops 1024 | bytes 1024 | tf_op jit(solution)/shard_map/grad/pallas_call | solution.py:29
  68.5 2.5 %collective-permute-start.10 = (bf16[8,64,384]{2,1,0:T(8,128)(2,1)}, bf16[8,64,384]{2,1,0:T(8,128)(2,1)}, u32[]{:S(2)}, u32[]{:S(2)}) collective-permute-start(bf16[8,64,384]{2,1,0:T(8,128)(2,1)} %grad.6), channel_id=1, source_target_pairs={{0,192},{64,0},{128,64},{192,128},{1,193},{65,1},{129,65},{193,129... | collective-permute-start | bytes 1179656 | tf_op jit(solution)/shard_map/grad/ppermute | solution.py:118
  71.0 1.7 %collective-permute-start.8 = (bf16[8,64,384]{2,1,0:T(8,128)(2,1)S(1)}, bf16[8,64,384]{2,1,0:T(8,128)(2,1)}, u32[]{:S(2)}, u32[]{:S(2)}) collective-permute-start(bf16[8,64,384]{2,1,0:T(8,128)(2,1)S(1)} %copy-done.7), channel_id=1, source_target_pairs={{0,128},{64,192},{128,0},{192,64},{1,129},{65,193},{129,1},{193,65... | collective-permute-start | bytes 1179656 | tf_op jit(solution)/shard_map/grad/ppermute | solution.py:118
  72.8 4.2 %grad.7 = bf16[8,64,384]{2,1,0:T(8,128)(2,1)} custom-call(s32[1]{0:T(128)} %bitcast.12.where_ref, bf16[64,1024]{1,0:T(8,128)(2,1)} %fusion.3.ranks_ref, bf16[1024,12288]{1,0:T(8,128)(2,1)} %grads_ref.7), custom_call_target="tpu_custom_call" | custom-call | flops 1024 | bytes 1024 | tf_op jit(solution)/shard_map/grad/pallas_call | solution.py:29
  77.0 5.9 %collective-permute-done.10 = bf16[8,64,384]{2,1,0:T(8,128)(2,1)} collective-permute-done((bf16[8,64,384]{2,1,0:T(8,128)(2,1)}, bf16[8,64,384]{2,1,0:T(8,128)(2,1)}, u32[]{:S(2)}, u32[]{:S(2)}) %collective-permute-start.10) | collective-permute-done | bytes 393248 | tf_op jit(solution)/shard_map/grad/ppermute | solution.py:118
  83.9 8.8 %collective-permute-done.8 = bf16[8,64,384]{2,1,0:T(8,128)(2,1)} collective-permute-done((bf16[8,64,384]{2,1,0:T(8,128)(2,1)S(1)}, bf16[8,64,384]{2,1,0:T(8,128)(2,1)}, u32[]{:S(2)}, u32[]{:S(2)}) %collective-permute-start.8) | collective-permute-done | bytes 393248 | tf_op jit(solution)/shard_map/grad/ppermute | solution.py:118
  96.3 2.4 %collective-permute-start.14 = (bf16[2,64,384]{2,1,0:T(8,128)(2,1)}, bf16[2,64,384]{2,1,0:T(8,128)(2,1)S(1)}, u32[]{:S(2)}, u32[]{:S(2)}) collective-permute-start(bf16[2,64,384]{2,1,0:T(8,128)(2,1)} %get-tuple-element.63), channel_id=1, source_target_pairs={{0,32},{16,48},{32,0},{48,16},{1,33},{17,49},{33,1},{49,17},{2,34}... | collective-permute-start | bytes 294920 | tf_op jit(solution)/shard_map/grad/ppermute | solution.py:118
  101.4 2.5 %collective-permute-done.14 = bf16[2,64,384]{2,1,0:T(8,128)(2,1)S(1)} collective-permute-done((bf16[2,64,384]{2,1,0:T(8,128)(2,1)}, bf16[2,64,384]{2,1,0:T(8,128)(2,1)S(1)}, u32[]{:S(2)}, u32[]{:S(2)}) %collective-permute-start.14) | collective-permute-done | bytes 98336 | tf_op jit(solution)/shard_map/grad/ppermute | solution.py:118
  106.6 5.5 %collective-permute-start.17 = (bf16[64,384]{1,0:T(8,128)(2,1)S(1)}, bf16[64,384]{1,0:T(8,128)(2,1)S(1)}, u32[]{:S(2)}, u32[]{:S(2)}) collective-permute-start(bf16[64,384]{1,0:T(8,128)(2,1)S(1)} %fusion.13), channel_id=1, source_target_pairs={{0,8},{8,0},{1,9},{9,1},{2,10},{10,2},{3,11},{11,3},{4,12},{12,4},... | collective-permute-start | bytes 147464 | tf_op jit(solution)/shard_map/grad/ppermute | solution.py:114
  112.1 9.3 %collective-permute-done.17 = bf16[64,384]{1,0:T(8,128)(2,1)S(1)} collective-permute-done((bf16[64,384]{1,0:T(8,128)(2,1)S(1)}, bf16[64,384]{1,0:T(8,128)(2,1)S(1)}, u32[]{:S(2)}, u32[]{:S(2)}) %collective-permute-start.17) | collective-permute-done | bytes 49184 | tf_op jit(solution)/shard_map/grad/ppermute | solution.py:114
  121.4 1.7 %divide_convert_fusion = (bf16[64,384]{1,0:T(8,128)(2,1)S(1)}, f32[64,384]{1,0:T(8,128)}, f32[64,384]{1,0:T(8,128)}) fusion(bf16[64,384]{1,0:T(8,128)(2,1)S(1)} %collective-permute-done.17, f32[2,64,384]{2,1,0:T(8,128)S(1)} %fusion.5, s32[]{:T(128)S(6)} %select_n.120, f32[64,384]{1,0:T(8,128)} %param.10, f32[64,384]{1,0:T(8,128)} %param.11), kind=kLoop, calls=%fused_computation.28 | loop fusion | flops 344064 | bytes 589828 | tf_op jit(solution)/shard_map/adam/convert_element_type | solution.py:187
  123.1 2.5 %collective-permute-start.18 = (bf16[64,384]{1,0:T(8,128)(2,1)S(1)}, bf16[64,384]{1,0:T(8,128)(2,1)S(1)}, u32[]{:S(2)}, u32[]{:S(2)}) collective-permute-start(bf16[64,384]{1,0:T(8,128)(2,1)S(1)} %get-tuple-element.55), channel_id=1, source_target_pairs={{0,1},{1,0},{2,3},{3,2},{4,5},{5,4},{6,7},{7,6},{8,9},{9,8},{10,11... | collective-permute-start | bytes 147464 | tf_op jit(solution)/shard_map/lift/ppermute | solution.py:114
  127.6 3.2 %collective-permute-start.21 = (bf16[128,384]{1,0:T(8,128)(2,1)S(1)}, bf16[128,384]{1,0:T(8,128)(2,1)S(1)}, u32[]{:S(2)}, u32[]{:S(2)}) collective-permute-start(bf16[128,384]{1,0:T(8,128)(2,1)S(1)} %maximum_select_fusion.refs_0_), channel_id=1, source_target_pairs={{0,2},{2,4},{4,6},{6,0},{1,3},{3,5},{5,7},{7,1},{8,10},{10,12},{12... | collective-permute-start | bytes 294920 | tf_op jit(solution)/shard_map/lift/ppermute | solution.py:118
  133.9 4.7 %collective-permute-done.22.refs_2_ = bf16[128,384]{1,0:T(8,128)(2,1)S(1)} collective-permute-done((bf16[128,384]{1,0:T(8,128)(2,1)S(1)}, bf16[128,384]{1,0:T(8,128)(2,1)S(1)}, u32[]{:S(2)}, u32[]{:S(2)}) %collective-permute-start.22) | collective-permute-done | bytes 98336 | tf_op jit(solution)/shard_map/lift/ppermute | solution.py:118
  139.9 7.5 %lift.2.refs_9_ = bf16[7168,384]{1,0:T(8,128)(2,1)} custom-call(s32[2]{0:T(128)} %pad_add_fusion.1.where_ref, bf16[128,384]{1,0:T(8,128)(2,1)} %copy-done.1, bf16[128,384]{1,0:T(8,128)(2,1)} %copy-done.4, bf16[128,384]{1,0:T(8,128)(2,1)} %copy-done.5, bf16[128,384]{1,0:T(8,128)(2,1)} %copy-done.6, bf16[896,384]{1,0:T(8,128)(2,1)} %refs_4_, ...), custom_call_target="tpu_custom_call" | custom-call | flops 1409286144 | bytes 9175040 | tf_op jit(solution)/shard_map/lift/pallas_call | solution.py:84
  147.5 7.5 %lift.3 = bf16[7168,384]{1,0:T(8,128)(2,1)} custom-call(s32[2]{0:T(128)} %pad_add_fusion.where_ref, bf16[128,384]{1,0:T(8,128)(2,1)} %copy-done.1, bf16[128,384]{1,0:T(8,128)(2,1)} %copy-done.4, bf16[128,384]{1,0:T(8,128)(2,1)} %copy-done.5, bf16[128,384]{1,0:T(8,128)(2,1)} %copy-done.6, ...), custom_call_target="tpu_custom_call", output_to_operand_aliasing={{}: (10, {})} | custom-call | flops 1409286144 | bytes 9175040 | tf_op jit(solution)/shard_map/lift/pallas_call | solution.py:84
  (74 shorter events, 30.5 us)
Async XLA Ops:
  7.2 119.3 %all-gather.3.cloned.1.call-start = ((), (), s32[]{:S(2)}) async-start(), calls=%async_computation | async-start | bytes 3899392 | tf_op jit(solution)/shard_map/gather_ahead/all_gather | solution.py:146
  8.2 10.0 %collective-permute-start = (bf16[224,128]{1,0:T(8,128)(2,1)S(1)}, bf16[224,128]{1,0:T(8,128)(2,1)S(1)}, u32[]{:S(2)}, u32[]{:S(2)}) collective-permute-start(bf16[224,128]{1,0:T(8,128)(2,1)S(1)} %dynamic_slice.43), channel_id=1, source_target_pairs={{0,2},{2,4},{4,6},{6,0},{1,3},{3,5},{5,7},{7,1},{8,10},{10,12},{12... | collective-permute-start | bytes 172040 | tf_op jit(solution)/shard_map/gather_ahead/ppermute | solution.py:118
  10.7 7.5 %collective-permute-start.1 = (bf16[224,128]{1,0:T(8,128)(2,1)S(1)}, bf16[224,128]{1,0:T(8,128)(2,1)S(1)}, u32[]{:S(2)}, u32[]{:S(2)}) collective-permute-start(bf16[224,128]{1,0:T(8,128)(2,1)S(1)} %dynamic_slice.43), channel_id=1, source_target_pairs={{0,4},{2,6},{4,0},{6,2},{1,5},{3,7},{5,1},{7,3},{8,12},{10,14},{12... | collective-permute-start | bytes 172040 | tf_op jit(solution)/shard_map/gather_ahead/ppermute | solution.py:118
  21.8 29.5 %collective-permute-start.7 = (bf16[896,384]{1,0:T(8,128)(2,1)}, bf16[896,384]{1,0:T(8,128)(2,1)}, u32[]{:S(2)}, u32[]{:S(2)}) collective-permute-start(bf16[896,384]{1,0:T(8,128)(2,1)} %refs_4_), channel_id=1, source_target_pairs={{0,2},{2,4},{4,6},{6,0},{1,3},{3,5},{5,7},{7,1},{8,10},{10,12},{12... | collective-permute-start | bytes 2064392 | tf_op jit(solution)/shard_map/gather_ahead/ppermute | solution.py:118
  24.8 18.9 %collective-permute-start.4 = (bf16[64,1024]{1,0:T(8,128)(2,1)S(1)}, bf16[64,1024]{1,0:T(8,128)(2,1)S(1)}, u32[]{:S(2)}, u32[]{:S(2)}) collective-permute-start(bf16[64,1024]{1,0:T(8,128)(2,1)S(1)} %get-tuple-element.58), channel_id=1, source_target_pairs={{0,2},{2,4},{4,6},{6,0},{1,3},{3,5},{5,7},{7,1},{8,10},{10,12},{12... | collective-permute-start | bytes 393224 | tf_op jit(solution)/shard_map/project/ppermute | solution.py:118
  25.6 24.1 %collective-permute-start.5 = (bf16[64,1024]{1,0:T(8,128)(2,1)S(1)}, bf16[64,1024]{1,0:T(8,128)(2,1)S(1)}, u32[]{:S(2)}, u32[]{:S(2)}) collective-permute-start(bf16[64,1024]{1,0:T(8,128)(2,1)S(1)} %get-tuple-element.60), channel_id=1, source_target_pairs={{0,4},{2,6},{4,0},{6,2},{1,5},{3,7},{5,1},{7,3},{8,12},{10,14},{12... | collective-permute-start | bytes 393224 | tf_op jit(solution)/shard_map/project/ppermute | solution.py:118
  27.2 22.5 %collective-permute-start.6 = (bf16[64,1024]{1,0:T(8,128)(2,1)S(1)}, bf16[64,1024]{1,0:T(8,128)(2,1)}, u32[]{:S(2)}, u32[]{:S(2)}) collective-permute-start(bf16[64,1024]{1,0:T(8,128)(2,1)S(1)} %get-tuple-element.59), channel_id=1, source_target_pairs={{0,6},{2,0},{4,2},{6,4},{1,7},{3,1},{5,3},{7,5},{8,14},{10,8},{12,... | collective-permute-start | bytes 393224 | tf_op jit(solution)/shard_map/project/ppermute | solution.py:118
  51.3 43.0 %collective-permute-start.11 = (bf16[896,384]{1,0:T(8,128)(2,1)}, bf16[896,384]{1,0:T(8,128)(2,1)}, u32[]{:S(2)}, u32[]{:S(2)}) collective-permute-start(bf16[896,384]{1,0:T(8,128)(2,1)} %collective-permute-done.7.refs_5_), channel_id=1, source_target_pairs={{0,2},{2,4},{4,6},{6,0},{1,3},{3,5},{5,7},{7,1},{8,10},{10,12},{12... | collective-permute-start | bytes 2064392 | tf_op jit(solution)/shard_map/gather_ahead/ppermute | solution.py:118
  54.5 39.8 %collective-permute-start.12 = (bf16[896,384]{1,0:T(8,128)(2,1)}, bf16[896,384]{1,0:T(8,128)(2,1)S(1)}, u32[]{:S(2)}, u32[]{:S(2)}) collective-permute-start(bf16[896,384]{1,0:T(8,128)(2,1)} %refs_4_), channel_id=1, source_target_pairs={{0,1},{1,0},{2,3},{3,2},{4,5},{5,4},{6,7},{7,6},{8,9},{9,8},{10,11... | collective-permute-start | bytes 2064392 | tf_op jit(solution)/shard_map/gather_ahead/ppermute | solution.py:114
  68.5 14.4 %collective-permute-start.10 = (bf16[8,64,384]{2,1,0:T(8,128)(2,1)}, bf16[8,64,384]{2,1,0:T(8,128)(2,1)}, u32[]{:S(2)}, u32[]{:S(2)}) collective-permute-start(bf16[8,64,384]{2,1,0:T(8,128)(2,1)} %grad.6), channel_id=1, source_target_pairs={{0,192},{64,0},{128,64},{192,128},{1,193},{65,1},{129,65},{193,129... | collective-permute-start | bytes 1179656 | tf_op jit(solution)/shard_map/grad/ppermute | solution.py:118
  71.0 12.9 %collective-permute-start.9 = (bf16[8,64,384]{2,1,0:T(8,128)(2,1)S(1)}, bf16[8,64,384]{2,1,0:T(8,128)(2,1)}, u32[]{:S(2)}, u32[]{:S(2)}) collective-permute-start(bf16[8,64,384]{2,1,0:T(8,128)(2,1)S(1)} %copy-done.8), channel_id=1, source_target_pairs={{0,64},{64,128},{128,192},{192,0},{1,65},{65,129},{129,193},{193,1... | collective-permute-start | bytes 1179656 | tf_op jit(solution)/shard_map/grad/ppermute | solution.py:118
  71.0 21.7 %collective-permute-start.8 = (bf16[8,64,384]{2,1,0:T(8,128)(2,1)S(1)}, bf16[8,64,384]{2,1,0:T(8,128)(2,1)}, u32[]{:S(2)}, u32[]{:S(2)}) collective-permute-start(bf16[8,64,384]{2,1,0:T(8,128)(2,1)S(1)} %copy-done.7), channel_id=1, source_target_pairs={{0,128},{64,192},{128,0},{192,64},{1,129},{65,193},{129,1},{193,65... | collective-permute-start | bytes 1179656 | tf_op jit(solution)/shard_map/grad/ppermute | solution.py:118
  94.3 11.3 %collective-permute-start.16 = (bf16[896,384]{1,0:T(8,128)(2,1)}, bf16[896,384]{1,0:T(8,128)(2,1)}, u32[]{:S(2)}, u32[]{:S(2)}) collective-permute-start(bf16[896,384]{1,0:T(8,128)(2,1)} %collective-permute-done.7.refs_5_), channel_id=1, source_target_pairs={{0,1},{1,0},{2,3},{3,2},{4,5},{5,4},{6,7},{7,6},{8,9},{9,8},{10,11... | collective-permute-start | bytes 2064392 | tf_op jit(solution)/shard_map/gather_ahead/ppermute | solution.py:114
  95.6 5.8 %collective-permute-start.13 = (bf16[2,64,384]{2,1,0:T(8,128)(2,1)}, bf16[2,64,384]{2,1,0:T(8,128)(2,1)S(1)}, u32[]{:S(2)}, u32[]{:S(2)}) collective-permute-start(bf16[2,64,384]{2,1,0:T(8,128)(2,1)} %get-tuple-element.61), channel_id=1, source_target_pairs={{0,16},{16,32},{32,48},{48,0},{1,17},{17,33},{33,49},{49,1},{2,18}... | collective-permute-start | bytes 294920 | tf_op jit(solution)/shard_map/grad/ppermute | solution.py:118
  96.3 7.6 %collective-permute-start.14 = (bf16[2,64,384]{2,1,0:T(8,128)(2,1)}, bf16[2,64,384]{2,1,0:T(8,128)(2,1)S(1)}, u32[]{:S(2)}, u32[]{:S(2)}) collective-permute-start(bf16[2,64,384]{2,1,0:T(8,128)(2,1)} %get-tuple-element.63), channel_id=1, source_target_pairs={{0,32},{16,48},{32,0},{48,16},{1,33},{17,49},{33,1},{49,17},{2,34}... | collective-permute-start | bytes 294920 | tf_op jit(solution)/shard_map/grad/ppermute | solution.py:118
  98.7 5.8 %collective-permute-start.15 = (bf16[2,64,384]{2,1,0:T(8,128)(2,1)}, bf16[2,64,384]{2,1,0:T(8,128)(2,1)}, u32[]{:S(2)}, u32[]{:S(2)}) collective-permute-start(bf16[2,64,384]{2,1,0:T(8,128)(2,1)} %get-tuple-element.62), channel_id=1, source_target_pairs={{0,48},{16,0},{32,16},{48,32},{1,49},{17,1},{33,17},{49,33},{2,50}... | collective-permute-start | bytes 294920 | tf_op jit(solution)/shard_map/grad/ppermute | solution.py:118
  99.9 25.7 %collective-permute-start.19 = (bf16[896,384]{1,0:T(8,128)(2,1)}, bf16[896,384]{1,0:T(8,128)(2,1)}, u32[]{:S(2)}, u32[]{:S(2)}) collective-permute-start(bf16[896,384]{1,0:T(8,128)(2,1)} %collective-permute-done.11.refs_6_), channel_id=1, source_target_pairs={{0,2},{2,4},{4,6},{6,0},{1,3},{3,5},{5,7},{7,1},{8,10},{10,12},{12... | collective-permute-start | bytes 2064392 | tf_op jit(solution)/shard_map/gather_ahead/ppermute | solution.py:118
  105.6 20.8 %collective-permute-start.20 = (bf16[896,384]{1,0:T(8,128)(2,1)}, bf16[896,384]{1,0:T(8,128)(2,1)S(1)}, u32[]{:S(2)}, u32[]{:S(2)}) collective-permute-start(bf16[896,384]{1,0:T(8,128)(2,1)} %collective-permute-done.11.refs_6_), channel_id=1, source_target_pairs={{0,1},{1,0},{2,3},{3,2},{4,5},{5,4},{6,7},{7,6},{8,9},{9,8},{10,11... | collective-permute-start | bytes 2064392 | tf_op jit(solution)/shard_map/gather_ahead/ppermute | solution.py:114
  106.6 14.8 %collective-permute-start.17 = (bf16[64,384]{1,0:T(8,128)(2,1)S(1)}, bf16[64,384]{1,0:T(8,128)(2,1)S(1)}, u32[]{:S(2)}, u32[]{:S(2)}) collective-permute-start(bf16[64,384]{1,0:T(8,128)(2,1)S(1)} %fusion.13), channel_id=1, source_target_pairs={{0,8},{8,0},{1,9},{9,1},{2,10},{10,2},{3,11},{11,3},{4,12},{12,4},... | collective-permute-start | bytes 147464 | tf_op jit(solution)/shard_map/grad/ppermute | solution.py:114
  126.4 21.0 %collective-permute-start.25 = (bf16[4,4,4,224,128]{4,3,2,1,0:T(8,128)(2,1)}, bf16[4,4,4,224,128]{4,3,2,1,0:T(8,128)(2,1)}, u32[]{:S(2)}, u32[]{:S(2)}) collective-permute-start(bf16[4,4,4,224,128]{4,3,2,1,0:T(8,128)(2,1)} %bitcast.56), channel_id=1, source_target_pairs={{0,1},{1,0},{2,3},{3,2},{4,5},{5,4},{6,7},{7,6},{8,9},{9,8},{10,11... | collective-permute-start | bytes 11010056 | tf_op jit(solution)/shard_map/lift/ppermute | solution.py:114
  126.9 20.6 %collective-permute-start.24 = (bf16[896,384]{1,0:T(8,128)(2,1)}, bf16[896,384]{1,0:T(8,128)(2,1)}, u32[]{:S(2)}, u32[]{:S(2)}) collective-permute-start(bf16[896,384]{1,0:T(8,128)(2,1)} %collective-permute-done.19.refs_7_), channel_id=1, source_target_pairs={{0,1},{1,0},{2,3},{3,2},{4,5},{5,4},{6,7},{7,6},{8,9},{9,8},{10,11... | collective-permute-start | bytes 2064392 | tf_op jit(solution)/shard_map/lift/ppermute | solution.py:114
  127.6 6.3 %collective-permute-start.21 = (bf16[128,384]{1,0:T(8,128)(2,1)S(1)}, bf16[128,384]{1,0:T(8,128)(2,1)S(1)}, u32[]{:S(2)}, u32[]{:S(2)}) collective-permute-start(bf16[128,384]{1,0:T(8,128)(2,1)S(1)} %maximum_select_fusion.refs_0_), channel_id=1, source_target_pairs={{0,2},{2,4},{4,6},{6,0},{1,3},{3,5},{5,7},{7,1},{8,10},{10,12},{12... | collective-permute-start | bytes 294920 | tf_op jit(solution)/shard_map/lift/ppermute | solution.py:118
  130.9 7.8 %collective-permute-start.22 = (bf16[128,384]{1,0:T(8,128)(2,1)S(1)}, bf16[128,384]{1,0:T(8,128)(2,1)S(1)}, u32[]{:S(2)}, u32[]{:S(2)}) collective-permute-start(bf16[128,384]{1,0:T(8,128)(2,1)S(1)} %maximum_select_fusion.refs_0_), channel_id=1, source_target_pairs={{0,4},{2,6},{4,0},{6,2},{1,5},{3,7},{5,1},{7,3},{8,12},{10,14},{12... | collective-permute-start | bytes 294920 | tf_op jit(solution)/shard_map/lift/ppermute | solution.py:118
  131.4 7.2 %collective-permute-start.23 = (bf16[128,384]{1,0:T(8,128)(2,1)S(1)}, bf16[128,384]{1,0:T(8,128)(2,1)S(1)}, u32[]{:S(2)}, u32[]{:S(2)}) collective-permute-start(bf16[128,384]{1,0:T(8,128)(2,1)S(1)} %maximum_select_fusion.refs_0_), channel_id=1, source_target_pairs={{0,6},{2,0},{4,2},{6,4},{1,7},{3,1},{5,3},{7,5},{8,14},{10,8},{12,... | collective-permute-start | bytes 294920 | tf_op jit(solution)/shard_map/lift/ppermute | solution.py:118
  (14 other events, 126.5 us)
Sparse Core Ops, SparseCore 0:
  19.0 57.5 all-gather.2

commit v3 on v1

v3 whole, which is shorter than its diff:
```python
import jax
import jax.numpy as jnp
from jax import lax
from jax.experimental import pallas as pl
from jax.experimental.pallas import tpu as pltpu
from jax.sharding import Mesh, PartitionSpec as P

first_fix = 0.99997343860111
second_fix = 0.0952078528

DP = ("x", "y", "zh")
FSDP = ("zl", "core")
BF = jnp.bfloat16
F32 = jnp.float32


def grad_kernel(ranks_ref, grads_ref, out_ref):
    product = jnp.dot(ranks_ref[...], grads_ref[...], preferred_element_type=F32).astype(BF)
    width = out_ref.shape[-1]
    for i in range(out_ref.shape[0]):
        out_ref[i] = product[:, i * width : (i + 1) * width]


def grad_blocks(ranks, out_grads, width):
    rank_local, tokens = ranks.shape
    blocks = out_grads.shape[1] // width
    step = 8
    return pl.pallas_call(
        grad_kernel,
        grid=(blocks // step,),
        in_specs=[
            pl.BlockSpec((rank_local, tokens), lambda j: (0, 0)),
            pl.BlockSpec((tokens, step * width), lambda j: (0, j)),
        ],
        out_specs=pl.BlockSpec((step, rank_local, width), lambda j: (j, 0, 0)),
        out_shape=jax.ShapeDtypeStruct((blocks, rank_local, width), BF),
        compiler_params=pltpu.CompilerParams(vmem_limit_bytes=60 * 2**20),
        cost_estimate=pl.CostEstimate(
            flops=8 * rank_local * tokens * blocks * width,
            bytes_accessed=2 * tokens * blocks * width,
            transcendentals=0,
        ),
    )(ranks, out_grads)


def lift_kernel(where_ref, *refs):
    pieces, weights, bases, rest = refs[:4], refs[4:12], refs[12:26], refs[26:]
    out_ref, dirs, old, base, done, in_sems, out_sems = rest
    y, zl, core = (where_ref[i] for i in range(3))
    pair = pieces[0].shape[0]
    rows = old.shape[2]
    lanes = base.shape[3] // 4
    loads = []
    for k in range(2):
        plane, *columns = bases[7 * k : 7 * k + 7]
        for z in range(4):
            sources = [plane.at[z]] + [columns[2 * i + z // 2].at[z % 2] for i in range(3)]
            group = [pltpu.make_async_copy(weights[4 * k + z], old.at[k, z], in_sems.at[k, z, 4])]
            for q, source in enumerate(sources):
                group.append(
                    pltpu.make_async_copy(
                        source,
                        base.at[k, z, :, q * lanes : (q + 1) * lanes],
                        in_sems.at[k, z, q],
                    )
                )
            for copy in group:
                copy.start()
            loads.append(group)
    for r, piece in enumerate(pieces):
        at = lax.rem(y - zl + r + 4, 4) * pair
        dirs[pl.ds(pl.multiple_of(at, pair), pair), :] = piece[...]
    stores = []
    for k in range(2):
        for z in range(4):
            for copy in loads[4 * k + z]:
                copy.wait()
            lifted = jnp.dot(base[k, z], dirs[...], preferred_element_type=F32)
            done[k, z] = (old[k, z].astype(F32) - 8.0 * lifted).astype(BF)
            owner = core if k == 0 else 1 - core
            at = (lax.rem(zl - z + 4, 4) * 2 + owner) * rows
            copy = pltpu.make_async_copy(
                done.at[k, z],
                out_ref.at[pl.ds(pl.multiple_of(at, rows), rows)],
                out_sems.at[k, z],
            )
            copy.start()
            stores.append(copy)
    for copy in stores:
        copy.wait()


def lift(where, pieces, weights, bases):
    rows, width = weights[0].shape
    pair = pieces[0].shape[0]
    lanes = bases[0].shape[2]
    anywhere = pl.BlockSpec(memory_space=pl.ANY)
    return pl.pallas_call(
        lift_kernel,
        in_specs=[pl.BlockSpec(memory_space=pltpu.SMEM)]
        + [pl.BlockSpec(memory_space=pltpu.VMEM)] * 4
        + [anywhere] * 22,
        out_specs=anywhere,
        scratch_shapes=[
            pltpu.VMEM((4 * pair, width), BF),
            pltpu.VMEM((2, 4, rows, width), BF),
            pltpu.VMEM((2, 4, rows, 4 * lanes), BF),
            pltpu.VMEM((2, 4, rows, width), BF),
            pltpu.SemaphoreType.DMA((2, 4, 5)),
            pltpu.SemaphoreType.DMA((2, 4)),
        ],
        out_shape=jax.ShapeDtypeStruct((8 * rows, width), BF),
        compiler_params=pltpu.CompilerParams(vmem_limit_bytes=56 * 2**20),
        cost_estimate=pl.CostEstimate(
            flops=16 * rows * 4 * pair * width,
            bytes_accessed=16 * rows * (2 * width + 4 * pair),
            transcendentals=0,
        ),
    )(where, *pieces, *weights, *bases)


def swap(value, axis):
    return lax.ppermute(value, axis, [(0, 1), (1, 0)])


def around(value, shift, axis="zl"):
    return lax.ppermute(value, axis, [(i, (i + shift) % 4) for i in range(4)])


def along_z(value, shift):
    return lax.ppermute(value, ("zh", "zl"), [(i, (i + shift) % 8) for i in range(8)])


def pick(value, at, axis=0):
    return lax.dynamic_index_in_dim(value, at, axis, keepdims=False)


def after(value, *others):
    return lax.optimization_barrier((value, *others))


def shards(acts, out_grads, basis, weight, first_moment, second_moment):
    rank_local, width = first_moment.shape
    rows, rank = basis.shape
    tokens = acts.shape[0]
    x, y, zh, zl, core = (lax.axis_index(a) for a in ("x", "y", "zh", "zl", "core"))

    with jax.named_scope("tiles"):
        tile = lax.dynamic_slice_in_dim(basis, y * (rank // 4), rank // 4, 1)
        below, above = along_z(tile, 1), along_z(tile, 7)
    with jax.named_scope("project"):
        partial_t = lax.dot_general(
            basis, acts, (((0,), (1,)), ((), ())), preferred_element_type=F32
        ).reshape(4, 2, rank_local, tokens)
    partial_t, below, above = after(partial_t, below, above)
    with jax.named_scope("tiles"):
        second = along_z(below, 1)
        low = jnp.stack([tile, below])
    with jax.named_scope("project"):
        got = swap(pick(partial_t, 1 - core, 1).astype(BF), "core")
        mixed = pick(partial_t, core, 1) + got.astype(F32)
    mixed, second = after(mixed, second)
    with jax.named_scope("tiles_y"):
        down_low, up_low = around(low, 1, "y"), around(low, 3, "y")
        high = jnp.stack([second, above])
    with jax.named_scope("project"):
        total = pick(mixed, zl)
        for r in range(1, 4):
            total = total + around(pick(mixed, (zl + r) % 4).astype(BF), r).astype(F32)
        ranks_t = total.astype(BF)
    ranks_t, down_low, up_low, weight = after(ranks_t, down_low, up_low, weight)
    with jax.named_scope("weight_hops"):
        hops = [weight, around(weight, 1)]
    with jax.named_scope("tiles_y"):
        down_high, up_high = around(high, 1, "y"), around(high, 3, "y")
    with jax.named_scope("grad"):
        blocks = grad_blocks(ranks_t, out_grads, width)
    blocks, hops[1], down_high, up_high = after(blocks, hops[1], down_high, up_high)
    with jax.named_scope("grad"):
        parts = lax.all_to_all(blocks.reshape(16, 2, rank_local, width), ("x", "y"), 0, 0)
    with jax.named_scope("tiles_y"):
        far_low, far_high = around(down_low, 1, "y"), around(up_high, 3, "y")
        plane = jnp.concatenate([low, high])
        bases = [plane, down_low, down_high, far_low, far_high, up_low, up_high]
    with jax.named_scope("weight_hops"):
        hops.append(around(hops[1], 1))
        hops.append(around(hops[2], 1))
    with jax.named_scope("other_core"):
        other_bases = [swap(b, "core") for b in bases]
        others = [swap(h, "core") for h in hops[:3]]
    parts, hops[3], *swapped = after(parts, hops[3], *other_bases, *others)
    other_bases, others = swapped[:7], swapped[7:]
    with jax.named_scope("grad"):
        halves = jnp.sum(parts.astype(F32), axis=0)
        grad = pick(halves, zh) + swap(pick(halves, 1 - zh).astype(BF), "zh").astype(F32)

    with jax.named_scope("adam"):
        new_first = 0.9 * first_moment + 0.1 * grad
        new_second = 0.999 * second_moment + 0.001 * grad * grad
        direction = (
            new_first / first_fix / (jnp.sqrt(new_second / second_fix) + 1e-08)
        ).astype(BF)

    with jax.named_scope("other_core"):
        others.append(swap(hops[3], "core"))
    with jax.named_scope("lift"):
        theirs = swap(direction, "core")
        pair = jnp.where(
            core == 0,
            jnp.concatenate([direction, theirs]),
            jnp.concatenate([theirs, direction]),
        )
        pieces = [pair] + [around(pair, r) for r in range(1, 4)]
        where = jnp.stack([y, zl, core]).astype(jnp.int32)
        new_weight = lift(where, pieces, hops + others, bases + other_bases)
    return (new_weight, new_first, new_second)


def solution(mesh):
    split = Mesh(mesh.devices.reshape(4, 4, 2, 4, 2), DP + FSDP)
    placed = (
        P(DP, FSDP),
        P(DP, None),
        P(FSDP, None),
        P(FSDP, DP),
        P(FSDP, DP),
        P(FSDP, DP),
    )
    return jax.shard_map(
        shards,
        mesh=split,
        in_specs=placed,
        out_specs=(P(None, DP), P(FSDP, DP), P(FSDP, DP)),
        check_vma=False,
    )
```

time: 231 us -> 141 us (0.61)
  waiting for transfers between devices: 147 us -> 57.7 us
  starting transfers between devices: 29.6 us -> 44.9 us
  between operations: 14.2 us -> 0.98 us
  other arithmetic: 4.31 us -> 10.5 us
  Pallas kernels: 25.4 us -> 19.9 us
  local copies, waits for them, and re-layouts: 7.64 us -> 3.52 us
    all_gather x2 -> x0, waiting for transfers between devices: 107 us -> none  [the longest x1 56.5 us: shards(): weight_mine = lax.all_gather(weight, 'zl')]
    ppermute x9 -> x18, waiting for transfers between devices: 11.4 us -> 48.2 us  [the longest x15 40.7 us: around(): return lax.ppermute(value, axis, [(i, (i + shift) % 4) for i in range(4)])]
    all_to_all x1, waiting for transfers between devices: 23.7 us -> 0.01 us  [shards(): lax.all_to_all(blocks.reshape(16, 2, rank_local, width), ('x', 'y'), 0, 0)]
    ppermute x9 -> x18, starting transfers between devices: 13.1 us -> 22 us  [the longest x15 15.4 us: around(): return lax.ppermute(value, axis, [(i, (i + shift) % 4) for i in range(4)])]
    pallas_call x2, Pallas kernels: 25.4 us -> 19.9 us  [the longest x1 11 us: grad_blocks(): pl.pallas_call(grad_kernel, grid=(blocks // step,), in_specs=[pl.BlockSpe...]
    ppermute x5 -> x14, waiting for transfers between devices: 4.08 us -> 9.55 us  [swap(): return lax.ppermute(value, axis, [(0, 1), (1, 0)])]
    unnamed x14 -> x18, local copies, waits for them, and re-layouts: 6.48 us -> 1.36 us
    ppermute x5 -> x14, starting transfers between devices: 10.2 us -> 14.9 us  [swap(): return lax.ppermute(value, axis, [(0, 1), (1, 0)])]
  transfers between devices with their start and end apart: 17 -> 33, of which waited for: 10 -> 14; matrix products, arithmetic and copies ran while one was open for 3% -> 10% of each run, Pallas kernels for 7% -> 8%
where the time goes in v3:
time: 141 us; the launch traced here: 140 us
  waiting for transfers between devices  57.7 us (41%)
  starting transfers between devices  44.9 us (32%)
  Pallas kernels  19.9 us (14%)
  other arithmetic  10.5 us (7%)
  local copies, waits for them, and re-layouts  3.52 us (2%)
  matrix products  2.48 us (2%)
    ppermute x15, waiting for transfers between devices, around(): return lax.ppermute(value, axis, [(i, (i + shift) % 4) for i in range(4)])  40.7 us
    ppermute x15, starting transfers between devices, around(): return lax.ppermute(value, axis, [(i, (i + shift) % 4) for i in range(4)])  15.4 us
    ppermute x14, starting transfers between devices, swap(): return lax.ppermute(value, axis, [(0, 1), (1, 0)])  14.9 us
    pallas_call x1, Pallas kernels, grad_blocks(): pl.pallas_call(grad_kernel, grid=(blocks // step,), in_specs=[pl.BlockSpe...  11 us
    ppermute x14, waiting for transfers between devices, swap(): return lax.ppermute(value, axis, [(0, 1), (1, 0)])  9.55 us
    pallas_call x1, Pallas kernels, lift(): pl.pallas_call(lift_kernel, in_specs=[pl.BlockSpec(memory_space=pltpu.SME...  8.86 us
    all_to_all x1, starting transfers between devices, shards(): lax.all_to_all(blocks.reshape(16, 2, rank_local, width), ('x', 'y'), 0, 0)  8.03 us
    ppermute x3, waiting for transfers between devices, along_z(): lax.ppermute(value, ('zh', 'zl'), [(i, (i + shift) % 8) for i in range(8)])  7.48 us
  transfers between devices with their start and end apart: 33, of which 14 were waited for; matrix products, arithmetic and copies ran while one was open for 10% of the time, Pallas kernels for 8%

profile of v3, /device:TPU:1, one launch (start us, length us, event | category | flops | bytes accessed | tf_op | source)
XLA Modules:
  0.0 140.0 jit_solution(3225182805329990949)
XLA Ops:
  1.7 6.5 %collective-permute-start.1 = (bf16[896,128]{1,0:T(8,128)(2,1)S(1)}, bf16[896,128]{1,0:T(8,128)(2,1)S(1)}, u32[]{:S(2)}, u32[]{:S(2)}) collective-permute-start(bf16[896,128]{1,0:T(8,128)(2,1)S(1)} %constant_dynamic-slice_fusion), channel_id=1, source_target_pairs={{0,14},{2,0},{4,2},{6,4},{8,6},{10,8},{12,10},{14,12},{1,15},{3,1}... | collective-permute-start | bytes 688136 | tf_op jit(solution)/shard_map/tiles/ppermute | solution.py:131
  8.2 2.5 %fusion.10 = f32[512,1024]{1,0:T(8,128)S(1)} fusion(bf16[896,512]{1,0:T(8,128)(2,1)} %param.8, bf16[1024,896]{1,0:T(8,128)(2,1)S(1)} %copy-done), kind=kOutput, calls=%fused_computation.27 | convolution fusion | flops 939524096 | bytes 4849664 | tf_op jit(solution)/shard_map/project/dot_general | solution.py:152
  12.5 3.2 %collective-permute-done = bf16[896,128]{1,0:T(8,128)(2,1)} collective-permute-done((bf16[896,128]{1,0:T(8,128)(2,1)S(1)}, bf16[896,128]{1,0:T(8,128)(2,1)}, u32[]{:S(2)}, u32[]{:S(2)}) %collective-permute-start) | collective-permute-done | bytes 229408 | tf_op jit(solution)/shard_map/tiles/ppermute | solution.py:131
  15.8 2.0 %collective-permute-start.2 = (bf16[4,64,1024]{2,1,0:T(8,128)(2,1)S(1)}, bf16[4,64,1024]{2,1,0:T(8,128)(2,1)}, u32[]{:S(2)}, u32[]{:S(2)}) collective-permute-start(bf16[4,64,1024]{2,1,0:T(8,128)(2,1)S(1)} %fusion), channel_id=1, source_target_pairs={{0,1},{1,0},{2,3},{3,2},{4,5},{5,4},{6,7},{7,6},{8,9},{9,8},{10,11... | collective-permute-start | bytes 1572872 | tf_op jit(solution)/shard_map/project/ppermute | solution.py:123
  20.6 2.7 %collective-permute-start.8 = (bf16[2,896,128]{2,1,0:T(8,128)(2,1)}, bf16[2,896,128]{2,1,0:T(8,128)(2,1)}, u32[]{:S(2)}, u32[]{:S(2)}) collective-permute-start(bf16[2,896,128]{2,1,0:T(8,128)(2,1)} %pad_maximum_fusion.1), channel_id=1, source_target_pairs={{0,48},{16,0},{32,16},{48,32},{1,49},{17,1},{33,17},{49,33},{2,50}... | collective-permute-start | bytes 1376264 | tf_op jit(solution)/shard_map/tiles_y/ppermute | solution.py:127
  24.8 2.5 %collective-permute-done.3 = bf16[896,128]{1,0:T(8,128)(2,1)S(1)} collective-permute-done((bf16[896,128]{1,0:T(8,128)(2,1)}, bf16[896,128]{1,0:T(8,128)(2,1)S(1)}, u32[]{:S(2)}, u32[]{:S(2)}) %collective-permute-start.3) | collective-permute-done | bytes 229408 | tf_op jit(solution)/shard_map/tiles/ppermute | solution.py:131
  27.5 3.2 %collective-permute-start.6 = (bf16[64,1024]{1,0:T(8,128)(2,1)S(1)}, bf16[64,1024]{1,0:T(8,128)(2,1)}, u32[]{:S(2)}, u32[]{:S(2)}) collective-permute-start(bf16[64,1024]{1,0:T(8,128)(2,1)S(1)} %get-tuple-element.57), channel_id=1, source_target_pairs={{0,6},{2,0},{4,2},{6,4},{1,7},{3,1},{5,3},{7,5},{8,14},{10,8},{12,... | collective-permute-start | bytes 393224 | tf_op jit(solution)/shard_map/project/ppermute | solution.py:127
  31.5 2.0 %collective-permute-done.4 = bf16[64,1024]{1,0:T(8,128)(2,1)} collective-permute-done((bf16[64,1024]{1,0:T(8,128)(2,1)S(1)}, bf16[64,1024]{1,0:T(8,128)(2,1)}, u32[]{:S(2)}, u32[]{:S(2)}) %collective-permute-start.4) | collective-permute-done | bytes 131104 | tf_op jit(solution)/shard_map/project/ppermute | solution.py:127
  33.5 3.0 %collective-permute-start.11 = (bf16[2,896,128]{2,1,0:T(8,128)(2,1)}, bf16[2,896,128]{2,1,0:T(8,128)(2,1)}, u32[]{:S(2)}, u32[]{:S(2)}) collective-permute-start(bf16[2,896,128]{2,1,0:T(8,128)(2,1)} %pad_maximum_fusion.2), channel_id=1, source_target_pairs={{0,48},{16,0},{32,16},{48,32},{1,49},{17,1},{33,17},{49,33},{2,50}... | collective-permute-start | bytes 1376264 | tf_op jit(solution)/shard_map/tiles_y/ppermute | solution.py:127
  41.2 2.1 %pad_maximum_fusion.refs_12_ = bf16[4,896,128]{2,1,0:T(8,128)(2,1)} fusion(bf16[1,896,128]{2,1,0:T(8,128)(2,1)S(1)} %bitcast.44, bf16[1,896,128]{2,1,0:T(8,128)(2,1)} %bitcast.46, bf16[1,896,128]{2,1,0:T(8,128)(2,1)} %bitcast.11, bf16[1,896,128]{2,1,0:T(8,128)(2,1)S(1)} %fusion.13), kind=kLoop, calls=%fused_computation.3 | loop fusion | flops 1376256 | bytes 1835008 | tf_op jit(solution)/shard_map/tiles_y/concatenate | solution.py:183
  43.3 2.1 %collective-permute-start.14 = (bf16[4,896,128]{2,1,0:T(8,128)(2,1)}, bf16[4,896,128]{2,1,0:T(8,128)(2,1)}, u32[]{:S(2)}, u32[]{:S(2)}) collective-permute-start(bf16[4,896,128]{2,1,0:T(8,128)(2,1)} %pad_maximum_fusion.refs_12_), channel_id=1, source_target_pairs={{0,1},{1,0},{2,3},{3,2},{4,5},{5,4},{6,7},{7,6},{8,9},{9,8},{10,11... | collective-permute-start | bytes 2752520 | tf_op jit(solution)/shard_map/other_core/ppermute | solution.py:123
  45.4 2.1 %collective-permute-start.21 = (bf16[2,896,128]{2,1,0:T(8,128)(2,1)}, bf16[2,896,128]{2,1,0:T(8,128)(2,1)}, u32[]{:S(2)}, u32[]{:S(2)}) collective-permute-start(bf16[2,896,128]{2,1,0:T(8,128)(2,1)} %collective-permute-done.8.refs_17_), channel_id=1, source_target_pairs={{0,1},{1,0},{2,3},{3,2},{4,5},{5,4},{6,7},{7,6},{8,9},{9,8},{10,11... | collective-permute-start | bytes 1376264 | tf_op jit(solution)/shard_map/other_core/ppermute | solution.py:123
  48.1 11.0 %grad.1 = bf16[32,64,384]{2,1,0:T(8,128)(2,1)} custom-call(bf16[64,1024]{1,0:T(8,128)(2,1)} %fusion.3.ranks_ref, bf16[1024,12288]{1,0:T(8,128)(2,1)} %grads_ref.1), custom_call_target="tpu_custom_call" | custom-call | flops 6442450944 | bytes 25165824 | tf_op jit(solution)/shard_map/grad/pallas_call | solution.py:28
  59.1 8.0 %all-to-all-start = ((bf16[16,2,64,384]{3,2,1,0:T(8,128)(2,1)}), bf16[16,2,64,384]{3,2,1,0:T(8,128)(2,1)S(1)}, u32[]{:S(2)}, u32[]{:S(2)}) async-start(bf16[16,2,64,384]{3,2,1,0:T(8,128)(2,1)} %bitcast.40), calls=%async_computation | async-start | bytes 3145728 | tf_op jit(solution)/shard_map/grad/all_to_all | solution.py:180
  67.2 2.1 %collective-permute-start.15 = (bf16[2,896,128]{2,1,0:T(8,128)(2,1)}, bf16[2,896,128]{2,1,0:T(8,128)(2,1)}, u32[]{:S(2)}, u32[]{:S(2)}) collective-permute-start(bf16[2,896,128]{2,1,0:T(8,128)(2,1)} %collective-permute-done.7.refs_13_), channel_id=1, source_target_pairs={{0,1},{1,0},{2,3},{3,2},{4,5},{5,4},{6,7},{7,6},{8,9},{9,8},{10,11... | collective-permute-start | bytes 1376264 | tf_op jit(solution)/shard_map/other_core/ppermute | solution.py:123
  71.5 2.8 %collective-permute-start.19 = (bf16[2,896,128]{2,1,0:T(8,128)(2,1)}, bf16[2,896,128]{2,1,0:T(8,128)(2,1)}, u32[]{:S(2)}, u32[]{:S(2)}) collective-permute-start(bf16[2,896,128]{2,1,0:T(8,128)(2,1)} %collective-permute-done.11.refs_18_), channel_id=1, source_target_pairs={{0,48},{16,0},{32,16},{48,32},{1,49},{17,1},{33,17},{49,33},{2,50}... | collective-permute-start | bytes 1376264 | tf_op jit(solution)/shard_map/tiles_y/ppermute | solution.py:127
  74.7 13.7 %collective-permute-done.12.refs_6_ = bf16[896,384]{1,0:T(8,128)(2,1)} collective-permute-done((bf16[896,384]{1,0:T(8,128)(2,1)}, bf16[896,384]{1,0:T(8,128)(2,1)}, u32[]{:S(2)}, u32[]{:S(2)}) %collective-permute-start.12) | collective-permute-done | bytes 688160 | tf_op jit(solution)/shard_map/weight_hops/ppermute | solution.py:127
  89.4 7.3 %collective-permute-done.19.refs_16_ = bf16[2,896,128]{2,1,0:T(8,128)(2,1)} collective-permute-done((bf16[2,896,128]{2,1,0:T(8,128)(2,1)}, bf16[2,896,128]{2,1,0:T(8,128)(2,1)}, u32[]{:S(2)}, u32[]{:S(2)}) %collective-permute-start.19) | collective-permute-done | bytes 458784 | tf_op jit(solution)/shard_map/tiles_y/ppermute | solution.py:127
  99.4 9.1 %collective-permute-done.13.refs_7_ = bf16[896,384]{1,0:T(8,128)(2,1)} collective-permute-done((bf16[896,384]{1,0:T(8,128)(2,1)}, bf16[896,384]{1,0:T(8,128)(2,1)}, u32[]{:S(2)}, u32[]{:S(2)}) %collective-permute-start.13) | collective-permute-done | bytes 688160 | tf_op jit(solution)/shard_map/weight_hops/ppermute | solution.py:127
  110.2 2.1 %collective-permute-start.26 = (bf16[64,384]{1,0:T(8,128)(2,1)S(1)}, bf16[64,384]{1,0:T(8,128)(2,1)S(1)}, u32[]{:S(2)}, u32[]{:S(2)}) collective-permute-start(bf16[64,384]{1,0:T(8,128)(2,1)S(1)} %fusion.8), channel_id=1, source_target_pairs={{0,8},{8,0},{1,9},{9,1},{2,10},{10,2},{3,11},{11,3},{4,12},{12,4},... | collective-permute-start | bytes 147464 | tf_op jit(solution)/shard_map/grad/ppermute | solution.py:123
  112.3 5.3 %collective-permute-done.26 = bf16[64,384]{1,0:T(8,128)(2,1)S(1)} collective-permute-done((bf16[64,384]{1,0:T(8,128)(2,1)S(1)}, bf16[64,384]{1,0:T(8,128)(2,1)S(1)}, u32[]{:S(2)}, u32[]{:S(2)}) %collective-permute-start.26) | collective-permute-done | bytes 49184 | tf_op jit(solution)/shard_map/grad/ppermute | solution.py:123
  123.1 2.9 %collective-permute-done.30.refs_3_ = bf16[128,384]{1,0:T(8,128)(2,1)S(1)} collective-permute-done((bf16[128,384]{1,0:T(8,128)(2,1)S(1)}, bf16[128,384]{1,0:T(8,128)(2,1)S(1)}, u32[]{:S(2)}, u32[]{:S(2)}) %collective-permute-start.30) | collective-permute-done | bytes 98336 | tf_op jit(solution)/shard_map/lift/ppermute | solution.py:127
  126.0 4.3 %collective-permute-done.29.refs_2_ = bf16[128,384]{1,0:T(8,128)(2,1)S(1)} collective-permute-done((bf16[128,384]{1,0:T(8,128)(2,1)S(1)}, bf16[128,384]{1,0:T(8,128)(2,1)S(1)}, u32[]{:S(2)}, u32[]{:S(2)}) %collective-permute-start.29) | collective-permute-done | bytes 98336 | tf_op jit(solution)/shard_map/lift/ppermute | solution.py:127
  131.0 8.9 %lift.1 = bf16[7168,384]{1,0:T(8,128)(2,1)} custom-call(s32[3]{0:T(128)} %pad_add_fusion.where_ref, bf16[128,384]{1,0:T(8,128)(2,1)} %copy-done.4, bf16[128,384]{1,0:T(8,128)(2,1)} %copy-done.7, bf16[128,384]{1,0:T(8,128)(2,1)} %copy-done.6, bf16[128,384]{1,0:T(8,128)(2,1)} %copy-done.5, bf16[896,384]{1,0:T(8,128)(2,1)} %refs_4_, ...), custom_call_target="tpu_custom_call" | custom-call | flops 2818572288 | bytes 18350080 | tf_op jit(solution)/shard_map/lift/pallas_call | solution.py:98
  (77 shorter events, 27.6 us)
Async XLA Ops:
  1.7 10.8 %collective-permute-start.1 = (bf16[896,128]{1,0:T(8,128)(2,1)S(1)}, bf16[896,128]{1,0:T(8,128)(2,1)S(1)}, u32[]{:S(2)}, u32[]{:S(2)}) collective-permute-start(bf16[896,128]{1,0:T(8,128)(2,1)S(1)} %constant_dynamic-slice_fusion), channel_id=1, source_target_pairs={{0,14},{2,0},{4,2},{6,4},{8,6},{10,8},{12,10},{14,12},{1,15},{3,1}... | collective-permute-start | bytes 688136 | tf_op jit(solution)/shard_map/tiles/ppermute | solution.py:131
  18.7 8.7 %collective-permute-start.3 = (bf16[896,128]{1,0:T(8,128)(2,1)}, bf16[896,128]{1,0:T(8,128)(2,1)S(1)}, u32[]{:S(2)}, u32[]{:S(2)}) collective-permute-start(bf16[896,128]{1,0:T(8,128)(2,1)} %collective-permute-done), channel_id=1, source_target_pairs={{0,2},{2,4},{4,6},{6,8},{8,10},{10,12},{12,14},{14,0},{1,3},{3,5},... | collective-permute-start | bytes 688136 | tf_op jit(solution)/shard_map/tiles/ppermute | solution.py:131
  20.6 19.1 %collective-permute-start.8 = (bf16[2,896,128]{2,1,0:T(8,128)(2,1)}, bf16[2,896,128]{2,1,0:T(8,128)(2,1)}, u32[]{:S(2)}, u32[]{:S(2)}) collective-permute-start(bf16[2,896,128]{2,1,0:T(8,128)(2,1)} %pad_maximum_fusion.1), channel_id=1, source_target_pairs={{0,48},{16,0},{32,16},{48,32},{1,49},{17,1},{33,17},{49,33},{2,50}... | collective-permute-start | bytes 1376264 | tf_op jit(solution)/shard_map/tiles_y/ppermute | solution.py:127
  23.3 16.3 %collective-permute-start.7 = (bf16[2,896,128]{2,1,0:T(8,128)(2,1)}, bf16[2,896,128]{2,1,0:T(8,128)(2,1)}, u32[]{:S(2)}, u32[]{:S(2)}) collective-permute-start(bf16[2,896,128]{2,1,0:T(8,128)(2,1)} %pad_maximum_fusion.1), channel_id=1, source_target_pairs={{0,16},{16,32},{32,48},{48,0},{1,17},{17,33},{33,49},{49,1},{2,18}... | collective-permute-start | bytes 1376264 | tf_op jit(solution)/shard_map/tiles_y/ppermute | solution.py:127
  27.5 9.0 %collective-permute-start.6 = (bf16[64,1024]{1,0:T(8,128)(2,1)S(1)}, bf16[64,1024]{1,0:T(8,128)(2,1)}, u32[]{:S(2)}, u32[]{:S(2)}) collective-permute-start(bf16[64,1024]{1,0:T(8,128)(2,1)S(1)} %get-tuple-element.57), channel_id=1, source_target_pairs={{0,6},{2,0},{4,2},{6,4},{1,7},{3,1},{5,3},{7,5},{8,14},{10,8},{12,... | collective-permute-start | bytes 393224 | tf_op jit(solution)/shard_map/project/ppermute | solution.py:127
  33.5 11.9 %collective-permute-start.11 = (bf16[2,896,128]{2,1,0:T(8,128)(2,1)}, bf16[2,896,128]{2,1,0:T(8,128)(2,1)}, u32[]{:S(2)}, u32[]{:S(2)}) collective-permute-start(bf16[2,896,128]{2,1,0:T(8,128)(2,1)} %pad_maximum_fusion.2), channel_id=1, source_target_pairs={{0,48},{16,0},{32,16},{48,32},{1,49},{17,1},{33,17},{49,33},{2,50}... | collective-permute-start | bytes 1376264 | tf_op jit(solution)/shard_map/tiles_y/ppermute | solution.py:127
  36.5 11.0 %collective-permute-start.10 = (bf16[2,896,128]{2,1,0:T(8,128)(2,1)}, bf16[2,896,128]{2,1,0:T(8,128)(2,1)}, u32[]{:S(2)}, u32[]{:S(2)}) collective-permute-start(bf16[2,896,128]{2,1,0:T(8,128)(2,1)} %pad_maximum_fusion.2), channel_id=1, source_target_pairs={{0,16},{16,32},{32,48},{48,0},{1,17},{17,33},{33,49},{49,1},{2,18}... | collective-permute-start | bytes 1376264 | tf_op jit(solution)/shard_map/tiles_y/ppermute | solution.py:127
  39.6 19.5 %collective-permute-start.9 = (bf16[896,384]{1,0:T(8,128)(2,1)}, bf16[896,384]{1,0:T(8,128)(2,1)}, u32[]{:S(2)}, u32[]{:S(2)}) collective-permute-start(bf16[896,384]{1,0:T(8,128)(2,1)} %refs_4_), channel_id=1, source_target_pairs={{0,2},{2,4},{4,6},{6,0},{1,3},{3,5},{5,7},{7,1},{8,10},{10,12},{12... | collective-permute-start | bytes 2064392 | tf_op jit(solution)/shard_map/weight_hops/ppermute | solution.py:127
  43.3 31.0 %collective-permute-start.14 = (bf16[4,896,128]{2,1,0:T(8,128)(2,1)}, bf16[4,896,128]{2,1,0:T(8,128)(2,1)}, u32[]{:S(2)}, u32[]{:S(2)}) collective-permute-start(bf16[4,896,128]{2,1,0:T(8,128)(2,1)} %pad_maximum_fusion.refs_12_), channel_id=1, source_target_pairs={{0,1},{1,0},{2,3},{3,2},{4,5},{5,4},{6,7},{7,6},{8,9},{9,8},{10,11... | collective-permute-start | bytes 2752520 | tf_op jit(solution)/shard_map/other_core/ppermute | solution.py:123
  45.4 26.1 %collective-permute-start.23 = (bf16[896,384]{1,0:T(8,128)(2,1)}, bf16[896,384]{1,0:T(8,128)(2,1)}, u32[]{:S(2)}, u32[]{:S(2)}) collective-permute-start(bf16[896,384]{1,0:T(8,128)(2,1)} %refs_4_), channel_id=1, source_target_pairs={{0,1},{1,0},{2,3},{3,2},{4,5},{5,4},{6,7},{7,6},{8,9},{9,8},{10,11... | collective-permute-start | bytes 2064392 | tf_op jit(solution)/shard_map/other_core/ppermute | solution.py:123
  45.4 23.9 %collective-permute-start.21 = (bf16[2,896,128]{2,1,0:T(8,128)(2,1)}, bf16[2,896,128]{2,1,0:T(8,128)(2,1)}, u32[]{:S(2)}, u32[]{:S(2)}) collective-permute-start(bf16[2,896,128]{2,1,0:T(8,128)(2,1)} %collective-permute-done.8.refs_17_), channel_id=1, source_target_pairs={{0,1},{1,0},{2,3},{3,2},{4,5},{5,4},{6,7},{7,6},{8,9},{9,8},{10,11... | collective-permute-start | bytes 1376264 | tf_op jit(solution)/shard_map/other_core/ppermute | solution.py:123
  47.5 21.8 %collective-permute-start.17 = (bf16[2,896,128]{2,1,0:T(8,128)(2,1)}, bf16[2,896,128]{2,1,0:T(8,128)(2,1)}, u32[]{:S(2)}, u32[]{:S(2)}) collective-permute-start(bf16[2,896,128]{2,1,0:T(8,128)(2,1)} %collective-permute-done.7.refs_13_), channel_id=1, source_target_pairs={{0,16},{16,32},{32,48},{48,0},{1,17},{17,33},{33,49},{49,1},{2,18}... | collective-permute-start | bytes 1376264 | tf_op jit(solution)/shard_map/tiles_y/ppermute | solution.py:127
  59.1 49.4 %all-to-all-start = ((bf16[16,2,64,384]{3,2,1,0:T(8,128)(2,1)}), bf16[16,2,64,384]{3,2,1,0:T(8,128)(2,1)S(1)}, u32[]{:S(2)}, u32[]{:S(2)}) async-start(bf16[16,2,64,384]{3,2,1,0:T(8,128)(2,1)} %bitcast.40), calls=%async_computation | async-start | bytes 3145728 | tf_op jit(solution)/shard_map/grad/all_to_all | solution.py:180
  69.3 19.1 %collective-permute-start.12 = (bf16[896,384]{1,0:T(8,128)(2,1)}, bf16[896,384]{1,0:T(8,128)(2,1)}, u32[]{:S(2)}, u32[]{:S(2)}) collective-permute-start(bf16[896,384]{1,0:T(8,128)(2,1)} %collective-permute-done.9.refs_5_), channel_id=1, source_target_pairs={{0,2},{2,4},{4,6},{6,0},{1,3},{3,5},{5,7},{7,1},{8,10},{10,12},{12... | collective-permute-start | bytes 2064392 | tf_op jit(solution)/shard_map/weight_hops/ppermute | solution.py:127
  69.3 20.0 %collective-permute-start.18 = (bf16[2,896,128]{2,1,0:T(8,128)(2,1)}, bf16[2,896,128]{2,1,0:T(8,128)(2,1)}, u32[]{:S(2)}, u32[]{:S(2)}) collective-permute-start(bf16[2,896,128]{2,1,0:T(8,128)(2,1)} %collective-permute-done.17.refs_15_), channel_id=1, source_target_pairs={{0,1},{1,0},{2,3},{3,2},{4,5},{5,4},{6,7},{7,6},{8,9},{9,8},{10,11... | collective-permute-start | bytes 1376264 | tf_op jit(solution)/shard_map/other_core/ppermute | solution.py:123
  71.1 18.2 %collective-permute-start.16 = (bf16[2,896,128]{2,1,0:T(8,128)(2,1)}, bf16[2,896,128]{2,1,0:T(8,128)(2,1)}, u32[]{:S(2)}, u32[]{:S(2)}) collective-permute-start(bf16[2,896,128]{2,1,0:T(8,128)(2,1)} %collective-permute-done.10.refs_14_), channel_id=1, source_target_pairs={{0,1},{1,0},{2,3},{3,2},{4,5},{5,4},{6,7},{7,6},{8,9},{9,8},{10,11... | collective-permute-start | bytes 1376264 | tf_op jit(solution)/shard_map/other_core/ppermute | solution.py:123
  71.5 25.2 %collective-permute-start.19 = (bf16[2,896,128]{2,1,0:T(8,128)(2,1)}, bf16[2,896,128]{2,1,0:T(8,128)(2,1)}, u32[]{:S(2)}, u32[]{:S(2)}) collective-permute-start(bf16[2,896,128]{2,1,0:T(8,128)(2,1)} %collective-permute-done.11.refs_18_), channel_id=1, source_target_pairs={{0,48},{16,0},{32,16},{48,32},{1,49},{17,1},{33,17},{49,33},{2,50}... | collective-permute-start | bytes 1376264 | tf_op jit(solution)/shard_map/tiles_y/ppermute | solution.py:127
  74.2 23.3 %collective-permute-start.24 = (bf16[896,384]{1,0:T(8,128)(2,1)}, bf16[896,384]{1,0:T(8,128)(2,1)}, u32[]{:S(2)}, u32[]{:S(2)}) collective-permute-start(bf16[896,384]{1,0:T(8,128)(2,1)} %collective-permute-done.9.refs_5_), channel_id=1, source_target_pairs={{0,1},{1,0},{2,3},{3,2},{4,5},{5,4},{6,7},{7,6},{8,9},{9,8},{10,11... | collective-permute-start | bytes 2064392 | tf_op jit(solution)/shard_map/other_core/ppermute | solution.py:123
  88.4 10.9 %collective-permute-start.25 = (bf16[896,384]{1,0:T(8,128)(2,1)}, bf16[896,384]{1,0:T(8,128)(2,1)}, u32[]{:S(2)}, u32[]{:S(2)}) collective-permute-start(bf16[896,384]{1,0:T(8,128)(2,1)} %collective-permute-done.12.refs_6_), channel_id=1, source_target_pairs={{0,1},{1,0},{2,3},{3,2},{4,5},{5,4},{6,7},{7,6},{8,9},{9,8},{10,11... | collective-permute-start | bytes 2064392 | tf_op jit(solution)/shard_map/other_core/ppermute | solution.py:123
  89.3 19.2 %collective-permute-start.13 = (bf16[896,384]{1,0:T(8,128)(2,1)}, bf16[896,384]{1,0:T(8,128)(2,1)}, u32[]{:S(2)}, u32[]{:S(2)}) collective-permute-start(bf16[896,384]{1,0:T(8,128)(2,1)} %collective-permute-done.12.refs_6_), channel_id=1, source_target_pairs={{0,2},{2,4},{4,6},{6,0},{1,3},{3,5},{5,7},{7,1},{8,10},{10,12},{12... | collective-permute-start | bytes 2064392 | tf_op jit(solution)/shard_map/weight_hops/ppermute | solution.py:127
  89.3 8.3 %collective-permute-start.22 = (bf16[2,896,128]{2,1,0:T(8,128)(2,1)}, bf16[2,896,128]{2,1,0:T(8,128)(2,1)}, u32[]{:S(2)}, u32[]{:S(2)}) collective-permute-start(bf16[2,896,128]{2,1,0:T(8,128)(2,1)} %collective-permute-done.11.refs_18_), channel_id=1, source_target_pairs={{0,1},{1,0},{2,3},{3,2},{4,5},{5,4},{6,7},{7,6},{8,9},{9,8},{10,11... | collective-permute-start | bytes 1376264 | tf_op jit(solution)/shard_map/other_core/ppermute | solution.py:123
  108.5 21.8 %collective-permute-start.31 = (bf16[896,384]{1,0:T(8,128)(2,1)}, bf16[896,384]{1,0:T(8,128)(2,1)}, u32[]{:S(2)}, u32[]{:S(2)}) collective-permute-start(bf16[896,384]{1,0:T(8,128)(2,1)} %collective-permute-done.13.refs_7_), channel_id=1, source_target_pairs={{0,1},{1,0},{2,3},{3,2},{4,5},{5,4},{6,7},{7,6},{8,9},{9,8},{10,11... | collective-permute-start | bytes 2064392 | tf_op jit(solution)/shard_map/other_core/ppermute | solution.py:123
  121.3 8.9 %collective-permute-start.29 = (bf16[128,384]{1,0:T(8,128)(2,1)S(1)}, bf16[128,384]{1,0:T(8,128)(2,1)S(1)}, u32[]{:S(2)}, u32[]{:S(2)}) collective-permute-start(bf16[128,384]{1,0:T(8,128)(2,1)S(1)} %maximum_select_fusion.refs_0_), channel_id=1, source_target_pairs={{0,4},{2,6},{4,0},{6,2},{1,5},{3,7},{5,1},{7,3},{8,12},{10,14},{12... | collective-permute-start | bytes 294920 | tf_op jit(solution)/shard_map/lift/ppermute | solution.py:127
  121.3 8.9 %collective-permute-start.28 = (bf16[128,384]{1,0:T(8,128)(2,1)S(1)}, bf16[128,384]{1,0:T(8,128)(2,1)S(1)}, u32[]{:S(2)}, u32[]{:S(2)}) collective-permute-start(bf16[128,384]{1,0:T(8,128)(2,1)S(1)} %maximum_select_fusion.refs_0_), channel_id=1, source_target_pairs={{0,2},{2,4},{4,6},{6,0},{1,3},{3,5},{5,7},{7,1},{8,10},{10,12},{12... | collective-permute-start | bytes 294920 | tf_op jit(solution)/shard_map/lift/ppermute | solution.py:127
  (18 other events, 139.1 us)

commit v4 on v3

--- a/solution.py
+++ b/solution.py
@@ -44,17 +44,18 @@
 
 
 def lift_kernel(where_ref, *refs):
-    pieces, weights, bases, rest = refs[:4], refs[4:12], refs[12:26], refs[26:]
+    pieces, weights, bases, rest = refs[:4], refs[4:12], refs[12:22], refs[22:]
     out_ref, dirs, old, base, done, in_sems, out_sems = rest
-    y, zl, core = (where_ref[i] for i in range(3))
+    color, zl, core = (where_ref[i] for i in range(3))
     pair = pieces[0].shape[0]
     rows = old.shape[2]
     lanes = base.shape[3] // 4
     loads = []
     for k in range(2):
-        plane, *columns = bases[7 * k : 7 * k + 7]
+        plane, right, far_low, far_high, left = bases[5 * k : 5 * k + 5]
         for z in range(4):
-            sources = [plane.at[z]] + [columns[2 * i + z // 2].at[z % 2] for i in range(3)]
+            far = (far_low, far_high)[z // 2].at[z % 2]
+            sources = [plane.at[z], right.at[z], far, left.at[z]]
             group = [pltpu.make_async_copy(weights[4 * k + z], old.at[k, z], in_sems.at[k, z, 4])]
             for q, source in enumerate(sources):
                 group.append(
@@ -68,7 +69,7 @@
                 copy.start()
             loads.append(group)
     for r, piece in enumerate(pieces):
-        at = lax.rem(y - zl + r + 4, 4) * pair
+        at = lax.rem(zl - r - color + 8, 4) * pair
         dirs[pl.ds(pl.multiple_of(at, pair), pair), :] = piece[...]
     stores = []
     for k in range(2):
@@ -99,7 +100,7 @@
         lift_kernel,
         in_specs=[pl.BlockSpec(memory_space=pltpu.SMEM)]
         + [pl.BlockSpec(memory_space=pltpu.VMEM)] * 4
-        + [anywhere] * 22,
+        + [anywhere] * 18,
         out_specs=anywhere,
         scratch_shapes=[
             pltpu.VMEM((4 * pair, width), BF),
@@ -135,8 +136,8 @@
     return lax.dynamic_index_in_dim(value, at, axis, keepdims=False)
 
 
-def after(value, *others):
-    return lax.optimization_barrier((value, *others))
+def after(*values):
+    return lax.optimization_barrier(values)
 
 
 def shards(acts, out_grads, basis, weight, first_moment, second_moment):
@@ -145,51 +146,50 @@
     tokens = acts.shape[0]
     x, y, zh, zl, core = (lax.axis_index(a) for a in ("x", "y", "zh", "zl", "core"))
 
+    color = (x + 2 * y) % 4
     with jax.named_scope("tiles"):
-        tile = lax.dynamic_slice_in_dim(basis, y * (rank // 4), rank // 4, 1)
+        tile = lax.dynamic_slice_in_dim(basis, color * (rank // 4), rank // 4, 1)
+        (tile,) = after(tile)
         below, above = along_z(tile, 1), along_z(tile, 7)
     with jax.named_scope("project"):
         partial_t = lax.dot_general(
             basis, acts, (((0,), (1,)), ((), ())), preferred_element_type=F32
         ).reshape(4, 2, rank_local, tokens)
     partial_t, below, above = after(partial_t, below, above)
-    with jax.named_scope("tiles"):
-        second = along_z(below, 1)
-        low = jnp.stack([tile, below])
     with jax.named_scope("project"):
         got = swap(pick(partial_t, 1 - core, 1).astype(BF), "core")
         mixed = pick(partial_t, core, 1) + got.astype(F32)
-    mixed, second = after(mixed, second)
-    with jax.named_scope("tiles_y"):
-        down_low, up_low = around(low, 1, "y"), around(low, 3, "y")
-        high = jnp.stack([second, above])
-    with jax.named_scope("project"):
-        total = pick(mixed, zl)
-        for r in range(1, 4):
-            total = total + around(pick(mixed, (zl + r) % 4).astype(BF), r).astype(F32)
-        ranks_t = total.astype(BF)
-    ranks_t, down_low, up_low, weight = after(ranks_t, down_low, up_low, weight)
+        got = [around(pick(mixed, (zl + r) % 4).astype(BF), r) for r in range(1, 4)]
+    got[0], below, weight = after(got[0], below, weight)
     with jax.named_scope("weight_hops"):
         hops = [weight, around(weight, 1)]
-    with jax.named_scope("tiles_y"):
-        down_high, up_high = around(high, 1, "y"), around(high, 3, "y")
+    with jax.named_scope("tiles"):
+        second = along_z(below, 1)
+    with jax.named_scope("project"):
+        total = pick(mixed, zl) + sum(part.astype(F32) for part in got)
+        ranks_t = total.astype(BF)
+    ranks_t, tile, below, second, above = after(ranks_t, tile, below, second, above)
+    with jax.named_scope("tiles_xy"):
+        plane = jnp.stack([tile, below, second, above])
+        right, left = around(plane, 3, "x"), around(plane, 1, "x")
+        far_low, far_high = around(plane[:2], 1, "y"), around(plane[2:], 3, "y")
     with jax.named_scope("grad"):
         blocks = grad_blocks(ranks_t, out_grads, width)
-    blocks, hops[1], down_high, up_high = after(blocks, hops[1], down_high, up_high)
+    blocks, weight, hops[1], *bases = after(
+        blocks, weight, hops[1], plane, right, far_low, far_high, left
+    )
+    hops[0] = weight
     with jax.named_scope("grad"):
         parts = lax.all_to_all(blocks.reshape(16, 2, rank_local, width), ("x", "y"), 0, 0)
-    with jax.named_scope("tiles_y"):
-        far_low, far_high = around(down_low, 1, "y"), around(up_high, 3, "y")
-        plane = jnp.concatenate([low, high])
-        bases = [plane, down_low, down_high, far_low, far_high, up_low, up_high]
     with jax.named_scope("weight_hops"):
         hops.append(around(hops[1], 1))
         hops.append(around(hops[2], 1))
+    hops[3], bases[2] = after(hops[3], bases[2])
     with jax.named_scope("other_core"):
         other_bases = [swap(b, "core") for b in bases]
         others = [swap(h, "core") for h in hops[:3]]
     parts, hops[3], *swapped = after(parts, hops[3], *other_bases, *others)
-    other_bases, others = swapped[:7], swapped[7:]
+    other_bases, others = swapped[:5], swapped[5:]
     with jax.named_scope("grad"):
         halves = jnp.sum(parts.astype(F32), axis=0)
         grad = pick(halves, zh) + swap(pick(halves, 1 - zh).astype(BF), "zh").astype(F32)
@@ -211,7 +211,7 @@
             jnp.concatenate([theirs, direction]),
         )
         pieces = [pair] + [around(pair, r) for r in range(1, 4)]
-        where = jnp.stack([y, zl, core]).astype(jnp.int32)
+        where = jnp.stack([color, zl, core]).astype(jnp.int32)
         new_weight = lift(where, pieces, hops + others, bases + other_bases)
     return (new_weight, new_first, new_second)
 

time: 141 us -> 131 us (0.929)
  waiting for transfers between devices: 57.7 us -> 42.4 us
  starting transfers between devices: 44.9 us -> 53.3 us
  other arithmetic: 10.5 us -> 7.67 us
    ppermute x15 -> x13, waiting for transfers between devices: 40.7 us -> 27.2 us  [around(): return lax.ppermute(value, axis, [(i, (i + shift) % 4) for i in range(4)])]
    ppermute x15 -> x13, starting transfers between devices: 15.4 us -> 21.3 us  [around(): return lax.ppermute(value, axis, [(i, (i + shift) % 4) for i in range(4)])]
    ppermute x14 -> x12, starting transfers between devices: 14.9 us -> 18.7 us  [swap(): return lax.ppermute(value, axis, [(0, 1), (1, 0)])]
    concatenate x1 -> x0, other arithmetic: 2.11 us -> none  [shards(): plane = jnp.concatenate([low, high])]
    ppermute x14 -> x12, waiting for transfers between devices: 9.55 us -> 8.5 us  [swap(): return lax.ppermute(value, axis, [(0, 1), (1, 0)])]
    another operation x3 -> x4, other arithmetic: 3.21 us -> 2.51 us  [the longest x3 1.93 us: shards(): plane = jnp.stack([tile, below, second, above])]
  transfers between devices with their start and end apart: 33 -> 29, of which waited for: 14 -> 14; matrix products, arithmetic and copies ran while one was open for 10% -> 6% of each run, Pallas kernels for 8% -> 8%
where the time goes in v4:
time: 131 us
  starting transfers between devices  53.3 us (41%)
  waiting for transfers between devices  42.4 us (32%)
  Pallas kernels  19.9 us (15%)
  other arithmetic  7.67 us (6%)
  local copies, waits for them, and re-layouts  3.79 us (3%)
  matrix products  2.48 us (2%)
    ppermute x13, waiting for transfers between devices, around(): return lax.ppermute(value, axis, [(i, (i + shift) % 4) for i in range(4)])  27.2 us
    ppermute x13, starting transfers between devices, around(): return lax.ppermute(value, axis, [(i, (i + shift) % 4) for i in range(4)])  21.3 us
    ppermute x12, starting transfers between devices, swap(): return lax.ppermute(value, axis, [(0, 1), (1, 0)])  18.7 us
    pallas_call x1, Pallas kernels, grad_blocks(): pl.pallas_call(grad_kernel, grid=(blocks // step,), in_specs=[pl.BlockSpe...  11.1 us
    pallas_call x1, Pallas kernels, lift(): pl.pallas_call(lift_kernel, in_specs=[pl.BlockSpec(memory_space=pltpu.SME...  8.86 us
    ppermute x12, waiting for transfers between devices, swap(): return lax.ppermute(value, axis, [(0, 1), (1, 0)])  8.5 us
    all_to_all x1, starting transfers between devices, shards(): lax.all_to_all(blocks.reshape(16, 2, rank_local, width), ('x', 'y'), 0, 0)  6.81 us
    ppermute x3, waiting for transfers between devices, along_z(): lax.ppermute(value, ('zh', 'zl'), [(i, (i + shift) % 8) for i in range(8)])  6.71 us
  transfers between devices with their start and end apart: 29, of which 14 were waited for; matrix products, arithmetic and copies ran while one was open for 6% of the time, Pallas kernels for 8%

profile of v4, /device:TPU:1, one launch (start us, length us, event | category | flops | bytes accessed | tf_op | source)
XLA Modules:
  0.0 130.6 jit_solution(9856641642358293765)
XLA Ops:
  1.8 6.5 %collective-permute-start.1 = (bf16[896,128]{1,0:T(8,128)(2,1)S(1)}, bf16[896,128]{1,0:T(8,128)(2,1)S(1)}, u32[]{:S(2)}, u32[]{:S(2)}) collective-permute-start(bf16[896,128]{1,0:T(8,128)(2,1)S(1)} %constant_dynamic-slice_fusion), channel_id=1, source_target_pairs={{0,14},{2,0},{4,2},{6,4},{8,6},{10,8},{12,10},{14,12},{1,15},{3,1}... | collective-permute-start | bytes 688136 | tf_op jit(solution)/shard_map/tiles/ppermute | solution.py:132
  8.2 2.5 %fusion.8 = f32[512,1024]{1,0:T(8,128)S(1)} fusion(bf16[896,512]{1,0:T(8,128)(2,1)} %param.8, bf16[1024,896]{1,0:T(8,128)(2,1)S(1)} %copy-done), kind=kOutput, calls=%fused_computation.25 | convolution fusion | flops 939524096 | bytes 4849664 | tf_op jit(solution)/shard_map/project/dot_general | solution.py:155
  12.5 3.1 %collective-permute-done = bf16[896,128]{1,0:T(8,128)(2,1)S(1)} collective-permute-done((bf16[896,128]{1,0:T(8,128)(2,1)S(1)}, bf16[896,128]{1,0:T(8,128)(2,1)S(1)}, u32[]{:S(2)}, u32[]{:S(2)}) %collective-permute-start) | collective-permute-done | bytes 229408 | tf_op jit(solution)/shard_map/tiles/ppermute | solution.py:132
  15.7 2.0 %collective-permute-start.2 = (bf16[4,64,1024]{2,1,0:T(8,128)(2,1)S(1)}, bf16[4,64,1024]{2,1,0:T(8,128)(2,1)}, u32[]{:S(2)}, u32[]{:S(2)}) collective-permute-start(bf16[4,64,1024]{2,1,0:T(8,128)(2,1)S(1)} %fusion), channel_id=1, source_target_pairs={{0,1},{1,0},{2,3},{3,2},{4,5},{5,4},{6,7},{7,6},{8,9},{9,8},{10,11... | collective-permute-start | bytes 1572872 | tf_op jit(solution)/shard_map/project/ppermute | solution.py:124
  21.6 3.3 %collective-permute-start.5 = (bf16[64,1024]{1,0:T(8,128)(2,1)}, bf16[64,1024]{1,0:T(8,128)(2,1)}, u32[]{:S(2)}, u32[]{:S(2)}) collective-permute-start(bf16[64,1024]{1,0:T(8,128)(2,1)} %get-tuple-element.69), channel_id=1, source_target_pairs={{0,6},{2,0},{4,2},{6,4},{1,7},{3,1},{5,3},{7,5},{8,14},{10,8},{12,... | collective-permute-start | bytes 393224 | tf_op jit(solution)/shard_map/project/ppermute | solution.py:128
  24.9 3.6 %collective-permute-done.3 = bf16[64,1024]{1,0:T(8,128)(2,1)} collective-permute-done((bf16[64,1024]{1,0:T(8,128)(2,1)}, bf16[64,1024]{1,0:T(8,128)(2,1)}, u32[]{:S(2)}, u32[]{:S(2)}) %collective-permute-start.3) | collective-permute-done | bytes 131104 | tf_op jit(solution)/shard_map/project/ppermute | solution.py:128
  28.4 3.1 %collective-permute-done.5 = bf16[64,1024]{1,0:T(8,128)(2,1)} collective-permute-done((bf16[64,1024]{1,0:T(8,128)(2,1)}, bf16[64,1024]{1,0:T(8,128)(2,1)}, u32[]{:S(2)}, u32[]{:S(2)}) %collective-permute-start.5) | collective-permute-done | bytes 131104 | tf_op jit(solution)/shard_map/project/ppermute | solution.py:128
  33.2 1.8 %collective-permute-done.6 = bf16[896,128]{1,0:T(8,128)(2,1)S(1)} collective-permute-done((bf16[896,128]{1,0:T(8,128)(2,1)S(1)}, bf16[896,128]{1,0:T(8,128)(2,1)S(1)}, u32[]{:S(2)}, u32[]{:S(2)}) %collective-permute-start.6) | collective-permute-done | bytes 229408 | tf_op jit(solution)/shard_map/tiles/ppermute | solution.py:132
  38.9 2.8 %collective-permute-start.7 = (bf16[896,384]{1,0:T(8,128)(2,1)}, bf16[896,384]{1,0:T(8,128)(2,1)}, u32[]{:S(2)}, u32[]{:S(2)}) collective-permute-start(bf16[896,384]{1,0:T(8,128)(2,1)} %refs_4_), channel_id=1, source_target_pairs={{0,2},{2,4},{4,6},{6,0},{1,3},{3,5},{5,7},{7,1},{8,10},{10,12},{12... | collective-permute-start | bytes 2064392 | tf_op jit(solution)/shard_map/weight_hops/ppermute | solution.py:128
  41.7 2.8 %collective-permute-start.10 = (bf16[2,896,128]{2,1,0:T(8,128)(2,1)S(1)}, bf16[2,896,128]{2,1,0:T(8,128)(2,1)}, u32[]{:S(2)}, u32[]{:S(2)}) collective-permute-start(bf16[2,896,128]{2,1,0:T(8,128)(2,1)S(1)} %pad_maximum_fusion.2), channel_id=1, source_target_pairs={{0,48},{16,0},{32,16},{48,32},{1,49},{17,1},{33,17},{49,33},{2,50}... | collective-permute-start | bytes 1376264 | tf_op jit(solution)/shard_map/tiles_xy/ppermute | solution.py:128
  45.4 11.1 %grad.1 = bf16[32,64,384]{2,1,0:T(8,128)(2,1)} custom-call(bf16[64,1024]{1,0:T(8,128)(2,1)} %fusion.1.ranks_ref, bf16[1024,12288]{1,0:T(8,128)(2,1)} %grads_ref.1), custom_call_target="tpu_custom_call" | custom-call | flops 6442450944 | bytes 25165824 | tf_op jit(solution)/shard_map/grad/pallas_call | solution.py:28
  57.2 3.4 %collective-permute-start.12 = (bf16[896,384]{1,0:T(8,128)(2,1)}, bf16[896,384]{1,0:T(8,128)(2,1)}, u32[]{:S(2)}, u32[]{:S(2)}) collective-permute-start(bf16[896,384]{1,0:T(8,128)(2,1)} %collective-permute-done.7.refs_5_), channel_id=1, source_target_pairs={{0,2},{2,4},{4,6},{6,0},{1,3},{3,5},{5,7},{7,1},{8,10},{10,12},{12... | collective-permute-start | bytes 2064392 | tf_op jit(solution)/shard_map/weight_hops/ppermute | solution.py:128
  60.7 2.7 %collective-permute-start.19 = (bf16[896,384]{1,0:T(8,128)(2,1)}, bf16[896,384]{1,0:T(8,128)(2,1)}, u32[]{:S(2)}, u32[]{:S(2)}) collective-permute-start(bf16[896,384]{1,0:T(8,128)(2,1)} %refs_4_), channel_id=1, source_target_pairs={{0,1},{1,0},{2,3},{3,2},{4,5},{5,4},{6,7},{7,6},{8,9},{9,8},{10,11... | collective-permute-start | bytes 2064392 | tf_op jit(solution)/shard_map/other_core/ppermute | solution.py:124
  63.4 6.8 %all-to-all-start = ((bf16[16,2,64,384]{3,2,1,0:T(8,128)(2,1)}), bf16[16,2,64,384]{3,2,1,0:T(8,128)(2,1)S(1)}, u32[]{:S(2)}, u32[]{:S(2)}) async-start(bf16[16,2,64,384]{3,2,1,0:T(8,128)(2,1)} %bitcast.35), calls=%async_computation | async-start | bytes 3145728 | tf_op jit(solution)/shard_map/grad/all_to_all | solution.py:183
  70.6 2.7 %collective-permute-done.12.refs_6_ = bf16[896,384]{1,0:T(8,128)(2,1)} collective-permute-done((bf16[896,384]{1,0:T(8,128)(2,1)}, bf16[896,384]{1,0:T(8,128)(2,1)}, u32[]{:S(2)}, u32[]{:S(2)}) %collective-permute-start.12) | collective-permute-done | bytes 688160 | tf_op jit(solution)/shard_map/weight_hops/ppermute | solution.py:128
  73.3 2.2 %collective-permute-start.13 = (bf16[896,384]{1,0:T(8,128)(2,1)}, bf16[896,384]{1,0:T(8,128)(2,1)}, u32[]{:S(2)}, u32[]{:S(2)}) collective-permute-start(bf16[896,384]{1,0:T(8,128)(2,1)} %collective-permute-done.12.refs_6_), channel_id=1, source_target_pairs={{0,2},{2,4},{4,6},{6,0},{1,3},{3,5},{5,7},{7,1},{8,10},{10,12},{12... | collective-permute-start | bytes 2064392 | tf_op jit(solution)/shard_map/weight_hops/ppermute | solution.py:128
  75.5 3.6 %collective-permute-start.20 = (bf16[896,384]{1,0:T(8,128)(2,1)}, bf16[896,384]{1,0:T(8,128)(2,1)}, u32[]{:S(2)}, u32[]{:S(2)}) collective-permute-start(bf16[896,384]{1,0:T(8,128)(2,1)} %collective-permute-done.7.refs_5_), channel_id=1, source_target_pairs={{0,1},{1,0},{2,3},{3,2},{4,5},{5,4},{6,7},{7,6},{8,9},{9,8},{10,11... | collective-permute-start | bytes 2064392 | tf_op jit(solution)/shard_map/other_core/ppermute | solution.py:124
  79.7 10.4 %collective-permute-done.13.refs_7_ = bf16[896,384]{1,0:T(8,128)(2,1)} collective-permute-done((bf16[896,384]{1,0:T(8,128)(2,1)}, bf16[896,384]{1,0:T(8,128)(2,1)}, u32[]{:S(2)}, u32[]{:S(2)}) %collective-permute-start.13) | collective-permute-done | bytes 688160 | tf_op jit(solution)/shard_map/weight_hops/ppermute | solution.py:128
  90.1 4.0 %collective-permute-start.21 = (bf16[896,384]{1,0:T(8,128)(2,1)}, bf16[896,384]{1,0:T(8,128)(2,1)}, u32[]{:S(2)}, u32[]{:S(2)}) collective-permute-start(bf16[896,384]{1,0:T(8,128)(2,1)} %collective-permute-done.12.refs_6_), channel_id=1, source_target_pairs={{0,1},{1,0},{2,3},{3,2},{4,5},{5,4},{6,7},{7,6},{8,9},{9,8},{10,11... | collective-permute-start | bytes 2064392 | tf_op jit(solution)/shard_map/other_core/ppermute | solution.py:124
  94.1 2.1 %collective-permute-done.21.refs_10_ = bf16[896,384]{1,0:T(8,128)(2,1)} collective-permute-done((bf16[896,384]{1,0:T(8,128)(2,1)}, bf16[896,384]{1,0:T(8,128)(2,1)}, u32[]{:S(2)}, u32[]{:S(2)}) %collective-permute-start.21) | collective-permute-done | bytes 688160 | tf_op jit(solution)/shard_map/other_core/ppermute | solution.py:124
  98.1 3.8 %collective-permute-start.22 = (bf16[64,384]{1,0:T(8,128)(2,1)S(1)}, bf16[64,384]{1,0:T(8,128)(2,1)S(1)}, u32[]{:S(2)}, u32[]{:S(2)}) collective-permute-start(bf16[64,384]{1,0:T(8,128)(2,1)S(1)} %fusion.6), channel_id=1, source_target_pairs={{0,8},{8,0},{1,9},{9,1},{2,10},{10,2},{3,11},{11,3},{4,12},{12,4},... | collective-permute-start | bytes 147464 | tf_op jit(solution)/shard_map/grad/ppermute | solution.py:124
  102.0 3.2 %collective-permute-done.22 = bf16[64,384]{1,0:T(8,128)(2,1)S(1)} collective-permute-done((bf16[64,384]{1,0:T(8,128)(2,1)S(1)}, bf16[64,384]{1,0:T(8,128)(2,1)S(1)}, u32[]{:S(2)}, u32[]{:S(2)}) %collective-permute-start.22) | collective-permute-done | bytes 49184 | tf_op jit(solution)/shard_map/grad/ppermute | solution.py:124
  113.7 7.2 %collective-permute-done.25.refs_2_ = bf16[128,384]{1,0:T(8,128)(2,1)S(1)} collective-permute-done((bf16[128,384]{1,0:T(8,128)(2,1)S(1)}, bf16[128,384]{1,0:T(8,128)(2,1)S(1)}, u32[]{:S(2)}, u32[]{:S(2)}) %collective-permute-start.25) | collective-permute-done | bytes 98336 | tf_op jit(solution)/shard_map/lift/ppermute | solution.py:128
  121.6 8.9 %lift.1 = bf16[7168,384]{1,0:T(8,128)(2,1)} custom-call(s32[3]{0:T(128)} %pad_add_fusion.where_ref, bf16[128,384]{1,0:T(8,128)(2,1)} %copy-done.7, bf16[128,384]{1,0:T(8,128)(2,1)} %copy-done.10, bf16[128,384]{1,0:T(8,128)(2,1)} %copy-done.9, bf16[128,384]{1,0:T(8,128)(2,1)} %copy-done.8, bf16[896,384]{1,0:T(8,128)(2,1)} %refs_4_, ...), custom_call_target="tpu_custom_call" | custom-call | flops 2818572288 | bytes 18350080 | tf_op jit(solution)/shard_map/lift/pallas_call | solution.py:99
  (74 shorter events, 26.1 us)
Async XLA Ops:
  1.8 10.8 %collective-permute-start.1 = (bf16[896,128]{1,0:T(8,128)(2,1)S(1)}, bf16[896,128]{1,0:T(8,128)(2,1)S(1)}, u32[]{:S(2)}, u32[]{:S(2)}) collective-permute-start(bf16[896,128]{1,0:T(8,128)(2,1)S(1)} %constant_dynamic-slice_fusion), channel_id=1, source_target_pairs={{0,14},{2,0},{4,2},{6,4},{8,6},{10,8},{12,10},{14,12},{1,15},{3,1}... | collective-permute-start | bytes 688136 | tf_op jit(solution)/shard_map/tiles/ppermute | solution.py:132
  8.2 7.4 %collective-permute-start = (bf16[896,128]{1,0:T(8,128)(2,1)S(1)}, bf16[896,128]{1,0:T(8,128)(2,1)S(1)}, u32[]{:S(2)}, u32[]{:S(2)}) collective-permute-start(bf16[896,128]{1,0:T(8,128)(2,1)S(1)} %constant_dynamic-slice_fusion), channel_id=1, source_target_pairs={{0,2},{2,4},{4,6},{6,8},{8,10},{10,12},{12,14},{14,0},{1,3},{3,5},... | collective-permute-start | bytes 688136 | tf_op jit(solution)/shard_map/tiles/ppermute | solution.py:132
  21.6 6.8 %collective-permute-start.3 = (bf16[64,1024]{1,0:T(8,128)(2,1)}, bf16[64,1024]{1,0:T(8,128)(2,1)}, u32[]{:S(2)}, u32[]{:S(2)}) collective-permute-start(bf16[64,1024]{1,0:T(8,128)(2,1)} %get-tuple-element.68), channel_id=1, source_target_pairs={{0,2},{2,4},{4,6},{6,0},{1,3},{3,5},{5,7},{7,1},{8,10},{10,12},{12... | collective-permute-start | bytes 393224 | tf_op jit(solution)/shard_map/project/ppermute | solution.py:128
  21.6 9.9 %collective-permute-start.5 = (bf16[64,1024]{1,0:T(8,128)(2,1)}, bf16[64,1024]{1,0:T(8,128)(2,1)}, u32[]{:S(2)}, u32[]{:S(2)}) collective-permute-start(bf16[64,1024]{1,0:T(8,128)(2,1)} %get-tuple-element.69), channel_id=1, source_target_pairs={{0,6},{2,0},{4,2},{6,4},{1,7},{3,1},{5,3},{7,5},{8,14},{10,8},{12,... | collective-permute-start | bytes 393224 | tf_op jit(solution)/shard_map/project/ppermute | solution.py:128
  24.9 6.6 %collective-permute-start.4 = (bf16[64,1024]{1,0:T(8,128)(2,1)S(1)}, bf16[64,1024]{1,0:T(8,128)(2,1)}, u32[]{:S(2)}, u32[]{:S(2)}) collective-permute-start(bf16[64,1024]{1,0:T(8,128)(2,1)S(1)} %get-tuple-element.70), channel_id=1, source_target_pairs={{0,4},{2,6},{4,0},{6,2},{1,5},{3,7},{5,1},{7,3},{8,12},{10,14},{12... | collective-permute-start | bytes 393224 | tf_op jit(solution)/shard_map/project/ppermute | solution.py:128
  28.4 6.7 %collective-permute-start.6 = (bf16[896,128]{1,0:T(8,128)(2,1)S(1)}, bf16[896,128]{1,0:T(8,128)(2,1)S(1)}, u32[]{:S(2)}, u32[]{:S(2)}) collective-permute-start(bf16[896,128]{1,0:T(8,128)(2,1)S(1)} %collective-permute-done), channel_id=1, source_target_pairs={{0,2},{2,4},{4,6},{6,8},{8,10},{10,12},{12,14},{14,0},{1,3},{3,5},... | collective-permute-start | bytes 688136 | tf_op jit(solution)/shard_map/tiles/ppermute | solution.py:132
  36.1 20.6 %collective-permute-start.11 = (bf16[4,896,128]{2,1,0:T(8,128)(2,1)S(1)}, bf16[4,896,128]{2,1,0:T(8,128)(2,1)}, u32[]{:S(2)}, u32[]{:S(2)}) collective-permute-start(bf16[4,896,128]{2,1,0:T(8,128)(2,1)S(1)} %pad_maximum_fusion.refs_12_), channel_id=1, source_target_pairs={{0,64},{64,128},{128,192},{192,0},{1,65},{65,129},{129,193},{193,1... | collective-permute-start | bytes 2752520 | tf_op jit(solution)/shard_map/tiles_xy/ppermute | solution.py:128
  37.4 19.3 %collective-permute-start.8 = (bf16[4,896,128]{2,1,0:T(8,128)(2,1)S(1)}, bf16[4,896,128]{2,1,0:T(8,128)(2,1)}, u32[]{:S(2)}, u32[]{:S(2)}) collective-permute-start(bf16[4,896,128]{2,1,0:T(8,128)(2,1)S(1)} %pad_maximum_fusion.refs_12_), channel_id=1, source_target_pairs={{0,192},{64,0},{128,64},{192,128},{1,193},{65,1},{129,65},{193,129... | collective-permute-start | bytes 2752520 | tf_op jit(solution)/shard_map/tiles_xy/ppermute | solution.py:128
  38.9 17.6 %collective-permute-start.7 = (bf16[896,384]{1,0:T(8,128)(2,1)}, bf16[896,384]{1,0:T(8,128)(2,1)}, u32[]{:S(2)}, u32[]{:S(2)}) collective-permute-start(bf16[896,384]{1,0:T(8,128)(2,1)} %refs_4_), channel_id=1, source_target_pairs={{0,2},{2,4},{4,6},{6,0},{1,3},{3,5},{5,7},{7,1},{8,10},{10,12},{12... | collective-permute-start | bytes 2064392 | tf_op jit(solution)/shard_map/weight_hops/ppermute | solution.py:128
  41.7 14.7 %collective-permute-start.10 = (bf16[2,896,128]{2,1,0:T(8,128)(2,1)S(1)}, bf16[2,896,128]{2,1,0:T(8,128)(2,1)}, u32[]{:S(2)}, u32[]{:S(2)}) collective-permute-start(bf16[2,896,128]{2,1,0:T(8,128)(2,1)S(1)} %pad_maximum_fusion.2), channel_id=1, source_target_pairs={{0,48},{16,0},{32,16},{48,32},{1,49},{17,1},{33,17},{49,33},{2,50}... | collective-permute-start | bytes 1376264 | tf_op jit(solution)/shard_map/tiles_xy/ppermute | solution.py:128
  45.4 11.1 %collective-permute-start.9 = (bf16[2,896,128]{2,1,0:T(8,128)(2,1)}, bf16[2,896,128]{2,1,0:T(8,128)(2,1)S(1)}, u32[]{:S(2)}, u32[]{:S(2)}) collective-permute-start(bf16[2,896,128]{2,1,0:T(8,128)(2,1)} %pad_maximum_fusion.1), channel_id=1, source_target_pairs={{0,16},{16,32},{32,48},{48,0},{1,17},{17,33},{33,49},{49,1},{2,18}... | collective-permute-start | bytes 1376264 | tf_op jit(solution)/shard_map/tiles_xy/ppermute | solution.py:128
  57.2 16.0 %collective-permute-start.12 = (bf16[896,384]{1,0:T(8,128)(2,1)}, bf16[896,384]{1,0:T(8,128)(2,1)}, u32[]{:S(2)}, u32[]{:S(2)}) collective-permute-start(bf16[896,384]{1,0:T(8,128)(2,1)} %collective-permute-done.7.refs_5_), channel_id=1, source_target_pairs={{0,2},{2,4},{4,6},{6,0},{1,3},{3,5},{5,7},{7,1},{8,10},{10,12},{12... | collective-permute-start | bytes 2064392 | tf_op jit(solution)/shard_map/weight_hops/ppermute | solution.py:128
  60.7 19.0 %collective-permute-start.19 = (bf16[896,384]{1,0:T(8,128)(2,1)}, bf16[896,384]{1,0:T(8,128)(2,1)}, u32[]{:S(2)}, u32[]{:S(2)}) collective-permute-start(bf16[896,384]{1,0:T(8,128)(2,1)} %refs_4_), channel_id=1, source_target_pairs={{0,1},{1,0},{2,3},{3,2},{4,5},{5,4},{6,7},{7,6},{8,9},{9,8},{10,11... | collective-permute-start | bytes 2064392 | tf_op jit(solution)/shard_map/other_core/ppermute | solution.py:124
  63.4 32.8 %all-to-all-start = ((bf16[16,2,64,384]{3,2,1,0:T(8,128)(2,1)}), bf16[16,2,64,384]{3,2,1,0:T(8,128)(2,1)S(1)}, u32[]{:S(2)}, u32[]{:S(2)}) async-start(bf16[16,2,64,384]{3,2,1,0:T(8,128)(2,1)} %bitcast.35), calls=%async_computation | async-start | bytes 3145728 | tf_op jit(solution)/shard_map/grad/all_to_all | solution.py:183
  70.2 8.9 %collective-permute-start.17 = (bf16[2,896,128]{2,1,0:T(8,128)(2,1)}, bf16[2,896,128]{2,1,0:T(8,128)(2,1)}, u32[]{:S(2)}, u32[]{:S(2)}) collective-permute-start(bf16[2,896,128]{2,1,0:T(8,128)(2,1)} %collective-permute-done.10.refs_15_), channel_id=1, source_target_pairs={{0,1},{1,0},{2,3},{3,2},{4,5},{5,4},{6,7},{7,6},{8,9},{9,8},{10,11... | collective-permute-start | bytes 1376264 | tf_op jit(solution)/shard_map/other_core/ppermute | solution.py:124
  73.3 16.8 %collective-permute-start.13 = (bf16[896,384]{1,0:T(8,128)(2,1)}, bf16[896,384]{1,0:T(8,128)(2,1)}, u32[]{:S(2)}, u32[]{:S(2)}) collective-permute-start(bf16[896,384]{1,0:T(8,128)(2,1)} %collective-permute-done.12.refs_6_), channel_id=1, source_target_pairs={{0,2},{2,4},{4,6},{6,0},{1,3},{3,5},{5,7},{7,1},{8,10},{10,12},{12... | collective-permute-start | bytes 2064392 | tf_op jit(solution)/shard_map/weight_hops/ppermute | solution.py:128
  75.5 18.6 %collective-permute-start.20 = (bf16[896,384]{1,0:T(8,128)(2,1)}, bf16[896,384]{1,0:T(8,128)(2,1)}, u32[]{:S(2)}, u32[]{:S(2)}) collective-permute-start(bf16[896,384]{1,0:T(8,128)(2,1)} %collective-permute-done.7.refs_5_), channel_id=1, source_target_pairs={{0,1},{1,0},{2,3},{3,2},{4,5},{5,4},{6,7},{7,6},{8,9},{9,8},{10,11... | collective-permute-start | bytes 2064392 | tf_op jit(solution)/shard_map/other_core/ppermute | solution.py:124
  79.1 15.0 %collective-permute-start.14 = (bf16[4,896,128]{2,1,0:T(8,128)(2,1)}, bf16[4,896,128]{2,1,0:T(8,128)(2,1)}, u32[]{:S(2)}, u32[]{:S(2)}) collective-permute-start(bf16[4,896,128]{2,1,0:T(8,128)(2,1)} %copy-done.1), channel_id=1, source_target_pairs={{0,1},{1,0},{2,3},{3,2},{4,5},{5,4},{6,7},{7,6},{8,9},{9,8},{10,11... | collective-permute-start | bytes 2752520 | tf_op jit(solution)/shard_map/other_core/ppermute | solution.py:124
  79.1 15.0 %collective-permute-start.15 = (bf16[4,896,128]{2,1,0:T(8,128)(2,1)}, bf16[4,896,128]{2,1,0:T(8,128)(2,1)}, u32[]{:S(2)}, u32[]{:S(2)}) collective-permute-start(bf16[4,896,128]{2,1,0:T(8,128)(2,1)} %collective-permute-done.8.refs_13_), channel_id=1, source_target_pairs={{0,1},{1,0},{2,3},{3,2},{4,5},{5,4},{6,7},{7,6},{8,9},{9,8},{10,11... | collective-permute-start | bytes 2752520 | tf_op jit(solution)/shard_map/other_core/ppermute | solution.py:124
  79.6 14.5 %collective-permute-start.18 = (bf16[4,896,128]{2,1,0:T(8,128)(2,1)}, bf16[4,896,128]{2,1,0:T(8,128)(2,1)}, u32[]{:S(2)}, u32[]{:S(2)}) collective-permute-start(bf16[4,896,128]{2,1,0:T(8,128)(2,1)} %collective-permute-done.11.refs_16_), channel_id=1, source_target_pairs={{0,1},{1,0},{2,3},{3,2},{4,5},{5,4},{6,7},{7,6},{8,9},{9,8},{10,11... | collective-permute-start | bytes 2752520 | tf_op jit(solution)/shard_map/other_core/ppermute | solution.py:124
  96.9 24.0 %collective-permute-start.27 = (bf16[896,384]{1,0:T(8,128)(2,1)}, bf16[896,384]{1,0:T(8,128)(2,1)}, u32[]{:S(2)}, u32[]{:S(2)}) collective-permute-start(bf16[896,384]{1,0:T(8,128)(2,1)} %collective-permute-done.13.refs_7_), channel_id=1, source_target_pairs={{0,1},{1,0},{2,3},{3,2},{4,5},{5,4},{6,7},{7,6},{8,9},{9,8},{10,11... | collective-permute-start | bytes 2064392 | tf_op jit(solution)/shard_map/other_core/ppermute | solution.py:124
  98.1 7.0 %collective-permute-start.22 = (bf16[64,384]{1,0:T(8,128)(2,1)S(1)}, bf16[64,384]{1,0:T(8,128)(2,1)S(1)}, u32[]{:S(2)}, u32[]{:S(2)}) collective-permute-start(bf16[64,384]{1,0:T(8,128)(2,1)S(1)} %fusion.6), channel_id=1, source_target_pairs={{0,8},{8,0},{1,9},{9,1},{2,10},{10,2},{3,11},{11,3},{4,12},{12,4},... | collective-permute-start | bytes 147464 | tf_op jit(solution)/shard_map/grad/ppermute | solution.py:124
  110.5 10.3 %collective-permute-start.25 = (bf16[128,384]{1,0:T(8,128)(2,1)S(1)}, bf16[128,384]{1,0:T(8,128)(2,1)S(1)}, u32[]{:S(2)}, u32[]{:S(2)}) collective-permute-start(bf16[128,384]{1,0:T(8,128)(2,1)S(1)} %maximum_select_fusion.refs_0_), channel_id=1, source_target_pairs={{0,4},{2,6},{4,0},{6,2},{1,5},{3,7},{5,1},{7,3},{8,12},{10,14},{12... | collective-permute-start | bytes 294920 | tf_op jit(solution)/shard_map/lift/ppermute | solution.py:128
  112.0 8.9 %collective-permute-start.24 = (bf16[128,384]{1,0:T(8,128)(2,1)S(1)}, bf16[128,384]{1,0:T(8,128)(2,1)S(1)}, u32[]{:S(2)}, u32[]{:S(2)}) collective-permute-start(bf16[128,384]{1,0:T(8,128)(2,1)S(1)} %maximum_select_fusion.refs_0_), channel_id=1, source_target_pairs={{0,2},{2,4},{4,6},{6,0},{1,3},{3,5},{5,7},{7,1},{8,10},{10,12},{12... | collective-permute-start | bytes 294920 | tf_op jit(solution)/shard_map/lift/ppermute | solution.py:128
  (17 other events, 137.7 us)

commit v5 on v4

--- a/solution.py
+++ b/solution.py
@@ -44,7 +44,7 @@
 
 
 def lift_kernel(where_ref, *refs):
-    pieces, weights, bases, rest = refs[:4], refs[4:12], refs[12:22], refs[22:]
+    pieces, weights, bases, rest = refs[:4], refs[4:12], refs[12:28], refs[28:]
     out_ref, dirs, old, base, done, in_sems, out_sems = rest
     color, zl, core = (where_ref[i] for i in range(3))
     pair = pieces[0].shape[0]
@@ -52,10 +52,9 @@
     lanes = base.shape[3] // 4
     loads = []
     for k in range(2):
-        plane, right, far_low, far_high, left = bases[5 * k : 5 * k + 5]
+        three, one = bases[8 * k : 8 * k + 4], bases[8 * k + 4 : 8 * k + 8]
         for z in range(4):
-            far = (far_low, far_high)[z // 2].at[z % 2]
-            sources = [plane.at[z], right.at[z], far, left.at[z]]
+            sources = [b.at[0] for b in one] if z == 2 else [b.at[min(z, 2)] for b in three]
             group = [pltpu.make_async_copy(weights[4 * k + z], old.at[k, z], in_sems.at[k, z, 4])]
             for q, source in enumerate(sources):
                 group.append(
@@ -100,7 +99,7 @@
         lift_kernel,
         in_specs=[pl.BlockSpec(memory_space=pltpu.SMEM)]
         + [pl.BlockSpec(memory_space=pltpu.VMEM)] * 4
-        + [anywhere] * 18,
+        + [anywhere] * 24,
         out_specs=anywhere,
         scratch_shapes=[
             pltpu.VMEM((4 * pair, width), BF),
@@ -136,8 +135,8 @@
     return lax.dynamic_index_in_dim(value, at, axis, keepdims=False)
 
 
-def after(*values):
-    return lax.optimization_barrier(values)
+def after(value, *others):
+    return lax.optimization_barrier((value, *others))
 
 
 def shards(acts, out_grads, basis, weight, first_moment, second_moment):
@@ -160,23 +159,24 @@
         got = swap(pick(partial_t, 1 - core, 1).astype(BF), "core")
         mixed = pick(partial_t, core, 1) + got.astype(F32)
         got = [around(pick(mixed, (zl + r) % 4).astype(BF), r) for r in range(1, 4)]
-    got[0], below, weight = after(got[0], below, weight)
+    got[0], tile, below, above, weight = after(got[0], tile, below, above, weight)
     with jax.named_scope("weight_hops"):
         hops = [weight, around(weight, 1)]
     with jax.named_scope("tiles"):
         second = along_z(below, 1)
+        own = jnp.stack([tile, below, above])
+    with jax.named_scope("tiles_xy"):
+        right, left = around(own, 3, "x"), around(own, 1, "x")
     with jax.named_scope("project"):
         total = pick(mixed, zl) + sum(part.astype(F32) for part in got)
         ranks_t = total.astype(BF)
-    ranks_t, tile, below, second, above = after(ranks_t, tile, below, second, above)
+    ranks_t, own, second = after(ranks_t, own, second)
     with jax.named_scope("tiles_xy"):
-        plane = jnp.stack([tile, below, second, above])
-        right, left = around(plane, 3, "x"), around(plane, 1, "x")
-        far_low, far_high = around(plane[:2], 1, "y"), around(plane[2:], 3, "y")
+        far = around(own, 1, "y")
     with jax.named_scope("grad"):
         blocks = grad_blocks(ranks_t, out_grads, width)
-    blocks, weight, hops[1], *bases = after(
-        blocks, weight, hops[1], plane, right, far_low, far_high, left
+    blocks, second, weight, hops[1], *three = after(
+        blocks, second, weight, hops[1], own, right, far, left
     )
     hops[0] = weight
     with jax.named_scope("grad"):
@@ -184,12 +184,16 @@
     with jax.named_scope("weight_hops"):
         hops.append(around(hops[1], 1))
         hops.append(around(hops[2], 1))
-    hops[3], bases[2] = after(hops[3], bases[2])
+    with jax.named_scope("tiles_xy"):
+        second = second[None]
+        one = [second, around(second, 3, "x"), around(second, 3, "y"), around(second, 1, "x")]
+    hops[3], one[0] = after(hops[3], one[0])
+    bases = three + one
     with jax.named_scope("other_core"):
         other_bases = [swap(b, "core") for b in bases]
         others = [swap(h, "core") for h in hops[:3]]
     parts, hops[3], *swapped = after(parts, hops[3], *other_bases, *others)
-    other_bases, others = swapped[:5], swapped[5:]
+    other_bases, others = swapped[:8], swapped[8:]
     with jax.named_scope("grad"):
         halves = jnp.sum(parts.astype(F32), axis=0)
         grad = pick(halves, zh) + swap(pick(halves, 1 - zh).astype(BF), "zh").astype(F32)

time: 131 us -> 130 us (level)
  waiting for transfers between devices: 42.4 us -> 38.9 us
  starting transfers between devices: 53.3 us -> 55 us
    ppermute x13 -> x15, waiting for transfers between devices: 27.2 us -> 21.5 us  [around(): return lax.ppermute(value, axis, [(i, (i + shift) % 4) for i in range(4)])]
    ppermute x12 -> x15, waiting for transfers between devices: 8.5 us -> 12.2 us  [swap(): return lax.ppermute(value, axis, [(0, 1), (1, 0)])]
    ppermute x13 -> x15, starting transfers between devices: 21.3 us -> 23.1 us  [around(): return lax.ppermute(value, axis, [(i, (i + shift) % 4) for i in range(4)])]
    ppermute x3, waiting for transfers between devices: 6.71 us -> 5.2 us  [along_z(): lax.ppermute(value, ('zh', 'zl'), [(i, (i + shift) % 8) for i in range(8)])]
    all_to_all x1, starting transfers between devices: 6.81 us -> 5.5 us  [shards(): lax.all_to_all(blocks.reshape(16, 2, rank_local, width), ('x', 'y'), 0, 0)]
    ppermute x12 -> x15, starting transfers between devices: 18.7 us -> 19.8 us  [swap(): return lax.ppermute(value, axis, [(0, 1), (1, 0)])]
  transfers between devices with their start and end apart: 29 -> 34, of which waited for: 14 -> 18; matrix products, arithmetic and copies ran while one was open for 6% -> 7% of each run, Pallas kernels for 8% -> 9%
where the time goes in v5:
time: 130 us; the launch traced here: 129 us
  starting transfers between devices  55 us (42%)
  waiting for transfers between devices  38.9 us (30%)
  Pallas kernels  20 us (15%)
  other arithmetic  7.72 us (6%)
  local copies, waits for them, and re-layouts  3.61 us (3%)
  matrix products  2.48 us (2%)
    ppermute x15, starting transfers between devices, around(): return lax.ppermute(value, axis, [(i, (i + shift) % 4) for i in range(4)])  23.1 us
    ppermute x15, waiting for transfers between devices, around(): return lax.ppermute(value, axis, [(i, (i + shift) % 4) for i in range(4)])  21.5 us
    ppermute x15, starting transfers between devices, swap(): return lax.ppermute(value, axis, [(0, 1), (1, 0)])  19.8 us
    ppermute x15, waiting for transfers between devices, swap(): return lax.ppermute(value, axis, [(0, 1), (1, 0)])  12.2 us
    pallas_call x1, Pallas kernels, grad_blocks(): pl.pallas_call(grad_kernel, grid=(blocks // step,), in_specs=[pl.BlockSpe...  11.1 us
    pallas_call x1, Pallas kernels, lift(): pl.pallas_call(lift_kernel, in_specs=[pl.BlockSpec(memory_space=pltpu.SME...  8.92 us
    ppermute x3, starting transfers between devices, along_z(): lax.ppermute(value, ('zh', 'zl'), [(i, (i + shift) % 8) for i in range(8)])  6.49 us
    all_to_all x1, starting transfers between devices, shards(): lax.all_to_all(blocks.reshape(16, 2, rank_local, width), ('x', 'y'), 0, 0)  5.5 us
  transfers between devices with their start and end apart: 34, of which 18 were waited for; matrix products, arithmetic and copies ran while one was open for 7% of the time, Pallas kernels for 9%

profile of v5, /device:TPU:1, one launch (start us, length us, event | category | flops | bytes accessed | tf_op | source)
XLA Modules:
  0.0 128.6 jit_solution(16602807566624014315)
XLA Ops:
  1.8 6.5 %collective-permute-start.1 = (bf16[896,128]{1,0:T(8,128)(2,1)S(1)}, bf16[896,128]{1,0:T(8,128)(2,1)S(1)}, u32[]{:S(2)}, u32[]{:S(2)}) collective-permute-start(bf16[896,128]{1,0:T(8,128)(2,1)S(1)} %constant_dynamic-slice_fusion), channel_id=1, source_target_pairs={{0,14},{2,0},{4,2},{6,4},{8,6},{10,8},{12,10},{14,12},{1,15},{3,1}... | collective-permute-start | bytes 688136 | tf_op jit(solution)/shard_map/tiles/ppermute | solution.py:131
  8.2 2.5 %fusion.8 = f32[512,1024]{1,0:T(8,128)S(1)} fusion(bf16[896,512]{1,0:T(8,128)(2,1)} %param.8, bf16[1024,896]{1,0:T(8,128)(2,1)S(1)} %copy-done), kind=kOutput, calls=%fused_computation.23 | convolution fusion | flops 939524096 | bytes 4849664 | tf_op jit(solution)/shard_map/project/dot_general | solution.py:154
  10.7 1.8 %collective-permute-done.1 = bf16[896,128]{1,0:T(8,128)(2,1)S(1)} collective-permute-done((bf16[896,128]{1,0:T(8,128)(2,1)S(1)}, bf16[896,128]{1,0:T(8,128)(2,1)S(1)}, u32[]{:S(2)}, u32[]{:S(2)}) %collective-permute-start.1) | collective-permute-done | bytes 229408 | tf_op jit(solution)/shard_map/tiles/ppermute | solution.py:131
  12.5 3.1 %collective-permute-done = bf16[896,128]{1,0:T(8,128)(2,1)S(1)} collective-permute-done((bf16[896,128]{1,0:T(8,128)(2,1)S(1)}, bf16[896,128]{1,0:T(8,128)(2,1)S(1)}, u32[]{:S(2)}, u32[]{:S(2)}) %collective-permute-start) | collective-permute-done | bytes 229408 | tf_op jit(solution)/shard_map/tiles/ppermute | solution.py:131
  15.7 2.0 %collective-permute-start.2 = (bf16[4,64,1024]{2,1,0:T(8,128)(2,1)S(1)}, bf16[4,64,1024]{2,1,0:T(8,128)(2,1)}, u32[]{:S(2)}, u32[]{:S(2)}) collective-permute-start(bf16[4,64,1024]{2,1,0:T(8,128)(2,1)S(1)} %fusion), channel_id=1, source_target_pairs={{0,1},{1,0},{2,3},{3,2},{4,5},{5,4},{6,7},{7,6},{8,9},{9,8},{10,11... | collective-permute-start | bytes 1572872 | tf_op jit(solution)/shard_map/project/ppermute | solution.py:123
  21.6 3.3 %collective-permute-start.5 = (bf16[64,1024]{1,0:T(8,128)(2,1)}, bf16[64,1024]{1,0:T(8,128)(2,1)}, u32[]{:S(2)}, u32[]{:S(2)}) collective-permute-start(bf16[64,1024]{1,0:T(8,128)(2,1)} %get-tuple-element.75), channel_id=1, source_target_pairs={{0,6},{2,0},{4,2},{6,4},{1,7},{3,1},{5,3},{7,5},{8,14},{10,8},{12,... | collective-permute-start | bytes 393224 | tf_op jit(solution)/shard_map/project/ppermute | solution.py:127
  24.9 3.6 %collective-permute-done.3 = bf16[64,1024]{1,0:T(8,128)(2,1)} collective-permute-done((bf16[64,1024]{1,0:T(8,128)(2,1)}, bf16[64,1024]{1,0:T(8,128)(2,1)}, u32[]{:S(2)}, u32[]{:S(2)}) %collective-permute-start.3) | collective-permute-done | bytes 131104 | tf_op jit(solution)/shard_map/project/ppermute | solution.py:127
  28.4 1.9 %pad_maximum_fusion.refs_12_ = bf16[3,896,128]{2,1,0:T(8,128)(2,1)} fusion(bf16[1,896,128]{2,1,0:T(8,128)(2,1)} %bitcast.40, bf16[1,896,128]{2,1,0:T(8,128)(2,1)S(1)} %bitcast.39, bf16[1,896,128]{2,1,0:T(8,128)(2,1)S(1)} %bitcast.38), kind=kLoop, calls=%fused_computation.3 | loop fusion | flops 688128 | bytes 1376256 | tf_op jit(solution)/shard_map/tiles/stack | solution.py:167
  33.0 1.7 %fusion.1.ranks_ref = bf16[64,1024]{1,0:T(8,128)(2,1)} fusion(bf16[64,1024]{1,0:T(8,128)(2,1)} %collective-permute-done.5, bf16[64,1024]{1,0:T(8,128)(2,1)} %collective-permute-done.4, bf16[64,1024]{1,0:T(8,128)(2,1)} %collective-permute-done.3, f32[4,64,1024]{2,1,0:T(8,128)S(1)} %bitcast_add_fusion, s32[]{:T(128)S(6)} %select_n.62), kind=kLoop, calls=%fused_computation.6 | loop fusion | flops 458752 | bytes 786436 | tf_op jit(solution)/shard_map/project/convert_element_type | solution.py:172
  36.4 11.1 %grad.1 = bf16[32,64,384]{2,1,0:T(8,128)(2,1)} custom-call(bf16[64,1024]{1,0:T(8,128)(2,1)} %fusion.1.ranks_ref, bf16[1024,12288]{1,0:T(8,128)(2,1)} %grads_ref.1), custom_call_target="tpu_custom_call" | custom-call | flops 6442450944 | bytes 25165824 | tf_op jit(solution)/shard_map/grad/pallas_call | solution.py:28
  47.4 2.5 %collective-permute-done.7.refs_5_ = bf16[896,384]{1,0:T(8,128)(2,1)} collective-permute-done((bf16[896,384]{1,0:T(8,128)(2,1)}, bf16[896,384]{1,0:T(8,128)(2,1)}, u32[]{:S(2)}, u32[]{:S(2)}) %collective-permute-start.7) | collective-permute-done | bytes 688160 | tf_op jit(solution)/shard_map/weight_hops/ppermute | solution.py:127
  50.9 2.9 %collective-permute-start.11 = (bf16[896,384]{1,0:T(8,128)(2,1)}, bf16[896,384]{1,0:T(8,128)(2,1)}, u32[]{:S(2)}, u32[]{:S(2)}) collective-permute-start(bf16[896,384]{1,0:T(8,128)(2,1)} %collective-permute-done.7.refs_5_), channel_id=1, source_target_pairs={{0,2},{2,4},{4,6},{6,0},{1,3},{3,5},{5,7},{7,1},{8,10},{10,12},{12... | collective-permute-start | bytes 2064392 | tf_op jit(solution)/shard_map/weight_hops/ppermute | solution.py:127
  55.0 5.5 %all-to-all-start = ((bf16[16,2,64,384]{3,2,1,0:T(8,128)(2,1)}), bf16[16,2,64,384]{3,2,1,0:T(8,128)(2,1)S(1)}, u32[]{:S(2)}, u32[]{:S(2)}) async-start(bf16[16,2,64,384]{3,2,1,0:T(8,128)(2,1)} %bitcast.35), calls=%async_computation | async-start | bytes 3145728 | tf_op jit(solution)/shard_map/grad/all_to_all | solution.py:183
  60.5 2.6 %collective-permute-start.20 = (bf16[1,896,128]{2,1,0:T(8,128)(2,1)}, bf16[1,896,128]{2,1,0:T(8,128)(2,1)S(1)}, u32[]{:S(2)}, u32[]{:S(2)}) collective-permute-start(bf16[1,896,128]{2,1,0:T(8,128)(2,1)} %bitcast.14.refs_16_), channel_id=1, source_target_pairs={{0,48},{16,0},{32,16},{48,32},{1,49},{17,1},{33,17},{49,33},{2,50}... | collective-permute-start | bytes 688136 | tf_op jit(solution)/shard_map/tiles_xy/ppermute | solution.py:127
  63.1 4.7 %collective-permute-start.13 = (bf16[3,896,128]{2,1,0:T(8,128)(2,1)}, bf16[3,896,128]{2,1,0:T(8,128)(2,1)}, u32[]{:S(2)}, u32[]{:S(2)}) collective-permute-start(bf16[3,896,128]{2,1,0:T(8,128)(2,1)} %pad_maximum_fusion.refs_12_), channel_id=1, source_target_pairs={{0,1},{1,0},{2,3},{3,2},{4,5},{5,4},{6,7},{7,6},{8,9},{9,8},{10,11... | collective-permute-start | bytes 2064392 | tf_op jit(solution)/shard_map/other_core/ppermute | solution.py:123
  67.8 2.4 %collective-permute-start.18 = (bf16[1,896,128]{2,1,0:T(8,128)(2,1)}, bf16[1,896,128]{2,1,0:T(8,128)(2,1)S(1)}, u32[]{:S(2)}, u32[]{:S(2)}) collective-permute-start(bf16[1,896,128]{2,1,0:T(8,128)(2,1)} %bitcast.14.refs_16_), channel_id=1, source_target_pairs={{0,192},{64,0},{128,64},{192,128},{1,193},{65,1},{129,65},{193,129... | collective-permute-start | bytes 688136 | tf_op jit(solution)/shard_map/tiles_xy/ppermute | solution.py:127
  70.2 2.3 %collective-permute-start.12 = (bf16[896,384]{1,0:T(8,128)(2,1)}, bf16[896,384]{1,0:T(8,128)(2,1)}, u32[]{:S(2)}, u32[]{:S(2)}) collective-permute-start(bf16[896,384]{1,0:T(8,128)(2,1)} %collective-permute-done.11.refs_6_), channel_id=1, source_target_pairs={{0,2},{2,4},{4,6},{6,0},{1,3},{3,5},{5,7},{7,1},{8,10},{10,12},{12... | collective-permute-start | bytes 2064392 | tf_op jit(solution)/shard_map/weight_hops/ppermute | solution.py:127
  72.5 7.2 %collective-permute-done.20.refs_18_ = bf16[1,896,128]{2,1,0:T(8,128)(2,1)S(1)} collective-permute-done((bf16[1,896,128]{2,1,0:T(8,128)(2,1)}, bf16[1,896,128]{2,1,0:T(8,128)(2,1)S(1)}, u32[]{:S(2)}, u32[]{:S(2)}) %collective-permute-start.20) | collective-permute-done | bytes 229408 | tf_op jit(solution)/shard_map/tiles_xy/ppermute | solution.py:127
  79.8 6.0 %collective-permute-start.23 = (bf16[1,896,128]{2,1,0:T(8,128)(2,1)}, bf16[1,896,128]{2,1,0:T(8,128)(2,1)S(1)}, u32[]{:S(2)}, u32[]{:S(2)}) collective-permute-start(bf16[1,896,128]{2,1,0:T(8,128)(2,1)} %collective-permute-done.22.refs_19_), channel_id=1, source_target_pairs={{0,1},{1,0},{2,3},{3,2},{4,5},{5,4},{6,7},{7,6},{8,9},{9,8},{10,11... | collective-permute-start | bytes 688136 | tf_op jit(solution)/shard_map/other_core/ppermute | solution.py:123
  95.7 2.6 %collective-permute-start.27 = (bf16[64,384]{1,0:T(8,128)(2,1)S(1)}, bf16[64,384]{1,0:T(8,128)(2,1)S(1)}, u32[]{:S(2)}, u32[]{:S(2)}) collective-permute-start(bf16[64,384]{1,0:T(8,128)(2,1)S(1)} %fusion.6), channel_id=1, source_target_pairs={{0,8},{8,0},{1,9},{9,1},{2,10},{10,2},{3,11},{11,3},{4,12},{12,4},... | collective-permute-start | bytes 147464 | tf_op jit(solution)/shard_map/grad/ppermute | solution.py:123
  98.3 4.4 %collective-permute-done.27 = bf16[64,384]{1,0:T(8,128)(2,1)S(1)} collective-permute-done((bf16[64,384]{1,0:T(8,128)(2,1)S(1)}, bf16[64,384]{1,0:T(8,128)(2,1)S(1)}, u32[]{:S(2)}, u32[]{:S(2)}) %collective-permute-start.27) | collective-permute-done | bytes 49184 | tf_op jit(solution)/shard_map/grad/ppermute | solution.py:123
  107.4 2.6 %collective-permute-start.30 = (bf16[128,384]{1,0:T(8,128)(2,1)S(1)}, bf16[128,384]{1,0:T(8,128)(2,1)S(1)}, u32[]{:S(2)}, u32[]{:S(2)}) collective-permute-start(bf16[128,384]{1,0:T(8,128)(2,1)S(1)} %maximum_select_fusion.refs_0_), channel_id=1, source_target_pairs={{0,4},{2,6},{4,0},{6,2},{1,5},{3,7},{5,1},{7,3},{8,12},{10,14},{12... | collective-permute-start | bytes 294920 | tf_op jit(solution)/shard_map/lift/ppermute | solution.py:127
  111.7 7.2 %collective-permute-done.30.refs_2_ = bf16[128,384]{1,0:T(8,128)(2,1)S(1)} collective-permute-done((bf16[128,384]{1,0:T(8,128)(2,1)S(1)}, bf16[128,384]{1,0:T(8,128)(2,1)S(1)}, u32[]{:S(2)}, u32[]{:S(2)}) %collective-permute-start.30) | collective-permute-done | bytes 98336 | tf_op jit(solution)/shard_map/lift/ppermute | solution.py:127
  119.5 8.9 %lift.1 = bf16[7168,384]{1,0:T(8,128)(2,1)} custom-call(s32[3]{0:T(128)} %pad_add_fusion.where_ref, bf16[128,384]{1,0:T(8,128)(2,1)} %copy-done.3, bf16[128,384]{1,0:T(8,128)(2,1)} %copy-done.12, bf16[128,384]{1,0:T(8,128)(2,1)} %copy-done.11, bf16[128,384]{1,0:T(8,128)(2,1)} %copy-done.10, bf16[896,384]{1,0:T(8,128)(2,1)} %refs_4_, ...), custom_call_target="tpu_custom_call" | custom-call | flops 2818572288 | bytes 18350080 | tf_op jit(solution)/shard_map/lift/pallas_call | solution.py:98
  (86 shorter events, 28.6 us)
Async XLA Ops:
  1.8 10.8 %collective-permute-start.1 = (bf16[896,128]{1,0:T(8,128)(2,1)S(1)}, bf16[896,128]{1,0:T(8,128)(2,1)S(1)}, u32[]{:S(2)}, u32[]{:S(2)}) collective-permute-start(bf16[896,128]{1,0:T(8,128)(2,1)S(1)} %constant_dynamic-slice_fusion), channel_id=1, source_target_pairs={{0,14},{2,0},{4,2},{6,4},{8,6},{10,8},{12,10},{14,12},{1,15},{3,1}... | collective-permute-start | bytes 688136 | tf_op jit(solution)/shard_map/tiles/ppermute | solution.py:131
  8.2 7.4 %collective-permute-start = (bf16[896,128]{1,0:T(8,128)(2,1)S(1)}, bf16[896,128]{1,0:T(8,128)(2,1)S(1)}, u32[]{:S(2)}, u32[]{:S(2)}) collective-permute-start(bf16[896,128]{1,0:T(8,128)(2,1)S(1)} %constant_dynamic-slice_fusion), channel_id=1, source_target_pairs={{0,2},{2,4},{4,6},{6,8},{8,10},{10,12},{12,14},{14,0},{1,3},{3,5},... | collective-permute-start | bytes 688136 | tf_op jit(solution)/shard_map/tiles/ppermute | solution.py:131
  21.6 6.8 %collective-permute-start.3 = (bf16[64,1024]{1,0:T(8,128)(2,1)}, bf16[64,1024]{1,0:T(8,128)(2,1)}, u32[]{:S(2)}, u32[]{:S(2)}) collective-permute-start(bf16[64,1024]{1,0:T(8,128)(2,1)} %get-tuple-element.74), channel_id=1, source_target_pairs={{0,2},{2,4},{4,6},{6,0},{1,3},{3,5},{5,7},{7,1},{8,10},{10,12},{12... | collective-permute-start | bytes 393224 | tf_op jit(solution)/shard_map/project/ppermute | solution.py:127
  21.6 11.4 %collective-permute-start.5 = (bf16[64,1024]{1,0:T(8,128)(2,1)}, bf16[64,1024]{1,0:T(8,128)(2,1)}, u32[]{:S(2)}, u32[]{:S(2)}) collective-permute-start(bf16[64,1024]{1,0:T(8,128)(2,1)} %get-tuple-element.75), channel_id=1, source_target_pairs={{0,6},{2,0},{4,2},{6,4},{1,7},{3,1},{5,3},{7,5},{8,14},{10,8},{12,... | collective-permute-start | bytes 393224 | tf_op jit(solution)/shard_map/project/ppermute | solution.py:127
  24.9 8.1 %collective-permute-start.4 = (bf16[64,1024]{1,0:T(8,128)(2,1)S(1)}, bf16[64,1024]{1,0:T(8,128)(2,1)}, u32[]{:S(2)}, u32[]{:S(2)}) collective-permute-start(bf16[64,1024]{1,0:T(8,128)(2,1)S(1)} %get-tuple-element.76), channel_id=1, source_target_pairs={{0,4},{2,6},{4,0},{6,2},{1,5},{3,7},{5,1},{7,3},{8,12},{10,14},{12... | collective-permute-start | bytes 393224 | tf_op jit(solution)/shard_map/project/ppermute | solution.py:127
  28.4 6.7 %collective-permute-start.6 = (bf16[896,128]{1,0:T(8,128)(2,1)S(1)}, bf16[896,128]{1,0:T(8,128)(2,1)}, u32[]{:S(2)}, u32[]{:S(2)}) collective-permute-start(bf16[896,128]{1,0:T(8,128)(2,1)S(1)} %collective-permute-done), channel_id=1, source_target_pairs={{0,2},{2,4},{4,6},{6,8},{8,10},{10,12},{12,14},{14,0},{1,3},{3,5},... | collective-permute-start | bytes 688136 | tf_op jit(solution)/shard_map/tiles/ppermute | solution.py:131
  30.3 17.1 %collective-permute-start.10 = (bf16[3,896,128]{2,1,0:T(8,128)(2,1)}, bf16[3,896,128]{2,1,0:T(8,128)(2,1)}, u32[]{:S(2)}, u32[]{:S(2)}) collective-permute-start(bf16[3,896,128]{2,1,0:T(8,128)(2,1)} %pad_maximum_fusion.refs_12_), channel_id=1, source_target_pairs={{0,64},{64,128},{128,192},{192,0},{1,65},{65,129},{129,193},{193,1... | collective-permute-start | bytes 2064392 | tf_op jit(solution)/shard_map/tiles_xy/ppermute | solution.py:127
  31.5 15.9 %collective-permute-start.8 = (bf16[3,896,128]{2,1,0:T(8,128)(2,1)}, bf16[3,896,128]{2,1,0:T(8,128)(2,1)}, u32[]{:S(2)}, u32[]{:S(2)}) collective-permute-start(bf16[3,896,128]{2,1,0:T(8,128)(2,1)} %pad_maximum_fusion.refs_12_), channel_id=1, source_target_pairs={{0,192},{64,0},{128,64},{192,128},{1,193},{65,1},{129,65},{193,129... | collective-permute-start | bytes 2064392 | tf_op jit(solution)/shard_map/tiles_xy/ppermute | solution.py:127
  33.0 16.9 %collective-permute-start.7 = (bf16[896,384]{1,0:T(8,128)(2,1)}, bf16[896,384]{1,0:T(8,128)(2,1)}, u32[]{:S(2)}, u32[]{:S(2)}) collective-permute-start(bf16[896,384]{1,0:T(8,128)(2,1)} %refs_4_), channel_id=1, source_target_pairs={{0,2},{2,4},{4,6},{6,0},{1,3},{3,5},{5,7},{7,1},{8,10},{10,12},{12... | collective-permute-start | bytes 2064392 | tf_op jit(solution)/shard_map/weight_hops/ppermute | solution.py:127
  35.1 15.8 %collective-permute-start.9 = (bf16[3,896,128]{2,1,0:T(8,128)(2,1)}, bf16[3,896,128]{2,1,0:T(8,128)(2,1)}, u32[]{:S(2)}, u32[]{:S(2)}) collective-permute-start(bf16[3,896,128]{2,1,0:T(8,128)(2,1)} %pad_maximum_fusion.refs_12_), channel_id=1, source_target_pairs={{0,16},{16,32},{32,48},{48,0},{1,17},{17,33},{33,49},{49,1},{2,18}... | collective-permute-start | bytes 2064392 | tf_op jit(solution)/shard_map/tiles_xy/ppermute | solution.py:127
  50.9 19.3 %collective-permute-start.11 = (bf16[896,384]{1,0:T(8,128)(2,1)}, bf16[896,384]{1,0:T(8,128)(2,1)}, u32[]{:S(2)}, u32[]{:S(2)}) collective-permute-start(bf16[896,384]{1,0:T(8,128)(2,1)} %collective-permute-done.7.refs_5_), channel_id=1, source_target_pairs={{0,2},{2,4},{4,6},{6,0},{1,3},{3,5},{5,7},{7,1},{8,10},{10,12},{12... | collective-permute-start | bytes 2064392 | tf_op jit(solution)/shard_map/weight_hops/ppermute | solution.py:127
  53.8 14.0 %collective-permute-start.22 = (bf16[1,896,128]{2,1,0:T(8,128)(2,1)}, bf16[1,896,128]{2,1,0:T(8,128)(2,1)}, u32[]{:S(2)}, u32[]{:S(2)}) collective-permute-start(bf16[1,896,128]{2,1,0:T(8,128)(2,1)} %bitcast.14.refs_16_), channel_id=1, source_target_pairs={{0,64},{64,128},{128,192},{192,0},{1,65},{65,129},{129,193},{193,1... | collective-permute-start | bytes 688136 | tf_op jit(solution)/shard_map/tiles_xy/ppermute | solution.py:127
  55.0 39.0 %all-to-all-start = ((bf16[16,2,64,384]{3,2,1,0:T(8,128)(2,1)}), bf16[16,2,64,384]{3,2,1,0:T(8,128)(2,1)S(1)}, u32[]{:S(2)}, u32[]{:S(2)}) async-start(bf16[16,2,64,384]{3,2,1,0:T(8,128)(2,1)} %bitcast.35), calls=%async_computation | async-start | bytes 3145728 | tf_op jit(solution)/shard_map/grad/all_to_all | solution.py:183
  60.5 19.3 %collective-permute-start.20 = (bf16[1,896,128]{2,1,0:T(8,128)(2,1)}, bf16[1,896,128]{2,1,0:T(8,128)(2,1)S(1)}, u32[]{:S(2)}, u32[]{:S(2)}) collective-permute-start(bf16[1,896,128]{2,1,0:T(8,128)(2,1)} %bitcast.14.refs_16_), channel_id=1, source_target_pairs={{0,48},{16,0},{32,16},{48,32},{1,49},{17,1},{33,17},{49,33},{2,50}... | collective-permute-start | bytes 688136 | tf_op jit(solution)/shard_map/tiles_xy/ppermute | solution.py:127
  63.1 25.9 %collective-permute-start.13 = (bf16[3,896,128]{2,1,0:T(8,128)(2,1)}, bf16[3,896,128]{2,1,0:T(8,128)(2,1)}, u32[]{:S(2)}, u32[]{:S(2)}) collective-permute-start(bf16[3,896,128]{2,1,0:T(8,128)(2,1)} %pad_maximum_fusion.refs_12_), channel_id=1, source_target_pairs={{0,1},{1,0},{2,3},{3,2},{4,5},{5,4},{6,7},{7,6},{8,9},{9,8},{10,11... | collective-permute-start | bytes 2064392 | tf_op jit(solution)/shard_map/other_core/ppermute | solution.py:123
  67.8 21.8 %collective-permute-start.14 = (bf16[3,896,128]{2,1,0:T(8,128)(2,1)}, bf16[3,896,128]{2,1,0:T(8,128)(2,1)}, u32[]{:S(2)}, u32[]{:S(2)}) collective-permute-start(bf16[3,896,128]{2,1,0:T(8,128)(2,1)} %collective-permute-done.8.refs_13_), channel_id=1, source_target_pairs={{0,1},{1,0},{2,3},{3,2},{4,5},{5,4},{6,7},{7,6},{8,9},{9,8},{10,11... | collective-permute-start | bytes 2064392 | tf_op jit(solution)/shard_map/other_core/ppermute | solution.py:123
  67.8 18.0 %collective-permute-start.18 = (bf16[1,896,128]{2,1,0:T(8,128)(2,1)}, bf16[1,896,128]{2,1,0:T(8,128)(2,1)S(1)}, u32[]{:S(2)}, u32[]{:S(2)}) collective-permute-start(bf16[1,896,128]{2,1,0:T(8,128)(2,1)} %bitcast.14.refs_16_), channel_id=1, source_target_pairs={{0,192},{64,0},{128,64},{192,128},{1,193},{65,1},{129,65},{193,129... | collective-permute-start | bytes 688136 | tf_op jit(solution)/shard_map/tiles_xy/ppermute | solution.py:127
  70.2 19.6 %collective-permute-start.12 = (bf16[896,384]{1,0:T(8,128)(2,1)}, bf16[896,384]{1,0:T(8,128)(2,1)}, u32[]{:S(2)}, u32[]{:S(2)}) collective-permute-start(bf16[896,384]{1,0:T(8,128)(2,1)} %collective-permute-done.11.refs_6_), channel_id=1, source_target_pairs={{0,2},{2,4},{4,6},{6,0},{1,3},{3,5},{5,7},{7,1},{8,10},{10,12},{12... | collective-permute-start | bytes 2064392 | tf_op jit(solution)/shard_map/weight_hops/ppermute | solution.py:127
  79.8 7.3 %collective-permute-start.23 = (bf16[1,896,128]{2,1,0:T(8,128)(2,1)}, bf16[1,896,128]{2,1,0:T(8,128)(2,1)S(1)}, u32[]{:S(2)}, u32[]{:S(2)}) collective-permute-start(bf16[1,896,128]{2,1,0:T(8,128)(2,1)} %collective-permute-done.22.refs_19_), channel_id=1, source_target_pairs={{0,1},{1,0},{2,3},{3,2},{4,5},{5,4},{6,7},{7,6},{8,9},{9,8},{10,11... | collective-permute-start | bytes 688136 | tf_op jit(solution)/shard_map/other_core/ppermute | solution.py:123
  94.4 24.5 %collective-permute-start.32 = (bf16[896,384]{1,0:T(8,128)(2,1)}, bf16[896,384]{1,0:T(8,128)(2,1)}, u32[]{:S(2)}, u32[]{:S(2)}) collective-permute-start(bf16[896,384]{1,0:T(8,128)(2,1)} %collective-permute-done.12.refs_7_), channel_id=1, source_target_pairs={{0,1},{1,0},{2,3},{3,2},{4,5},{5,4},{6,7},{7,6},{8,9},{9,8},{10,11... | collective-permute-start | bytes 2064392 | tf_op jit(solution)/shard_map/other_core/ppermute | solution.py:123
  95.7 7.0 %collective-permute-start.27 = (bf16[64,384]{1,0:T(8,128)(2,1)S(1)}, bf16[64,384]{1,0:T(8,128)(2,1)S(1)}, u32[]{:S(2)}, u32[]{:S(2)}) collective-permute-start(bf16[64,384]{1,0:T(8,128)(2,1)S(1)} %fusion.6), channel_id=1, source_target_pairs={{0,8},{8,0},{1,9},{9,1},{2,10},{10,2},{3,11},{11,3},{4,12},{12,4},... | collective-permute-start | bytes 147464 | tf_op jit(solution)/shard_map/grad/ppermute | solution.py:123
  106.5 5.2 %collective-permute-start.31 = (bf16[128,384]{1,0:T(8,128)(2,1)S(1)}, bf16[128,384]{1,0:T(8,128)(2,1)S(1)}, u32[]{:S(2)}, u32[]{:S(2)}) collective-permute-start(bf16[128,384]{1,0:T(8,128)(2,1)S(1)} %maximum_select_fusion.refs_0_), channel_id=1, source_target_pairs={{0,6},{2,0},{4,2},{6,4},{1,7},{3,1},{5,3},{7,5},{8,14},{10,8},{12,... | collective-permute-start | bytes 294920 | tf_op jit(solution)/shard_map/lift/ppermute | solution.py:127
  107.4 11.4 %collective-permute-start.30 = (bf16[128,384]{1,0:T(8,128)(2,1)S(1)}, bf16[128,384]{1,0:T(8,128)(2,1)S(1)}, u32[]{:S(2)}, u32[]{:S(2)}) collective-permute-start(bf16[128,384]{1,0:T(8,128)(2,1)S(1)} %maximum_select_fusion.refs_0_), channel_id=1, source_target_pairs={{0,4},{2,6},{4,0},{6,2},{1,5},{3,7},{5,1},{7,3},{8,12},{10,14},{12... | collective-permute-start | bytes 294920 | tf_op jit(solution)/shard_map/lift/ppermute | solution.py:127
  109.9 8.9 %collective-permute-start.29 = (bf16[128,384]{1,0:T(8,128)(2,1)S(1)}, bf16[128,384]{1,0:T(8,128)(2,1)S(1)}, u32[]{:S(2)}, u32[]{:S(2)}) collective-permute-start(bf16[128,384]{1,0:T(8,128)(2,1)S(1)} %maximum_select_fusion.refs_0_), channel_id=1, source_target_pairs={{0,2},{2,4},{4,6},{6,0},{1,3},{3,5},{5,7},{7,1},{8,10},{10,12},{12... | collective-permute-start | bytes 294920 | tf_op jit(solution)/shard_map/lift/ppermute | solution.py:127
  (24 other events, 126.8 us)

commit v6 on v5

--- a/solution.py
+++ b/solution.py
@@ -44,7 +44,7 @@
 
 
 def lift_kernel(where_ref, *refs):
-    pieces, weights, bases, rest = refs[:4], refs[4:12], refs[12:28], refs[28:]
+    pieces, weights, bases, rest = refs[:4], refs[4:12], refs[12:30], refs[30:]
     out_ref, dirs, old, base, done, in_sems, out_sems = rest
     color, zl, core = (where_ref[i] for i in range(3))
     pair = pieces[0].shape[0]
@@ -52,9 +52,12 @@
     lanes = base.shape[3] // 4
     loads = []
     for k in range(2):
-        three, one = bases[8 * k : 8 * k + 4], bases[8 * k + 4 : 8 * k + 8]
+        own, right, far_low, far_high, left, *one = bases[9 * k : 9 * k + 9]
         for z in range(4):
-            sources = [b.at[0] for b in one] if z == 2 else [b.at[min(z, 2)] for b in three]
+            at = min(z, 2)
+            far = far_low.at[z] if z < 2 else far_high.at[0]
+            three = [own.at[at], right.at[at], far, left.at[at]]
+            sources = [b.at[0] for b in one] if z == 2 else three
             group = [pltpu.make_async_copy(weights[4 * k + z], old.at[k, z], in_sems.at[k, z, 4])]
             for q, source in enumerate(sources):
                 group.append(
@@ -99,7 +102,7 @@
         lift_kernel,
         in_specs=[pl.BlockSpec(memory_space=pltpu.SMEM)]
         + [pl.BlockSpec(memory_space=pltpu.VMEM)] * 4
-        + [anywhere] * 24,
+        + [anywhere] * 26,
         out_specs=anywhere,
         scratch_shapes=[
             pltpu.VMEM((4 * pair, width), BF),
@@ -172,11 +175,11 @@
         ranks_t = total.astype(BF)
     ranks_t, own, second = after(ranks_t, own, second)
     with jax.named_scope("tiles_xy"):
-        far = around(own, 1, "y")
+        far_low, far_high = around(own[:2], 1, "y"), around(own[2:], 3, "y")
     with jax.named_scope("grad"):
         blocks = grad_blocks(ranks_t, out_grads, width)
     blocks, second, weight, hops[1], *three = after(
-        blocks, second, weight, hops[1], own, right, far, left
+        blocks, second, weight, hops[1], own, right, far_low, far_high, left
     )
     hops[0] = weight
     with jax.named_scope("grad"):
@@ -193,7 +196,7 @@
         other_bases = [swap(b, "core") for b in bases]
         others = [swap(h, "core") for h in hops[:3]]
     parts, hops[3], *swapped = after(parts, hops[3], *other_bases, *others)
-    other_bases, others = swapped[:8], swapped[8:]
+    other_bases, others = swapped[:9], swapped[9:]
     with jax.named_scope("grad"):
         halves = jnp.sum(parts.astype(F32), axis=0)
         grad = pick(halves, zh) + swap(pick(halves, 1 - zh).astype(BF), "zh").astype(F32)

time: 130 us -> 139 us (1.069)
  starting transfers between devices: 55 us -> 65.6 us
  waiting for transfers between devices: 38.9 us -> 36.5 us
    ppermute x15 -> x16, starting transfers between devices: 19.8 us -> 29.8 us  [swap(): return lax.ppermute(value, axis, [(0, 1), (1, 0)])]
    ppermute x15 -> x16, waiting for transfers between devices: 12.2 us -> 10.5 us  [swap(): return lax.ppermute(value, axis, [(0, 1), (1, 0)])]
    ppermute x15 -> x16, starting transfers between devices: 23.1 us -> 22.7 us  [around(): return lax.ppermute(value, axis, [(i, (i + shift) % 4) for i in range(4)])]
    ppermute x15 -> x16, waiting for transfers between devices: 21.5 us -> 21.3 us  [around(): return lax.ppermute(value, axis, [(i, (i + shift) % 4) for i in range(4)])]
  transfers between devices with their start and end apart: 34 -> 36, of which waited for: 18 -> 19; matrix products, arithmetic and copies ran while one was open for 7% -> 7% of each run, Pallas kernels for 9% -> 8%
where the time goes in v6:
time: 139 us; the launch traced here: 138 us
  starting transfers between devices  65.6 us (47%)
  waiting for transfers between devices  36.5 us (26%)
  Pallas kernels  19.9 us (14%)
  other arithmetic  6.87 us (5%)
  local copies, waits for them, and re-layouts  4.68 us (3%)
  matrix products  3.8 us (3%)
    ppermute x16, starting transfers between devices, swap(): return lax.ppermute(value, axis, [(0, 1), (1, 0)])  29.8 us
    ppermute x16, starting transfers between devices, around(): return lax.ppermute(value, axis, [(i, (i + shift) % 4) for i in range(4)])  22.7 us
    ppermute x16, waiting for transfers between devices, around(): return lax.ppermute(value, axis, [(i, (i + shift) % 4) for i in range(4)])  21.3 us
    pallas_call x1, Pallas kernels, grad_blocks(): pl.pallas_call(grad_kernel, grid=(blocks // step,), in_specs=[pl.BlockSpe...  11.1 us
    ppermute x16, waiting for transfers between devices, swap(): return lax.ppermute(value, axis, [(0, 1), (1, 0)])  10.5 us
    pallas_call x1, Pallas kernels, lift(): pl.pallas_call(lift_kernel, in_specs=[pl.BlockSpec(memory_space=pltpu.SME...  8.86 us
    all_to_all x1, starting transfers between devices, shards(): lax.all_to_all(blocks.reshape(16, 2, rank_local, width), ('x', 'y'), 0, 0)  6.59 us
    ppermute x3, starting transfers between devices, along_z(): lax.ppermute(value, ('zh', 'zl'), [(i, (i + shift) % 8) for i in range(8)])  6.49 us
  transfers between devices with their start and end apart: 36, of which 19 were waited for; matrix products, arithmetic and copies ran while one was open for 7% of the time, Pallas kernels for 8%

profile of v6, /device:TPU:1, one launch (start us, length us, event | category | flops | bytes accessed | tf_op | source)
XLA Modules:
  0.0 138.3 jit_solution(3560261455708172771)
XLA Ops:
  1.8 6.5 %collective-permute-start.1 = (bf16[896,128]{1,0:T(8,128)(2,1)S(1)}, bf16[896,128]{1,0:T(8,128)(2,1)S(1)}, u32[]{:S(2)}, u32[]{:S(2)}) collective-permute-start(bf16[896,128]{1,0:T(8,128)(2,1)S(1)} %constant_dynamic-slice_fusion), channel_id=1, source_target_pairs={{0,14},{2,0},{4,2},{6,4},{8,6},{10,8},{12,10},{14,12},{1,15},{3,1}... | collective-permute-start | bytes 688136 | tf_op jit(solution)/shard_map/tiles/ppermute | solution.py:134
  8.2 3.8 %fusion.8 = f32[512,1024]{1,0:T(8,128)} fusion(bf16[896,512]{1,0:T(8,128)(2,1)} %param.8, bf16[1024,896]{1,0:T(8,128)(2,1)S(1)} %copy-done), kind=kOutput, calls=%fused_computation.23 | convolution fusion | flops 939524096 | bytes 4849664 | tf_op jit(solution)/shard_map/project/dot_general | solution.py:157
  12.5 3.1 %collective-permute-done = bf16[896,128]{1,0:T(8,128)(2,1)S(1)} collective-permute-done((bf16[896,128]{1,0:T(8,128)(2,1)S(1)}, bf16[896,128]{1,0:T(8,128)(2,1)S(1)}, u32[]{:S(2)}, u32[]{:S(2)}) %collective-permute-start) | collective-permute-done | bytes 229408 | tf_op jit(solution)/shard_map/tiles/ppermute | solution.py:134
  16.9 2.0 %collective-permute-start.2 = (bf16[4,64,1024]{2,1,0:T(8,128)(2,1)S(1)}, bf16[4,64,1024]{2,1,0:T(8,128)(2,1)}, u32[]{:S(2)}, u32[]{:S(2)}) collective-permute-start(bf16[4,64,1024]{2,1,0:T(8,128)(2,1)S(1)} %fusion), channel_id=1, source_target_pairs={{0,1},{1,0},{2,3},{3,2},{4,5},{5,4},{6,7},{7,6},{8,9},{9,8},{10,11... | collective-permute-start | bytes 1572872 | tf_op jit(solution)/shard_map/project/ppermute | solution.py:126
  18.9 1.7 %collective-permute-done.2 = bf16[4,64,1024]{2,1,0:T(8,128)(2,1)} collective-permute-done((bf16[4,64,1024]{2,1,0:T(8,128)(2,1)S(1)}, bf16[4,64,1024]{2,1,0:T(8,128)(2,1)}, u32[]{:S(2)}, u32[]{:S(2)}) %collective-permute-start.2) | collective-permute-done | bytes 524320 | tf_op jit(solution)/shard_map/project/ppermute | solution.py:126
  22.9 3.3 %collective-permute-start.5 = (bf16[64,1024]{1,0:T(8,128)(2,1)}, bf16[64,1024]{1,0:T(8,128)(2,1)}, u32[]{:S(2)}, u32[]{:S(2)}) collective-permute-start(bf16[64,1024]{1,0:T(8,128)(2,1)} %get-tuple-element.79), channel_id=1, source_target_pairs={{0,6},{2,0},{4,2},{6,4},{1,7},{3,1},{5,3},{7,5},{8,14},{10,8},{12,... | collective-permute-start | bytes 393224 | tf_op jit(solution)/shard_map/project/ppermute | solution.py:130
  26.1 3.6 %collective-permute-done.3 = bf16[64,1024]{1,0:T(8,128)(2,1)} collective-permute-done((bf16[64,1024]{1,0:T(8,128)(2,1)}, bf16[64,1024]{1,0:T(8,128)(2,1)}, u32[]{:S(2)}, u32[]{:S(2)}) %collective-permute-start.3) | collective-permute-done | bytes 131104 | tf_op jit(solution)/shard_map/project/ppermute | solution.py:130
  33.5 1.8 %fusion.1.ranks_ref = bf16[64,1024]{1,0:T(8,128)(2,1)} fusion(bf16[64,1024]{1,0:T(8,128)(2,1)} %collective-permute-done.5, bf16[64,1024]{1,0:T(8,128)(2,1)} %collective-permute-done.4, bf16[64,1024]{1,0:T(8,128)(2,1)} %collective-permute-done.3, f32[4,64,1024]{2,1,0:T(8,128)S(1)} %bitcast_add_fusion, s32[]{:T(128)S(6)} %select_n.62), kind=kLoop, calls=%fused_computation.6 | loop fusion | flops 458752 | bytes 786436 | tf_op jit(solution)/shard_map/project/convert_element_type | solution.py:175
  36.4 2.8 %collective-permute-start.10 = (bf16[1,896,128]{2,1,0:T(8,128)(2,1)S(1)}, bf16[1,896,128]{2,1,0:T(8,128)(2,1)S(1)}, u32[]{:S(2)}, u32[]{:S(2)}) collective-permute-start(bf16[1,896,128]{2,1,0:T(8,128)(2,1)S(1)} %slice.7), channel_id=1, source_target_pairs={{0,48},{16,0},{32,16},{48,32},{1,49},{17,1},{33,17},{49,33},{2,50}... | collective-permute-start | bytes 688136 | tf_op jit(solution)/shard_map/tiles_xy/ppermute | solution.py:130
  39.2 11.1 %grad.1 = bf16[32,64,384]{2,1,0:T(8,128)(2,1)} custom-call(bf16[64,1024]{1,0:T(8,128)(2,1)} %fusion.1.ranks_ref, bf16[1024,12288]{1,0:T(8,128)(2,1)} %grads_ref.1), custom_call_target="tpu_custom_call" | custom-call | flops 6442450944 | bytes 25165824 | tf_op jit(solution)/shard_map/grad/pallas_call | solution.py:28
  51.2 3.1 %collective-permute-start.12 = (bf16[896,384]{1,0:T(8,128)(2,1)}, bf16[896,384]{1,0:T(8,128)(2,1)}, u32[]{:S(2)}, u32[]{:S(2)}) collective-permute-start(bf16[896,384]{1,0:T(8,128)(2,1)} %collective-permute-done.7.refs_5_), channel_id=1, source_target_pairs={{0,2},{2,4},{4,6},{6,0},{1,3},{3,5},{5,7},{7,1},{8,10},{10,12},{12... | collective-permute-start | bytes 2064392 | tf_op jit(solution)/shard_map/weight_hops/ppermute | solution.py:130
  55.5 6.6 %all-to-all-start = ((bf16[16,2,64,384]{3,2,1,0:T(8,128)(2,1)}), bf16[16,2,64,384]{3,2,1,0:T(8,128)(2,1)S(1)}, u32[]{:S(2)}, u32[]{:S(2)}) async-start(bf16[16,2,64,384]{3,2,1,0:T(8,128)(2,1)} %bitcast.35), calls=%async_computation | async-start | bytes 3145728 | tf_op jit(solution)/shard_map/grad/all_to_all | solution.py:186
  62.2 2.6 %collective-permute-start.22 = (bf16[1,896,128]{2,1,0:T(8,128)(2,1)}, bf16[1,896,128]{2,1,0:T(8,128)(2,1)S(1)}, u32[]{:S(2)}, u32[]{:S(2)}) collective-permute-start(bf16[1,896,128]{2,1,0:T(8,128)(2,1)} %bitcast.14.refs_17_), channel_id=1, source_target_pairs={{0,48},{16,0},{32,16},{48,32},{1,49},{17,1},{33,17},{49,33},{2,50}... | collective-permute-start | bytes 688136 | tf_op jit(solution)/shard_map/tiles_xy/ppermute | solution.py:130
  64.7 2.4 %collective-permute-start.20 = (bf16[1,896,128]{2,1,0:T(8,128)(2,1)}, bf16[1,896,128]{2,1,0:T(8,128)(2,1)S(1)}, u32[]{:S(2)}, u32[]{:S(2)}) collective-permute-start(bf16[1,896,128]{2,1,0:T(8,128)(2,1)} %bitcast.14.refs_17_), channel_id=1, source_target_pairs={{0,192},{64,0},{128,64},{192,128},{1,193},{65,1},{129,65},{193,129... | collective-permute-start | bytes 688136 | tf_op jit(solution)/shard_map/tiles_xy/ppermute | solution.py:130
  67.1 3.6 %collective-permute-start.14 = (bf16[3,896,128]{2,1,0:T(8,128)(2,1)}, bf16[3,896,128]{2,1,0:T(8,128)(2,1)}, u32[]{:S(2)}, u32[]{:S(2)}) collective-permute-start(bf16[3,896,128]{2,1,0:T(8,128)(2,1)} %copy-done.1), channel_id=1, source_target_pairs={{0,1},{1,0},{2,3},{3,2},{4,5},{5,4},{6,7},{7,6},{8,9},{9,8},{10,11... | collective-permute-start | bytes 2064392 | tf_op jit(solution)/shard_map/other_core/ppermute | solution.py:126
  70.8 2.4 %collective-permute-start.13 = (bf16[896,384]{1,0:T(8,128)(2,1)}, bf16[896,384]{1,0:T(8,128)(2,1)}, u32[]{:S(2)}, u32[]{:S(2)}) collective-permute-start(bf16[896,384]{1,0:T(8,128)(2,1)} %collective-permute-done.12.refs_6_), channel_id=1, source_target_pairs={{0,2},{2,4},{4,6},{6,0},{1,3},{3,5},{5,7},{7,1},{8,10},{10,12},{12... | collective-permute-start | bytes 2064392 | tf_op jit(solution)/shard_map/weight_hops/ppermute | solution.py:130
  73.1 8.3 %collective-permute-done.22.refs_19_ = bf16[1,896,128]{2,1,0:T(8,128)(2,1)S(1)} collective-permute-done((bf16[1,896,128]{2,1,0:T(8,128)(2,1)}, bf16[1,896,128]{2,1,0:T(8,128)(2,1)S(1)}, u32[]{:S(2)}, u32[]{:S(2)}) %collective-permute-start.22) | collective-permute-done | bytes 229408 | tf_op jit(solution)/shard_map/tiles_xy/ppermute | solution.py:130
  81.4 6.2 %collective-permute-start.25 = (bf16[1,896,128]{2,1,0:T(8,128)(2,1)}, bf16[1,896,128]{2,1,0:T(8,128)(2,1)S(1)}, u32[]{:S(2)}, u32[]{:S(2)}) collective-permute-start(bf16[1,896,128]{2,1,0:T(8,128)(2,1)} %collective-permute-done.24.refs_20_), channel_id=1, source_target_pairs={{0,1},{1,0},{2,3},{3,2},{4,5},{5,4},{6,7},{7,6},{8,9},{9,8},{10,11... | collective-permute-start | bytes 688136 | tf_op jit(solution)/shard_map/other_core/ppermute | solution.py:126
  97.8 14.2 %collective-permute-start.29 = (bf16[64,384]{1,0:T(8,128)(2,1)S(1)}, bf16[64,384]{1,0:T(8,128)(2,1)S(1)}, u32[]{:S(2)}, u32[]{:S(2)}) collective-permute-start(bf16[64,384]{1,0:T(8,128)(2,1)S(1)} %fusion.6), channel_id=1, source_target_pairs={{0,8},{8,0},{1,9},{9,1},{2,10},{10,2},{3,11},{11,3},{4,12},{12,4},... | collective-permute-start | bytes 147464 | tf_op jit(solution)/shard_map/grad/ppermute | solution.py:126
  112.0 2.0 %collective-permute-done.29 = bf16[64,384]{1,0:T(8,128)(2,1)S(1)} collective-permute-done((bf16[64,384]{1,0:T(8,128)(2,1)S(1)}, bf16[64,384]{1,0:T(8,128)(2,1)S(1)}, u32[]{:S(2)}, u32[]{:S(2)}) %collective-permute-start.29) | collective-permute-done | bytes 49184 | tf_op jit(solution)/shard_map/grad/ppermute | solution.py:126
  114.0 1.7 %divide_convert_fusion = (bf16[64,384]{1,0:T(8,128)(2,1)S(1)}, f32[64,384]{1,0:T(8,128)}, f32[64,384]{1,0:T(8,128)}) fusion(bf16[64,384]{1,0:T(8,128)(2,1)S(1)} %collective-permute-done.29, f32[2,64,384]{2,1,0:T(8,128)} %copy-done.2, s32[]{:T(128)S(6)} %select_n.69, f32[64,384]{1,0:T(8,128)S(1)} %copy-done.16, f32[64,384]{1,0:T(8,128)} %param.11), kind=kLoop, calls=%fused_computation.17 | loop fusion | flops 344064 | bytes 589828 | tf_op jit(solution)/shard_map/adam/convert_element_type | solution.py:209
  117.3 1.8 %collective-permute-start.33 = (bf16[128,384]{1,0:T(8,128)(2,1)S(1)}, bf16[128,384]{1,0:T(8,128)(2,1)S(1)}, u32[]{:S(2)}, u32[]{:S(2)}) collective-permute-start(bf16[128,384]{1,0:T(8,128)(2,1)S(1)} %maximum_select_fusion.refs_0_), channel_id=1, source_target_pairs={{0,6},{2,0},{4,2},{6,4},{1,7},{3,1},{5,3},{7,5},{8,14},{10,8},{12,... | collective-permute-start | bytes 294920 | tf_op jit(solution)/shard_map/lift/ppermute | solution.py:130
  121.6 7.0 %collective-permute-done.32.refs_2_ = bf16[128,384]{1,0:T(8,128)(2,1)S(1)} collective-permute-done((bf16[128,384]{1,0:T(8,128)(2,1)S(1)}, bf16[128,384]{1,0:T(8,128)(2,1)S(1)}, u32[]{:S(2)}, u32[]{:S(2)}) %collective-permute-start.32) | collective-permute-done | bytes 98336 | tf_op jit(solution)/shard_map/lift/ppermute | solution.py:130
  129.3 8.9 %lift.1 = bf16[7168,384]{1,0:T(8,128)(2,1)} custom-call(s32[3]{0:T(128)} %pad_add_fusion.where_ref, bf16[128,384]{1,0:T(8,128)(2,1)} %copy-done.4, bf16[128,384]{1,0:T(8,128)(2,1)} %copy-done.15, bf16[128,384]{1,0:T(8,128)(2,1)} %copy-done.14, bf16[128,384]{1,0:T(8,128)(2,1)} %copy-done.13, bf16[896,384]{1,0:T(8,128)(2,1)} %refs_4_, ...), custom_call_target="tpu_custom_call" | custom-call | flops 2818572288 | bytes 18350080 | tf_op jit(solution)/shard_map/lift/pallas_call | solution.py:101
  (98 shorter events, 27.2 us)
Async XLA Ops:
  1.8 10.8 %collective-permute-start.1 = (bf16[896,128]{1,0:T(8,128)(2,1)S(1)}, bf16[896,128]{1,0:T(8,128)(2,1)S(1)}, u32[]{:S(2)}, u32[]{:S(2)}) collective-permute-start(bf16[896,128]{1,0:T(8,128)(2,1)S(1)} %constant_dynamic-slice_fusion), channel_id=1, source_target_pairs={{0,14},{2,0},{4,2},{6,4},{8,6},{10,8},{12,10},{14,12},{1,15},{3,1}... | collective-permute-start | bytes 688136 | tf_op jit(solution)/shard_map/tiles/ppermute | solution.py:134
  8.2 7.4 %collective-permute-start = (bf16[896,128]{1,0:T(8,128)(2,1)S(1)}, bf16[896,128]{1,0:T(8,128)(2,1)S(1)}, u32[]{:S(2)}, u32[]{:S(2)}) collective-permute-start(bf16[896,128]{1,0:T(8,128)(2,1)S(1)} %constant_dynamic-slice_fusion), channel_id=1, source_target_pairs={{0,2},{2,4},{4,6},{6,8},{8,10},{10,12},{12,14},{14,0},{1,3},{3,5},... | collective-permute-start | bytes 688136 | tf_op jit(solution)/shard_map/tiles/ppermute | solution.py:134
  22.9 6.8 %collective-permute-start.3 = (bf16[64,1024]{1,0:T(8,128)(2,1)}, bf16[64,1024]{1,0:T(8,128)(2,1)}, u32[]{:S(2)}, u32[]{:S(2)}) collective-permute-start(bf16[64,1024]{1,0:T(8,128)(2,1)} %get-tuple-element.78), channel_id=1, source_target_pairs={{0,2},{2,4},{4,6},{6,0},{1,3},{3,5},{5,7},{7,1},{8,10},{10,12},{12... | collective-permute-start | bytes 393224 | tf_op jit(solution)/shard_map/project/ppermute | solution.py:130
  22.9 10.6 %collective-permute-start.5 = (bf16[64,1024]{1,0:T(8,128)(2,1)}, bf16[64,1024]{1,0:T(8,128)(2,1)}, u32[]{:S(2)}, u32[]{:S(2)}) collective-permute-start(bf16[64,1024]{1,0:T(8,128)(2,1)} %get-tuple-element.79), channel_id=1, source_target_pairs={{0,6},{2,0},{4,2},{6,4},{1,7},{3,1},{5,3},{7,5},{8,14},{10,8},{12,... | collective-permute-start | bytes 393224 | tf_op jit(solution)/shard_map/project/ppermute | solution.py:130
  26.1 7.4 %collective-permute-start.4 = (bf16[64,1024]{1,0:T(8,128)(2,1)}, bf16[64,1024]{1,0:T(8,128)(2,1)}, u32[]{:S(2)}, u32[]{:S(2)}) collective-permute-start(bf16[64,1024]{1,0:T(8,128)(2,1)} %get-tuple-element.80), channel_id=1, source_target_pairs={{0,4},{2,6},{4,0},{6,2},{1,5},{3,7},{5,1},{7,3},{8,12},{10,14},{12... | collective-permute-start | bytes 393224 | tf_op jit(solution)/shard_map/project/ppermute | solution.py:130
  29.7 6.7 %collective-permute-start.6 = (bf16[896,128]{1,0:T(8,128)(2,1)S(1)}, bf16[896,128]{1,0:T(8,128)(2,1)}, u32[]{:S(2)}, u32[]{:S(2)}) collective-permute-start(bf16[896,128]{1,0:T(8,128)(2,1)S(1)} %collective-permute-done), channel_id=1, source_target_pairs={{0,2},{2,4},{4,6},{6,8},{8,10},{10,12},{12,14},{14,0},{1,3},{3,5},... | collective-permute-start | bytes 688136 | tf_op jit(solution)/shard_map/tiles/ppermute | solution.py:134
  30.7 19.6 %collective-permute-start.11 = (bf16[3,896,128]{2,1,0:T(8,128)(2,1)S(1)}, bf16[3,896,128]{2,1,0:T(8,128)(2,1)}, u32[]{:S(2)}, u32[]{:S(2)}) collective-permute-start(bf16[3,896,128]{2,1,0:T(8,128)(2,1)S(1)} %pad_maximum_fusion.refs_12_), channel_id=1, source_target_pairs={{0,64},{64,128},{128,192},{192,0},{1,65},{65,129},{129,193},{193,1... | collective-permute-start | bytes 2064392 | tf_op jit(solution)/shard_map/tiles_xy/ppermute | solution.py:130
  32.0 18.3 %collective-permute-start.8 = (bf16[3,896,128]{2,1,0:T(8,128)(2,1)S(1)}, bf16[3,896,128]{2,1,0:T(8,128)(2,1)}, u32[]{:S(2)}, u32[]{:S(2)}) collective-permute-start(bf16[3,896,128]{2,1,0:T(8,128)(2,1)S(1)} %pad_maximum_fusion.refs_12_), channel_id=1, source_target_pairs={{0,192},{64,0},{128,64},{192,128},{1,193},{65,1},{129,65},{193,129... | collective-permute-start | bytes 2064392 | tf_op jit(solution)/shard_map/tiles_xy/ppermute | solution.py:130
  33.5 17.7 %collective-permute-start.7 = (bf16[896,384]{1,0:T(8,128)(2,1)}, bf16[896,384]{1,0:T(8,128)(2,1)}, u32[]{:S(2)}, u32[]{:S(2)}) collective-permute-start(bf16[896,384]{1,0:T(8,128)(2,1)} %refs_4_), channel_id=1, source_target_pairs={{0,2},{2,4},{4,6},{6,0},{1,3},{3,5},{5,7},{7,1},{8,10},{10,12},{12... | collective-permute-start | bytes 2064392 | tf_op jit(solution)/shard_map/weight_hops/ppermute | solution.py:130
  36.4 13.9 %collective-permute-start.10 = (bf16[1,896,128]{2,1,0:T(8,128)(2,1)S(1)}, bf16[1,896,128]{2,1,0:T(8,128)(2,1)S(1)}, u32[]{:S(2)}, u32[]{:S(2)}) collective-permute-start(bf16[1,896,128]{2,1,0:T(8,128)(2,1)S(1)} %slice.7), channel_id=1, source_target_pairs={{0,48},{16,0},{32,16},{48,32},{1,49},{17,1},{33,17},{49,33},{2,50}... | collective-permute-start | bytes 688136 | tf_op jit(solution)/shard_map/tiles_xy/ppermute | solution.py:130
  39.2 11.1 %collective-permute-start.9 = (bf16[2,896,128]{2,1,0:T(8,128)(2,1)S(1)}, bf16[2,896,128]{2,1,0:T(8,128)(2,1)S(1)}, u32[]{:S(2)}, u32[]{:S(2)}) collective-permute-start(bf16[2,896,128]{2,1,0:T(8,128)(2,1)S(1)} %slice.6), channel_id=1, source_target_pairs={{0,16},{16,32},{32,48},{48,0},{1,17},{17,33},{33,49},{49,1},{2,18}... | collective-permute-start | bytes 1376264 | tf_op jit(solution)/shard_map/tiles_xy/ppermute | solution.py:130
  51.2 19.5 %collective-permute-start.12 = (bf16[896,384]{1,0:T(8,128)(2,1)}, bf16[896,384]{1,0:T(8,128)(2,1)}, u32[]{:S(2)}, u32[]{:S(2)}) collective-permute-start(bf16[896,384]{1,0:T(8,128)(2,1)} %collective-permute-done.7.refs_5_), channel_id=1, source_target_pairs={{0,2},{2,4},{4,6},{6,0},{1,3},{3,5},{5,7},{7,1},{8,10},{10,12},{12... | collective-permute-start | bytes 2064392 | tf_op jit(solution)/shard_map/weight_hops/ppermute | solution.py:130
  54.3 16.4 %collective-permute-start.24 = (bf16[1,896,128]{2,1,0:T(8,128)(2,1)}, bf16[1,896,128]{2,1,0:T(8,128)(2,1)}, u32[]{:S(2)}, u32[]{:S(2)}) collective-permute-start(bf16[1,896,128]{2,1,0:T(8,128)(2,1)} %bitcast.14.refs_17_), channel_id=1, source_target_pairs={{0,64},{64,128},{128,192},{192,0},{1,65},{65,129},{129,193},{193,1... | collective-permute-start | bytes 688136 | tf_op jit(solution)/shard_map/tiles_xy/ppermute | solution.py:130
  55.5 40.7 %all-to-all-start = ((bf16[16,2,64,384]{3,2,1,0:T(8,128)(2,1)}), bf16[16,2,64,384]{3,2,1,0:T(8,128)(2,1)S(1)}, u32[]{:S(2)}, u32[]{:S(2)}) async-start(bf16[16,2,64,384]{3,2,1,0:T(8,128)(2,1)} %bitcast.35), calls=%async_computation | async-start | bytes 3145728 | tf_op jit(solution)/shard_map/grad/all_to_all | solution.py:186
  62.2 19.3 %collective-permute-start.22 = (bf16[1,896,128]{2,1,0:T(8,128)(2,1)}, bf16[1,896,128]{2,1,0:T(8,128)(2,1)S(1)}, u32[]{:S(2)}, u32[]{:S(2)}) collective-permute-start(bf16[1,896,128]{2,1,0:T(8,128)(2,1)} %bitcast.14.refs_17_), channel_id=1, source_target_pairs={{0,48},{16,0},{32,16},{48,32},{1,49},{17,1},{33,17},{49,33},{2,50}... | collective-permute-start | bytes 688136 | tf_op jit(solution)/shard_map/tiles_xy/ppermute | solution.py:130
  64.7 22.9 %collective-permute-start.20 = (bf16[1,896,128]{2,1,0:T(8,128)(2,1)}, bf16[1,896,128]{2,1,0:T(8,128)(2,1)S(1)}, u32[]{:S(2)}, u32[]{:S(2)}) collective-permute-start(bf16[1,896,128]{2,1,0:T(8,128)(2,1)} %bitcast.14.refs_17_), channel_id=1, source_target_pairs={{0,192},{64,0},{128,64},{192,128},{1,193},{65,1},{129,65},{193,129... | collective-permute-start | bytes 688136 | tf_op jit(solution)/shard_map/tiles_xy/ppermute | solution.py:130
  67.1 24.1 %collective-permute-start.14 = (bf16[3,896,128]{2,1,0:T(8,128)(2,1)}, bf16[3,896,128]{2,1,0:T(8,128)(2,1)}, u32[]{:S(2)}, u32[]{:S(2)}) collective-permute-start(bf16[3,896,128]{2,1,0:T(8,128)(2,1)} %copy-done.1), channel_id=1, source_target_pairs={{0,1},{1,0},{2,3},{3,2},{4,5},{5,4},{6,7},{7,6},{8,9},{9,8},{10,11... | collective-permute-start | bytes 2064392 | tf_op jit(solution)/shard_map/other_core/ppermute | solution.py:126
  70.8 17.2 %collective-permute-start.17 = (bf16[1,896,128]{2,1,0:T(8,128)(2,1)}, bf16[1,896,128]{2,1,0:T(8,128)(2,1)S(1)}, u32[]{:S(2)}, u32[]{:S(2)}) collective-permute-start(bf16[1,896,128]{2,1,0:T(8,128)(2,1)} %copy-done.5), channel_id=1, source_target_pairs={{0,1},{1,0},{2,3},{3,2},{4,5},{5,4},{6,7},{7,6},{8,9},{9,8},{10,11... | collective-permute-start | bytes 688136 | tf_op jit(solution)/shard_map/other_core/ppermute | solution.py:126
  70.8 20.8 %collective-permute-start.13 = (bf16[896,384]{1,0:T(8,128)(2,1)}, bf16[896,384]{1,0:T(8,128)(2,1)}, u32[]{:S(2)}, u32[]{:S(2)}) collective-permute-start(bf16[896,384]{1,0:T(8,128)(2,1)} %collective-permute-done.12.refs_6_), channel_id=1, source_target_pairs={{0,2},{2,4},{4,6},{6,0},{1,3},{3,5},{5,7},{7,1},{8,10},{10,12},{12... | collective-permute-start | bytes 2064392 | tf_op jit(solution)/shard_map/weight_hops/ppermute | solution.py:130
  81.4 7.6 %collective-permute-start.25 = (bf16[1,896,128]{2,1,0:T(8,128)(2,1)}, bf16[1,896,128]{2,1,0:T(8,128)(2,1)S(1)}, u32[]{:S(2)}, u32[]{:S(2)}) collective-permute-start(bf16[1,896,128]{2,1,0:T(8,128)(2,1)} %collective-permute-done.24.refs_20_), channel_id=1, source_target_pairs={{0,1},{1,0},{2,3},{3,2},{4,5},{5,4},{6,7},{7,6},{8,9},{9,8},{10,11... | collective-permute-start | bytes 688136 | tf_op jit(solution)/shard_map/other_core/ppermute | solution.py:126
  96.6 32.0 %collective-permute-start.34 = (bf16[896,384]{1,0:T(8,128)(2,1)}, bf16[896,384]{1,0:T(8,128)(2,1)}, u32[]{:S(2)}, u32[]{:S(2)}) collective-permute-start(bf16[896,384]{1,0:T(8,128)(2,1)} %collective-permute-done.13.refs_7_), channel_id=1, source_target_pairs={{0,1},{1,0},{2,3},{3,2},{4,5},{5,4},{6,7},{7,6},{8,9},{9,8},{10,11... | collective-permute-start | bytes 2064392 | tf_op jit(solution)/shard_map/other_core/ppermute | solution.py:126
  97.8 16.1 %collective-permute-start.29 = (bf16[64,384]{1,0:T(8,128)(2,1)S(1)}, bf16[64,384]{1,0:T(8,128)(2,1)S(1)}, u32[]{:S(2)}, u32[]{:S(2)}) collective-permute-start(bf16[64,384]{1,0:T(8,128)(2,1)S(1)} %fusion.6), channel_id=1, source_target_pairs={{0,8},{8,0},{1,9},{9,1},{2,10},{10,2},{3,11},{11,3},{4,12},{12,4},... | collective-permute-start | bytes 147464 | tf_op jit(solution)/shard_map/grad/ppermute | solution.py:126
  119.0 9.6 %collective-permute-start.32 = (bf16[128,384]{1,0:T(8,128)(2,1)S(1)}, bf16[128,384]{1,0:T(8,128)(2,1)S(1)}, u32[]{:S(2)}, u32[]{:S(2)}) collective-permute-start(bf16[128,384]{1,0:T(8,128)(2,1)S(1)} %maximum_select_fusion.refs_0_), channel_id=1, source_target_pairs={{0,4},{2,6},{4,0},{6,2},{1,5},{3,7},{5,1},{7,3},{8,12},{10,14},{12... | collective-permute-start | bytes 294920 | tf_op jit(solution)/shard_map/lift/ppermute | solution.py:130
  119.0 9.6 %collective-permute-start.31 = (bf16[128,384]{1,0:T(8,128)(2,1)S(1)}, bf16[128,384]{1,0:T(8,128)(2,1)S(1)}, u32[]{:S(2)}, u32[]{:S(2)}) collective-permute-start(bf16[128,384]{1,0:T(8,128)(2,1)S(1)} %maximum_select_fusion.refs_0_), channel_id=1, source_target_pairs={{0,2},{2,4},{4,6},{6,0},{1,3},{3,5},{5,7},{7,1},{8,10},{10,12},{12... | collective-permute-start | bytes 294920 | tf_op jit(solution)/shard_map/lift/ppermute | solution.py:130
  (29 other events, 174.2 us)
